TPU v7x, 32 devices: a whole 2x2x4 slice. The times are simulated.
32 devices in a mesh: fsdp: 16 (over z, x, core), dp: 2 (over y).
Axes of the slice: x: 2, y: 2, z: 4, core: 2. Of those that a mesh axis runs over, the one named last changes fastest.
Arguments:
- inputs: bfloat16 [32, 1024, 1024], P(('fsdp', 'dp')), may hold values from -6 to 6
- encoder: bfloat16 [32, 1024, 1024], P(('fsdp', 'dp')), may hold values from -6 to 6
- grad_out: bfloat16 [32, 1024, 1024], P(('fsdp', 'dp')), may hold values from -6 to 6
- target_mask: int32 [32, 1024], P(('fsdp', 'dp')), may hold values from 0 to 1, as said below
- source_lengths: int32 [32], P(('fsdp', 'dp')), may hold values from 16 to 1024, as said below
- step: int32 [1], replicated, may hold values from 250 to 999
- attn_in: bfloat16 [1024, 6144], P('fsdp'), may hold values from -0.1875 to 0.1875
- attn_out: bfloat16 [1024, 2048], P('fsdp'), may hold values from -0.75 to 0.75
- ffn_in: bfloat16 [1024, 4096], P('fsdp'), may hold values from -0.1875 to 0.1875
- ffn_in_bias: float32 [4096], replicated, may hold values from -1.75 to 1.75
- ffn_out: bfloat16 [4096, 1024], P('fsdp'), may hold values from -0.09375 to 0.09375
- ffn_out_bias: float32 [1024], replicated, may hold values from -1.75 to 1.75
- attn_bias: float32 [6, 1024], replicated, may hold values from -1.75 to 1.75
- norm_gain: float32 [3, 1024], replicated, may hold values from 0.5 to 1.5
- norm_shift: float32 [3, 1024], replicated, may hold values from -1.75 to 1.75
- adapter_down: bfloat16 [1024, 512], replicated, may hold values from -0.1875 to 0.1875
- adapter_down_bias: float32 [512], replicated, may hold values from -1.75 to 1.75
- adapter_up: bfloat16 [512, 1024], replicated, may hold values from -0.25 to 0.25
- adapter_up_bias: float32 [1024], replicated, may hold values from -1.75 to 1.75
- adapter_gain: float32 [1024], replicated, may hold values from 0.5 to 1.5
- adapter_shift: float32 [1024], replicated, may hold values from -1.75 to 1.75
Outputs:
- layer_out: bfloat16 [32, 1024, 1024], P(('fsdp', 'dp'))
- grad_input: float32 [32, 1024, 1024], P(('fsdp', 'dp'))
- grad_encoder: float32 [32, 1024, 1024], P(('fsdp', 'dp'))
- grad_down: float32 [1024, 512], replicated
- grad_down_bias: float32 [512], replicated
- grad_up: float32 [512, 1024], replicated
- grad_up_bias: float32 [1024], replicated
- grad_gain: float32 [1024], replicated
- grad_shift: float32 [1024], replicated
Inputs may be any that keep to these rules, and one draw needn't show every extreme that they name: `target_mask`: each row is 1 on its first positions and 0 after them, with at least half of 1024 ones; the first sequence is all ones and the second has exactly half of 1024 ones. `source_lengths`: the first sequence has 1024, the last the least value.
All inputs are finite; a program needn't handle non-finite values.
Results may differ from a plain program's by a relative error of at most 0.023.
Values may be sent and summed in bfloat16 or wider, within the bound.
No kernel may reach another device: no remote copies, remote signals or barrier semaphores. Data moves between devices by JAX's collectives and lax.ppermute only.
A program may use at most 256 MiB of HBM per device.

v0:
```python
import math

import jax
import jax.numpy as jnp
from jax import lax
from jax.sharding import PartitionSpec as P

HEADS = 16
RAMP = 1000


def norm_rows(values, gain, shift):
    center = values - jnp.mean(values, -1, keepdims=True)
    spread = jnp.mean(center * center, -1, keepdims=True)
    return center * lax.rsqrt(spread + 1e-05) * gain + shift


def norm_back(values, gain, shift, cotangent):
    _, pull = jax.vjp(norm_rows, values, gain, shift)
    return pull(cotangent)


def matmul(left, right):
    return jnp.dot(left, right, preferred_element_type=jnp.float32)


def matmul_right_t(left, right):
    return lax.dot_general(
        left, right, (((1,), (1,)), ((), ())), preferred_element_type=jnp.float32
    )


def matmul_left_t(left, right):
    return lax.dot_general(
        left, right, (((0,), (0,)), ((), ())), preferred_element_type=jnp.float32
    )


def round_trip(values):
    return lax.optimization_barrier(values.astype(jnp.bfloat16)).astype(jnp.float32)


def split_heads(values):
    return values.reshape(values.shape[0], values.shape[1], HEADS, values.shape[2] // HEADS)


def block_scores(query_block, key_heads, mask_fn, start, block_rows, score_scale):
    scores = (
        jnp.einsum("sbhe,skhe->shbk", query_block, key_heads, preferred_element_type=jnp.float32)
        * score_scale
    )
    return jnp.where(mask_fn(start, block_rows), scores, -1e30)


def attend_forward(queries, key_rows, value_rows, mask_fn):
    sequences, row_count, model_width = queries.shape
    head_size = model_width // HEADS
    block_rows = min(512, row_count)
    block_count = row_count // block_rows
    score_scale = head_size ** (-0.5)
    key_heads = split_heads(key_rows)
    value_heads = split_heads(value_rows)
    query_blocks = split_heads(queries).reshape(
        sequences, block_count, block_rows, HEADS, head_size
    )

    def one_block(block_index):
        query_block = lax.dynamic_index_in_dim(query_blocks, block_index, 1, keepdims=False)
        scores = block_scores(
            query_block, key_heads, mask_fn, block_index * block_rows, block_rows, score_scale
        )
        row_max = jnp.max(scores, -1, keepdims=True)
        expo = jnp.exp(scores - row_max)
        row_total = jnp.sum(expo, -1, keepdims=True)
        probability = (expo / row_total).astype(jnp.bfloat16)
        mixed = jnp.einsum(
            "shbk,skhe->sbhe", probability, value_heads, preferred_element_type=jnp.float32
        )
        return (mixed.astype(jnp.bfloat16), (row_max + jnp.log(row_total))[..., 0])

    mixed_blocks, log_totals = lax.map(one_block, jnp.arange(block_count))
    context = jnp.moveaxis(mixed_blocks, 0, 1).reshape(sequences, row_count, model_width)
    return (context, log_totals)


def attend_backward(queries, key_rows, value_rows, log_totals, grad_context, mask_fn):
    sequences, row_count, model_width = queries.shape
    head_size = model_width // HEADS
    block_rows = min(512, row_count)
    block_count = row_count // block_rows
    score_scale = head_size ** (-0.5)
    key_heads = split_heads(key_rows)
    value_heads = split_heads(value_rows)
    query_blocks = split_heads(queries).reshape(
        sequences, block_count, block_rows, HEADS, head_size
    )
    grad_blocks = split_heads(grad_context).reshape(
        sequences, block_count, block_rows, HEADS, head_size
    )

    def one_block(carry, items):
        grad_keys, grad_values = carry
        block_index, block_lse = items
        query_block = lax.dynamic_index_in_dim(query_blocks, block_index, 1, keepdims=False)
        grad_block = lax.dynamic_index_in_dim(grad_blocks, block_index, 1, keepdims=False)
        scores = block_scores(
            query_block, key_heads, mask_fn, block_index * block_rows, block_rows, score_scale
        )
        probability = jnp.exp(scores - block_lse[..., None])
        grad_values = grad_values + jnp.einsum(
            "shbk,sbhe->skhe",
            probability.astype(jnp.bfloat16),
            grad_block,
            preferred_element_type=jnp.float32,
        )
        grad_prob = round_trip(
            jnp.einsum(
                "sbhe,skhe->shbk", grad_block, value_heads, preferred_element_type=jnp.float32
            )
        )
        row_dot = jnp.sum(probability * grad_prob, -1, keepdims=True)
        grad_scores = (probability * (grad_prob - row_dot)).astype(jnp.bfloat16)
        grad_query = (
            jnp.einsum(
                "shbk,skhe->sbhe", grad_scores, key_heads, preferred_element_type=jnp.float32
            )
            * score_scale
        )
        grad_keys = (
            grad_keys
            + jnp.einsum(
                "shbk,sbhe->skhe", grad_scores, query_block, preferred_element_type=jnp.float32
            )
            * score_scale
        )
        return ((grad_keys, grad_values), grad_query.astype(jnp.bfloat16))

    empty = jnp.zeros(key_heads.shape, jnp.float32)
    (grad_keys, grad_values), grad_query = lax.scan(
        one_block, (empty, empty), (jnp.arange(block_count), log_totals)
    )
    grad_query = jnp.moveaxis(grad_query, 0, 1).reshape(sequences, row_count, model_width)
    key_shape = key_rows.shape
    return (
        grad_query,
        grad_keys.astype(jnp.bfloat16).reshape(key_shape),
        grad_values.astype(jnp.bfloat16).reshape(key_shape),
    )


def local(
    inputs,
    encoder,
    grad_out,
    target_mask,
    source_lengths,
    step,
    attn_in,
    attn_out,
    ffn_in,
    ffn_in_bias,
    ffn_out,
    ffn_out_bias,
    attn_bias,
    norm_gain,
    norm_shift,
    adapter_down,
    adapter_down_bias,
    adapter_up,
    adapter_up_bias,
    adapter_gain,
    adapter_shift,
):
    sequences, row_count, model_width = inputs.shape
    source_count = encoder.shape[1]
    frozen = (
        lax.all_gather(attn_in, "fsdp", axis=0, tiled=True),
        lax.all_gather(attn_out, "fsdp", axis=0, tiled=True),
        lax.all_gather(ffn_in, "fsdp", axis=0, tiled=True),
        lax.all_gather(ffn_out, "fsdp", axis=0, tiled=True),
    )
    proj_in, proj_out, first_w, second_w = frozen
    ramp = 4.0 * step[0].astype(jnp.float32) / RAMP
    positions = jnp.arange(row_count, dtype=jnp.int32)
    live_keys = target_mask > 0
    source_slots = jnp.arange(source_count, dtype=jnp.int32)
    open_keys = source_slots[None, :] < source_lengths[:, None]

    def self_mask(start, block_rows):
        query_pos = start + jnp.arange(block_rows, dtype=jnp.int32)
        causal = positions[None, :] <= query_pos[:, None]
        return causal[None, None] & live_keys[:, None, None, :]

    def cross_mask(start, block_rows):
        return open_keys[:, None, None, :]

    token_rows = inputs.reshape(-1, model_width)
    self_proj = matmul(token_rows, proj_in[:, 0 : 3 * model_width])
    self_q = (self_proj[:, 0:model_width] + attn_bias[0]).astype(jnp.bfloat16).reshape(inputs.shape)
    self_k = self_proj[:, model_width : 2 * model_width].astype(jnp.bfloat16).reshape(inputs.shape)
    self_v = (
        (self_proj[:, 2 * model_width :] + attn_bias[1]).astype(jnp.bfloat16).reshape(inputs.shape)
    )
    self_ctx, self_lse = attend_forward(self_q, self_k, self_v, self_mask)
    sum_one = (
        token_rows.astype(jnp.float32)
        + matmul(self_ctx.reshape(-1, model_width), proj_out[:, 0:model_width])
        + attn_bias[2]
    )
    hidden_one = norm_rows(sum_one, norm_gain[0], norm_shift[0])
    cross_q = (
        (
            matmul(hidden_one.astype(jnp.bfloat16), proj_in[:, 3 * model_width : 4 * model_width])
            + attn_bias[3]
        )
        .astype(jnp.bfloat16)
        .reshape(inputs.shape)
    )
    state_rows = encoder.reshape(-1, model_width)
    cross_proj = matmul(state_rows, proj_in[:, 4 * model_width : 6 * model_width])
    cross_k = cross_proj[:, 0:model_width].astype(jnp.bfloat16).reshape(encoder.shape)
    cross_v = (
        (cross_proj[:, model_width:] + attn_bias[4]).astype(jnp.bfloat16).reshape(encoder.shape)
    )
    cross_ctx, cross_lse = attend_forward(cross_q, cross_k, cross_v, cross_mask)
    sum_two = (
        hidden_one
        + matmul(cross_ctx.reshape(-1, model_width), proj_out[:, model_width:])
        + attn_bias[5]
    )
    hidden_two = norm_rows(sum_two, norm_gain[1], norm_shift[1])
    pre_act = matmul(hidden_two.astype(jnp.bfloat16), first_w) + ffn_in_bias
    activation = jax.nn.gelu(pre_act, approximate=False).astype(jnp.bfloat16)
    ffn_part = matmul(activation, second_w) + ffn_out_bias
    adapt_in = norm_rows(hidden_two, adapter_gain, adapter_shift).astype(jnp.bfloat16)
    lower = matmul(adapt_in, adapter_down) + adapter_down_bias
    adapt_act = jax.nn.silu(lower).astype(jnp.bfloat16)
    branch = matmul(adapt_act, adapter_up) + adapter_up_bias
    sum_three = hidden_two + ffn_part + ramp * branch
    layer_out = (
        norm_rows(sum_three, norm_gain[2], norm_shift[2]).astype(jnp.bfloat16).reshape(inputs.shape)
    )
    back_in, back_out, back_first, back_second = (
        lax.all_gather(attn_in, "fsdp", axis=0, tiled=True),
        lax.all_gather(attn_out, "fsdp", axis=0, tiled=True),
        lax.all_gather(ffn_in, "fsdp", axis=0, tiled=True),
        lax.all_gather(ffn_out, "fsdp", axis=0, tiled=True),
    )
    grad_rows = grad_out.reshape(-1, model_width).astype(jnp.float32)
    d_sum_three = norm_back(sum_three, norm_gain[2], norm_shift[2], grad_rows)[0]
    d_act = round_trip(matmul_right_t(d_sum_three.astype(jnp.bfloat16), back_second))
    _, gelu_pull = jax.vjp(lambda values: jax.nn.gelu(values, approximate=False), pre_act)
    d_pre = gelu_pull(d_act)[0].astype(jnp.bfloat16)
    d_hidden_two = d_sum_three + matmul_right_t(d_pre, back_first)
    d_branch = (ramp * d_sum_three).astype(jnp.bfloat16)
    grad_up = matmul_left_t(adapt_act, d_branch)
    grad_up_bias = jnp.sum(d_branch.astype(jnp.float32), 0)
    d_adapt_act = round_trip(matmul_right_t(d_branch, adapter_up))
    _, silu_pull = jax.vjp(jax.nn.silu, lower)
    d_lower = silu_pull(d_adapt_act)[0].astype(jnp.bfloat16)
    grad_down = matmul_left_t(adapt_in, d_lower)
    grad_down_bias = jnp.sum(d_lower.astype(jnp.float32), 0)
    d_adapt = matmul_right_t(d_lower, adapter_down)
    d_hidden_adapter, grad_gain, grad_shift = norm_back(
        hidden_two, adapter_gain, adapter_shift, d_adapt
    )
    d_hidden_two = d_hidden_two + d_hidden_adapter
    d_sum_two = norm_back(sum_two, norm_gain[1], norm_shift[1], d_hidden_two)[0]
    d_cross_ctx = (
        matmul_right_t(d_sum_two.astype(jnp.bfloat16), back_out[:, model_width:])
        .astype(jnp.bfloat16)
        .reshape(inputs.shape)
    )
    d_cross_q, d_cross_k, d_cross_v = attend_backward(
        cross_q, cross_k, cross_v, cross_lse, d_cross_ctx, cross_mask
    )
    d_states = jnp.concatenate([d_cross_k, d_cross_v], -1).reshape(-1, 2 * model_width)
    grad_encoder = matmul_right_t(d_states, back_in[:, 4 * model_width : 6 * model_width]).reshape(
        encoder.shape
    )
    d_hidden_one = d_sum_two + matmul_right_t(
        d_cross_q.reshape(-1, model_width), back_in[:, 3 * model_width : 4 * model_width]
    )
    d_sum_one = norm_back(sum_one, norm_gain[0], norm_shift[0], d_hidden_one)[0]
    d_self_ctx = (
        matmul_right_t(d_sum_one.astype(jnp.bfloat16), back_out[:, 0:model_width])
        .astype(jnp.bfloat16)
        .reshape(inputs.shape)
    )
    d_self_q, d_self_k, d_self_v = attend_backward(
        self_q, self_k, self_v, self_lse, d_self_ctx, self_mask
    )
    d_tokens = jnp.concatenate([d_self_q, d_self_k, d_self_v], -1).reshape(-1, 3 * model_width)
    grad_input = (d_sum_one + matmul_right_t(d_tokens, back_in[:, 0 : 3 * model_width])).reshape(
        inputs.shape
    )
    summed = lax.psum(
        (grad_down, grad_down_bias, grad_up, grad_up_bias, grad_gain, grad_shift), ("fsdp", "dp")
    )
    token_total = sequences * row_count * lax.axis_size("fsdp") * lax.axis_size("dp")
    factor = 1.0 / math.sqrt(token_total)
    return (
        layer_out,
        grad_input,
        grad_encoder,
        summed[0] * factor,
        summed[1] * factor,
        summed[2] * factor,
        summed[3] * factor,
        summed[4] * factor,
        summed[5] * factor,
    )


def solution(mesh):
    placed = (
        P(("fsdp", "dp"), None, None),
        P(("fsdp", "dp"), None, None),
        P(("fsdp", "dp"), None, None),
        P(("fsdp", "dp"), None),
        P(("fsdp", "dp")),
        P(),
        P("fsdp", None),
        P("fsdp", None),
        P("fsdp", None),
        P(),
        P("fsdp", None),
        P(),
        P(),
        P(),
        P(),
        P(),
        P(),
        P(),
        P(),
        P(),
        P(),
    )
    return jax.shard_map(
        local,
        mesh=mesh,
        in_specs=placed,
        out_specs=(
            P(("fsdp", "dp"), None, None),
            P(("fsdp", "dp"), None, None),
            P(("fsdp", "dp"), None, None),
            P(),
            P(),
            P(),
            P(),
            P(),
            P(),
        ),
        check_vma=False,
    )
```

profile of v0, /device:TPU:0, one launch (start us, length us, event | category | flops | bytes accessed | tf_op | source)
XLA Modules:
  0.0 1163.5 jit_solution(2257706667867733053)
XLA Ops:
  22.2 91.6 %all-gather.5.cloned.1.call-done = bf16[1024,6144]{1,0:T(8,128)(2,1)} async-done(((bf16[64,6144]{1,0:T(8,128)(2,1)}), bf16[1024,6144]{1,0:T(8,128)(2,1)}) %all-gather.5.cloned.1.call-update) | async-done | bytes 12582928 | tf_op jit(solution)/shard_map/all_gather | solution.py:177
  113.8 9.4 fusion.148
  128.2 6.4 reshape.540
  134.5 5.4 copy.53
  149.6 100.8 %while.56 = (s32[]{:T(128)}, bf16[2,1,512,16,64]{2,4,3,1,0:T(8,128)(2,1)}, f32[2,1,16,512]{3,2,1,0:T(8,128)S(1)}, s32[2]{0:T(128)S(1)}, pred[1,1024]{1,0:T(4,128...) while((s32[]{:T(128)}, ...), condition=%wide.region_3.4_spmd.clone, body=%wide.region_0.3_spmd.clone.sunk | while | flops 2249712128 | bytes 117710560 | solution.py:81
  153.4 15.8 %fusion.284 = (f32[16,512]{1,0:T(8,128)S(1)}, f32[16,512,1024]{2,1,0:T(8,128)}) fusion(pred[512,1024]{1,0:T(8,128)(4,1)S(1)} %fusion.283, bf16[1,1024,16,64]{1,3,2,0:T(8,128)(2,1)} %get-tuple-element.857, bf16[1,2,512,16,64]{2,4,3,1,0:T(8,128)(2,1)} %get-tuple-element.856, s32[]{:T(128)S(6)} %select_n.116), kind=kOutput, calls=%fused_computation.7.clone.1 | convolution fusion | flops 1098899456 | bytes 37257220 | tf_op jit(solution)/shard_map/while/body/eval_jaxpr/sbhe,skhe->shbk/dot_general | solution.py:49
  169.2 15.4 %fusion.285 = f32[16,512]{1,0:T(8,128)S(1)} fusion(f32[16,512,1024]{2,1,0:T(8,128)} %get-tuple-element.787, f32[16,512]{1,0:T(8,128)S(1)} %get-tuple-element.788, pred[512,1024]{1,0:T(8,128)(4,1)S(1)} %fusion.283), kind=kLoop, calls=%fused_computation.8.clone.1 | loop fusion | flops 33546240 | bytes 34144256 | tf_op jit(solution)/shard_map/while/body/eval_jaxpr/reduce_sum | solution.py:74
  184.6 15.3 %fusion.286 = bf16[2,1,512,16,64]{2,4,3,1,0:T(8,128)(2,1)} fusion(bf16[2,1,512,16,64]{2,4,3,1,0:T(8,128)(2,1)} %get-tuple-element.839, s32[]{:T(128)} %get-tuple-element.838, bf16[1,1024,16,64]{1,3,2,0:T(8,128)(2,1)S(1)} %copy-done.9, f32[16,512,1024]{2,1,0:T(8,128)} %get-tuple-element.787, f32[16,512]{1,0:T(8,128)S(1)} %fusion.285, ...), kind=kOutput, calls=%fused_computation.17.clone.1 | convolution fusion | flops 1116209152 | bytes 37290496 | tf_op jit(solution)/shard_map/while/body/eval_jaxpr/shbk,skhe->sbhe/dot_general | solution.py:76
  203.5 15.7 %fusion.284 = (f32[16,512]{1,0:T(8,128)S(1)}, f32[16,512,1024]{2,1,0:T(8,128)}) fusion(pred[512,1024]{1,0:T(8,128)(4,1)S(1)} %fusion.283, bf16[1,1024,16,64]{1,3,2,0:T(8,128)(2,1)} %get-tuple-element.857, bf16[1,2,512,16,64]{2,4,3,1,0:T(8,128)(2,1)} %get-tuple-element.856, s32[]{:T(128)S(6)} %select_n.116), kind=kOutput, calls=%fused_computation.7.clone.1 | convolution fusion | flops 1098899456 | bytes 37257220 | tf_op jit(solution)/shard_map/while/body/eval_jaxpr/sbhe,skhe->shbk/dot_general | solution.py:49
  219.2 15.4 %fusion.285 = f32[16,512]{1,0:T(8,128)S(1)} fusion(f32[16,512,1024]{2,1,0:T(8,128)} %get-tuple-element.787, f32[16,512]{1,0:T(8,128)S(1)} %get-tuple-element.788, pred[512,1024]{1,0:T(8,128)(4,1)S(1)} %fusion.283), kind=kLoop, calls=%fused_computation.8.clone.1 | loop fusion | flops 33546240 | bytes 34144256 | tf_op jit(solution)/shard_map/while/body/eval_jaxpr/reduce_sum | solution.py:74
  234.7 15.4 %fusion.286 = bf16[2,1,512,16,64]{2,4,3,1,0:T(8,128)(2,1)} fusion(bf16[2,1,512,16,64]{2,4,3,1,0:T(8,128)(2,1)} %get-tuple-element.839, s32[]{:T(128)} %get-tuple-element.838, bf16[1,1024,16,64]{1,3,2,0:T(8,128)(2,1)S(1)} %copy-done.9, f32[16,512,1024]{2,1,0:T(8,128)} %get-tuple-element.787, f32[16,512]{1,0:T(8,128)S(1)} %fusion.285, ...), kind=kOutput, calls=%fused_computation.17.clone.1 | convolution fusion | flops 1116209152 | bytes 37290496 | tf_op jit(solution)/shard_map/while/body/eval_jaxpr/shbk,skhe->sbhe/dot_general | solution.py:76
  256.1 5.5 fusion.222
  263.7 5.6 add_convert_fusion.2
  269.3 6.3 reshape.541
  275.7 5.4 copy.58
  281.1 6.5 fusion.160
  296.9 95.5 %while.57 = (s32[]{:T(128)}, bf16[2,1,512,16,64]{2,4,3,1,0:T(8,128)(2,1)}, f32[2,1,16,512]{3,2,1,0:T(8,128)S(1)}, s32[2]{0:T(128)S(1)}, bf16[1,2,512,16,64]{2,4,...) while((s32[]{:T(128)}, ...), condition=%wide.region_9.10_spmd.clone, body=%wide.region_6.9_spmd.clone.sunk | while | flops 2248664064 | bytes 115610304 | solution.py:81
  300.1 15.4 %fusion.288 = (f32[16,512]{1,0:T(8,128)S(1)}, f32[16,512,1024]{2,1,0:T(8,128)}) fusion(pred[1024]{0:T(1024)(128)(4,1)S(1)} %compare_reduce_fusion.4, bf16[1,1024,16,64]{1,3,2,0:T(8,128)(2,1)S(1)} %get-tuple-element.891, bf16[1,2,512,16,64]{2,4,3,1,0:T(8,128)(2,1)} %get-tuple-element.890, s32[]{:T(128)S(6)} %select_n.120), kind=kOutput, calls=%fused_computation.28.clone.1 | convolution fusion | flops 1098899456 | bytes 36733956 | tf_op jit(solution)/shard_map/while/body/eval_jaxpr/sbhe,skhe->shbk/dot_general | solution.py:49
  315.5 14.7 %fusion.289 = f32[16,512]{1,0:T(8,128)S(1)} fusion(f32[16,512,1024]{2,1,0:T(8,128)} %get-tuple-element.797, f32[16,512]{1,0:T(8,128)S(1)} %get-tuple-element.798, pred[1024]{0:T(1024)(128)(4,1)S(1)} %compare_reduce_fusion.4), kind=kLoop, calls=%fused_computation.29.clone.1 | loop fusion | flops 33546240 | bytes 33620992 | tf_op jit(solution)/shard_map/while/body/eval_jaxpr/reduce_sum | solution.py:74
  330.3 14.6 %fusion.290 = bf16[2,1,512,16,64]{2,4,3,1,0:T(8,128)(2,1)} fusion(bf16[2,1,512,16,64]{2,4,3,1,0:T(8,128)(2,1)} %get-tuple-element.876, s32[]{:T(128)} %get-tuple-element.875, bf16[1,1024,16,64]{1,3,2,0:T(8,128)(2,1)S(1)} %copy-done.10, f32[16,512,1024]{2,1,0:T(8,128)} %get-tuple-element.797, f32[16,512]{1,0:T(8,128)S(1)} %fusion.289, ...), kind=kOutput, calls=%fused_computation.36.clone.1 | convolution fusion | flops 1116209152 | bytes 36767232 | tf_op jit(solution)/shard_map/while/body/eval_jaxpr/shbk,skhe->sbhe/dot_general | solution.py:76
  348.1 14.9 %fusion.288 = (f32[16,512]{1,0:T(8,128)S(1)}, f32[16,512,1024]{2,1,0:T(8,128)}) fusion(pred[1024]{0:T(1024)(128)(4,1)S(1)} %compare_reduce_fusion.4, bf16[1,1024,16,64]{1,3,2,0:T(8,128)(2,1)S(1)} %get-tuple-element.891, bf16[1,2,512,16,64]{2,4,3,1,0:T(8,128)(2,1)} %get-tuple-element.890, s32[]{:T(128)S(6)} %select_n.120), kind=kOutput, calls=%fused_computation.28.clone.1 | convolution fusion | flops 1098899456 | bytes 36733956 | tf_op jit(solution)/shard_map/while/body/eval_jaxpr/sbhe,skhe->shbk/dot_general | solution.py:49
  363.0 14.7 %fusion.289 = f32[16,512]{1,0:T(8,128)S(1)} fusion(f32[16,512,1024]{2,1,0:T(8,128)} %get-tuple-element.797, f32[16,512]{1,0:T(8,128)S(1)} %get-tuple-element.798, pred[1024]{0:T(1024)(128)(4,1)S(1)} %compare_reduce_fusion.4), kind=kLoop, calls=%fused_computation.29.clone.1 | loop fusion | flops 33546240 | bytes 33620992 | tf_op jit(solution)/shard_map/while/body/eval_jaxpr/reduce_sum | solution.py:74
  377.8 14.6 %fusion.290 = bf16[2,1,512,16,64]{2,4,3,1,0:T(8,128)(2,1)} fusion(bf16[2,1,512,16,64]{2,4,3,1,0:T(8,128)(2,1)} %get-tuple-element.876, s32[]{:T(128)} %get-tuple-element.875, bf16[1,1024,16,64]{1,3,2,0:T(8,128)(2,1)S(1)} %copy-done.10, f32[16,512,1024]{2,1,0:T(8,128)} %get-tuple-element.797, f32[16,512]{1,0:T(8,128)S(1)} %fusion.289, ...), kind=kOutput, calls=%fused_computation.36.clone.1 | convolution fusion | flops 1116209152 | bytes 36767232 | tf_op jit(solution)/shard_map/while/body/eval_jaxpr/shbk,skhe->sbhe/dot_general | solution.py:76
  392.5 4.6 copy.59
  397.7 4.7 fusion.223
  412.3 46.7 %fusion.131 = (f32[1024,4096]{1,0:T(8,128)}, f32[1024,4096]{1,0:T(8,128)}) fusion(f32[4096]{0:T(1024)S(1)} %copy-done.84, bf16[1024,4096]{1,0:T(8,128)(2,1)} %all-gather.9.cloned.1.call-done, bf16[1024,1024]{0,1:T(8,128)(2,1)} %fusion.182.clone.4), kind=kOutput, calls=%fused_computation.130 | convolution fusion | flops 8854175744 | bytes 44056576 | tf_op jit(solution)/shard_map/dot_general | solution.py:24
  459.1 20.6 %fusion.137 = f32[1024,1024]{0,1:T(8,128)} fusion(bf16[4096,1024]{1,0:T(8,128)(2,1)} %all-gather.11.cloned.1.call-done, f32[1024,4096]{1,0:T(8,128)} %get-tuple-element.566, f32[1024,4096]{1,0:T(8,128)} %get-tuple-element.567, f32[4096]{0:T(1024)S(1)} %copy-done.84), kind=kOutput, calls=%fused_computation.145 | convolution fusion | flops 8606711808 | bytes 46153728 | tf_op jit(solution)/shard_map/dot_general | solution.py:24
  479.9 4.9 fusion.224
  503.6 16.7 %convolution_convert_fusion = bf16[1024,4096]{1,0:T(8,128)(2,1)} fusion(bf16[4096,1024]{1,0:T(8,128)(2,1)} %all-gather.11.cloned.1.call-done, f32[1024]{0:T(1024)S(1)} %negate_multiply_fusion.4, f32[1024,1024]{0,1:T(8,128)} %copy-done.11, bf16[1,1024,1024]{1,2,0:T(8,128)(2,1)S(1)} %copy-done.12, f32[1024]{0:T(1024)S(1)} %get-tuple-element.560, ...), kind=kOutput, calls=%fused_computation.149 | convolution fusion | flops 8603566080 | bytes 23089152 | tf_op jit(solution)/shard_map/dot_general | solution.py:28
  520.3 4.7 multiply_reduce_fusion
  525.0 27.0 %multiply_reduce_fusion.2 = (f32[1024]{0:T(1024)S(1)}, f32[1024,1024]{0,1:T(8,128)}) fusion(f32[1024,1024]{0,1:T(8,128)S(1)} %copy-done.8, f32[1024]{0:T(1024)S(1)} %copy-done.33, f32[1024]{0:T(1024)S(1)} %negate_multiply_fusion.3, f32[1024]{0:T(1024)S(1)} %multiply_multiply_fusion.7, f32[1024]{0:T(1024)S(1)} %copy-done.41, f32[1024]{0:T(1024)S(1)} %bitcast.405, ...), kind=kOutput, calls=%fused_computation.184 | convolution fusion | flops 8682208256 | bytes 69283840 | tf_op jit(solution)/shard_map/dot_general | solution.py:28
  563.8 5.6 copy.63
  571.0 198.5 %while.58 = (s32[]{:T(128)}, f32[1,1024,16,64]{1,3,2,0:T(8,128)}, f32[1,1024,16,64]{1,3,2,0:T(8,128)}, bf16[2,1,512,16,64]{2,4,3,1,0:T(8,128)(2,1)}, s32[2]{0:T(...) while((s32[]{:T(128)}, f32[1,1024,16,64]{1,3,2,0:T(8,128)}, ...), condition=%wide.region_24.25_spmd.clone, body=%wide.region_22.24_spmd.clone.sunk | while | flops 5525988352 | bytes 229872336 | solution.py:139
  573.9 12.2 %convert_bitcast_fusion.4 = bf16[1,16,512,1024]{3,2,1,0:T(8,128)(2,1)} fusion(bf16[1,1024,16,64]{1,3,2,0:T(8,128)(2,1)} %get-tuple-element.934, bf16[1,2,512,16,64]{2,4,3,1,0:T(8,128)(2,1)} %get-tuple-element.933, s32[]{:T(128)S(6)} %select_n.124), kind=kOutput, calls=%fused_computation.52.clone.1 | convolution fusion | flops 1082130432 | bytes 19922948 | tf_op jit(solution)/shard_map/while/body/eval_jaxpr/sbhe,skhe->shbk/dot_general | solution.py:117
  586.7 20.2 %fusion.299 = (f32[16,512]{1,0:T(8,128)S(1)}, f32[16,512,1024]{2,1,0:T(8,128)}) fusion(bf16[1,16,512,1024]{3,2,1,0:T(8,128)(2,1)} %convert_bitcast_fusion.4, f32[16,512]{1,0:T(8,128)S(1)} %dynamic-slice_bitcast_fusion.4, pred[1024]{0:T(1024)(128)(4,1)S(1)} %compare_reduce_fusion.5, bf16[1,1024,16,64]{1,3,2,0:T(8,128)(2,1)S(1)} %get-tuple-element.931, ...), kind=kOutput, calls=%fused_computation.46.clone.1 | convolution fusion | flops 1124065280 | bytes 53543940 | tf_op jit(solution)/shard_map/while/body/eval_jaxpr/sbhe,skhe->shbk/dot_general | solution.py:49
  606.9 24.2 %fusion.300 = bf16[16,512,1024]{2,1,0:T(8,128)(2,1)} fusion(bf16[1,16,512,1024]{3,2,1,0:T(8,128)(2,1)} %convert_bitcast_fusion.4, f32[16,512,1024]{2,1,0:T(8,128)} %get-tuple-element.810, f32[16,512]{1,0:T(8,128)S(1)} %get-tuple-element.811, f32[16,512]{1,0:T(8,128)S(1)} %dynamic-slice_bitcast_fusion.4, pred[1024]{0:T(1024)(128)(4,1)S(1)} %compare_reduce_fusion.5), kind=kLoop, calls=%fused_computation.51.clone.1 | loop fusion | flops 58720256 | bytes 67175424 | tf_op jit(solution)/shard_map/reshape.63
  631.1 11.1 bitcast_add_fusion.8
  642.2 9.7 fusion.301
  652.0 16.9 %bitcast_add_fusion.9 = f32[1,1024,16,64]{1,3,2,0:T(8,128)} fusion(f32[1,1024,16,64]{1,3,2,0:T(8,128)} %get-tuple-element.913, f32[16,512,1024]{2,1,0:T(8,128)} %get-tuple-element.810, f32[16,512]{1,0:T(8,128)S(1)} %dynamic-slice_bitcast_fusion.4, pred[1024]{0:T(1024)(128)(4,1)S(1)} %compare_reduce_fusion.5, pred[]{:T(512)S(6)} %compare.6, ...), kind=kOutput, calls=%fused_computation.55.clone.1 | convolution fusion | flops 1109393408 | bytes 43025412 | tf_op jit(solution)/shard_map/while/body/eval_jaxpr/shbk,sbhe->skhe/dot_general | solution.py:110
  671.5 12.2 %convert_bitcast_fusion.4 = bf16[1,16,512,1024]{3,2,1,0:T(8,128)(2,1)} fusion(bf16[1,1024,16,64]{1,3,2,0:T(8,128)(2,1)} %get-tuple-element.934, bf16[1,2,512,16,64]{2,4,3,1,0:T(8,128)(2,1)} %get-tuple-element.933, s32[]{:T(128)S(6)} %select_n.124), kind=kOutput, calls=%fused_computation.52.clone.1 | convolution fusion | flops 1082130432 | bytes 19922948 | tf_op jit(solution)/shard_map/while/body/eval_jaxpr/sbhe,skhe->shbk/dot_general | solution.py:117
  684.4 20.2 %fusion.299 = (f32[16,512]{1,0:T(8,128)S(1)}, f32[16,512,1024]{2,1,0:T(8,128)}) fusion(bf16[1,16,512,1024]{3,2,1,0:T(8,128)(2,1)} %convert_bitcast_fusion.4, f32[16,512]{1,0:T(8,128)S(1)} %dynamic-slice_bitcast_fusion.4, pred[1024]{0:T(1024)(128)(4,1)S(1)} %compare_reduce_fusion.5, bf16[1,1024,16,64]{1,3,2,0:T(8,128)(2,1)S(1)} %get-tuple-element.931, ...), kind=kOutput, calls=%fused_computation.46.clone.1 | convolution fusion | flops 1124065280 | bytes 53543940 | tf_op jit(solution)/shard_map/while/body/eval_jaxpr/sbhe,skhe->shbk/dot_general | solution.py:49
  704.6 24.2 %fusion.300 = bf16[16,512,1024]{2,1,0:T(8,128)(2,1)} fusion(bf16[1,16,512,1024]{3,2,1,0:T(8,128)(2,1)} %convert_bitcast_fusion.4, f32[16,512,1024]{2,1,0:T(8,128)} %get-tuple-element.810, f32[16,512]{1,0:T(8,128)S(1)} %get-tuple-element.811, f32[16,512]{1,0:T(8,128)S(1)} %dynamic-slice_bitcast_fusion.4, pred[1024]{0:T(1024)(128)(4,1)S(1)} %compare_reduce_fusion.5), kind=kLoop, calls=%fused_computation.51.clone.1 | loop fusion | flops 58720256 | bytes 67175424 | tf_op jit(solution)/shard_map/reshape.63
  728.8 12.3 %bitcast_add_fusion.8 = f32[1,1024,16,64]{1,3,2,0:T(8,128)} fusion(f32[1,1024,16,64]{1,3,2,0:T(8,128)} %get-tuple-element.912, bf16[16,512,1024]{2,1,0:T(8,128)(2,1)} %fusion.300, pred[]{:T(512)S(6)} %compare.6, bf16[1,2,512,16,64]{2,4,3,1,0:T(8,128)(2,1)} %get-tuple-element.930, s32[]{:T(128)S(6)} %select_n.124), kind=kOutput, calls=%fused_computation.56.clone.1 | convolution fusion | flops 1076887552 | bytes 26214404 | tf_op jit(solution)/shard_map/while/body/eval_jaxpr/shbk,sbhe->skhe/dot_general | solution.py:131
  741.1 9.7 fusion.301
  750.8 18.3 %bitcast_add_fusion.9 = f32[1,1024,16,64]{1,3,2,0:T(8,128)} fusion(f32[1,1024,16,64]{1,3,2,0:T(8,128)} %get-tuple-element.913, f32[16,512,1024]{2,1,0:T(8,128)} %get-tuple-element.810, f32[16,512]{1,0:T(8,128)S(1)} %dynamic-slice_bitcast_fusion.4, pred[1024]{0:T(1024)(128)(4,1)S(1)} %compare_reduce_fusion.5, pred[]{:T(512)S(6)} %compare.6, ...), kind=kOutput, calls=%fused_computation.55.clone.1 | convolution fusion | flops 1109393408 | bytes 43025412 | tf_op jit(solution)/shard_map/while/body/eval_jaxpr/shbk,sbhe->skhe/dot_general | solution.py:110
  788.6 5.6 copy.67
  795.7 203.4 %while.59 = (s32[]{:T(128)}, f32[1,1024,16,64]{1,3,2,0:T(8,128)}, f32[1,1024,16,64]{1,3,2,0:T(8,128)}, bf16[2,1,512,16,64]{2,4,3,1,0:T(8,128)(2,1)}, s32[2]{0:T(...) while((s32[]{:T(128)}, f32[1,1024,16,64]{1,3,2,0:T(8,128)}, ...), condition=%wide.region_29.30_spmd.clone, body=%wide.region_27.29_spmd.clone.sunk | while | flops 5527036416 | bytes 231972608 | solution.py:139
  798.4 12.2 %convert_bitcast_fusion.5 = bf16[1,16,512,1024]{3,2,1,0:T(8,128)(2,1)} fusion(bf16[1,1024,16,64]{1,3,2,0:T(8,128)(2,1)} %get-tuple-element.981, bf16[1,2,512,16,64]{2,4,3,1,0:T(8,128)(2,1)} %get-tuple-element.980, s32[]{:T(128)S(6)} %select_n.128), kind=kOutput, calls=%fused_computation.89.clone.1 | convolution fusion | flops 1082130432 | bytes 19922948 | tf_op jit(solution)/shard_map/while/body/eval_jaxpr/sbhe,skhe->shbk/dot_general | solution.py:117
  811.8 21.9 %fusion.311 = (f32[16,512]{1,0:T(8,128)S(1)}, f32[16,512,1024]{2,1,0:T(8,128)}) fusion(bf16[1,16,512,1024]{3,2,1,0:T(8,128)(2,1)} %convert_bitcast_fusion.5, f32[16,512]{1,0:T(8,128)S(1)} %dynamic-slice_bitcast_fusion.5, pred[512,1024]{1,0:T(8,128)(4,1)S(1)} %fusion.310, bf16[1,1024,16,64]{1,3,2,0:T(8,128)(2,1)S(1)} %get-tuple-element.978, ...), kind=kOutput, calls=%fused_computation.83.clone.1 | convolution fusion | flops 1124065280 | bytes 54067204 | tf_op jit(solution)/shard_map/while/body/eval_jaxpr/sbhe,skhe->shbk/dot_general | solution.py:49
  833.6 24.2 %fusion.312 = bf16[16,512,1024]{2,1,0:T(8,128)(2,1)} fusion(bf16[1,16,512,1024]{3,2,1,0:T(8,128)(2,1)} %convert_bitcast_fusion.5, f32[16,512,1024]{2,1,0:T(8,128)} %get-tuple-element.823, f32[16,512]{1,0:T(8,128)S(1)} %get-tuple-element.824, f32[16,512]{1,0:T(8,128)S(1)} %dynamic-slice_bitcast_fusion.5, pred[512,1024]{1,0:T(8,128)(4,1)S(1)} %fusion.310), kind=kLoop, calls=%fused_computation.88.clone.1 | loop fusion | flops 58720256 | bytes 67698688 | tf_op jit(solution)/shard_map/reshape.83
  857.8 11.1 bitcast_add_fusion.10
  869.0 9.7 fusion.313
  878.7 17.6 %bitcast_add_fusion.11 = f32[1,1024,16,64]{1,3,2,0:T(8,128)} fusion(f32[1,1024,16,64]{1,3,2,0:T(8,128)} %get-tuple-element.957, f32[16,512,1024]{2,1,0:T(8,128)} %get-tuple-element.823, f32[16,512]{1,0:T(8,128)S(1)} %dynamic-slice_bitcast_fusion.5, pred[512,1024]{1,0:T(8,128)(4,1)S(1)} %fusion.310, pred[]{:T(512)S(6)} %compare.7, ...), kind=kOutput, calls=%fused_computation.92.clone.1 | convolution fusion | flops 1109393408 | bytes 43548676 | tf_op jit(solution)/shard_map/while/body/eval_jaxpr/shbk,sbhe->skhe/dot_general | solution.py:110
  898.8 12.2 %convert_bitcast_fusion.5 = bf16[1,16,512,1024]{3,2,1,0:T(8,128)(2,1)} fusion(bf16[1,1024,16,64]{1,3,2,0:T(8,128)(2,1)} %get-tuple-element.981, bf16[1,2,512,16,64]{2,4,3,1,0:T(8,128)(2,1)} %get-tuple-element.980, s32[]{:T(128)S(6)} %select_n.128), kind=kOutput, calls=%fused_computation.89.clone.1 | convolution fusion | flops 1082130432 | bytes 19922948 | tf_op jit(solution)/shard_map/while/body/eval_jaxpr/sbhe,skhe->shbk/dot_general | solution.py:117
  912.1 21.8 %fusion.311 = (f32[16,512]{1,0:T(8,128)S(1)}, f32[16,512,1024]{2,1,0:T(8,128)}) fusion(bf16[1,16,512,1024]{3,2,1,0:T(8,128)(2,1)} %convert_bitcast_fusion.5, f32[16,512]{1,0:T(8,128)S(1)} %dynamic-slice_bitcast_fusion.5, pred[512,1024]{1,0:T(8,128)(4,1)S(1)} %fusion.310, bf16[1,1024,16,64]{1,3,2,0:T(8,128)(2,1)S(1)} %get-tuple-element.978, ...), kind=kOutput, calls=%fused_computation.83.clone.1 | convolution fusion | flops 1124065280 | bytes 54067204 | tf_op jit(solution)/shard_map/while/body/eval_jaxpr/sbhe,skhe->shbk/dot_general | solution.py:49
  933.9 24.2 %fusion.312 = bf16[16,512,1024]{2,1,0:T(8,128)(2,1)} fusion(bf16[1,16,512,1024]{3,2,1,0:T(8,128)(2,1)} %convert_bitcast_fusion.5, f32[16,512,1024]{2,1,0:T(8,128)} %get-tuple-element.823, f32[16,512]{1,0:T(8,128)S(1)} %get-tuple-element.824, f32[16,512]{1,0:T(8,128)S(1)} %dynamic-slice_bitcast_fusion.5, pred[512,1024]{1,0:T(8,128)(4,1)S(1)} %fusion.310), kind=kLoop, calls=%fused_computation.88.clone.1 | loop fusion | flops 58720256 | bytes 67698688 | tf_op jit(solution)/shard_map/reshape.83
  958.2 12.3 %bitcast_add_fusion.10 = f32[1,1024,16,64]{1,3,2,0:T(8,128)} fusion(f32[1,1024,16,64]{1,3,2,0:T(8,128)} %get-tuple-element.956, bf16[16,512,1024]{2,1,0:T(8,128)(2,1)} %fusion.312, pred[]{:T(512)S(6)} %compare.7, bf16[1,2,512,16,64]{2,4,3,1,0:T(8,128)(2,1)} %get-tuple-element.976, s32[]{:T(128)S(6)} %select_n.128), kind=kOutput, calls=%fused_computation.93.clone.1 | convolution fusion | flops 1076887552 | bytes 26214404 | tf_op jit(solution)/shard_map/while/body/eval_jaxpr/shbk,sbhe->skhe/dot_general | solution.py:131
  970.5 9.7 fusion.313
  980.2 18.7 %bitcast_add_fusion.11 = f32[1,1024,16,64]{1,3,2,0:T(8,128)} fusion(f32[1,1024,16,64]{1,3,2,0:T(8,128)} %get-tuple-element.957, f32[16,512,1024]{2,1,0:T(8,128)} %get-tuple-element.823, f32[16,512]{1,0:T(8,128)S(1)} %dynamic-slice_bitcast_fusion.5, pred[512,1024]{1,0:T(8,128)(4,1)S(1)} %fusion.310, pred[]{:T(512)S(6)} %compare.7, ...), kind=kOutput, calls=%fused_computation.92.clone.1 | convolution fusion | flops 1109393408 | bytes 43548676 | tf_op jit(solution)/shard_map/while/body/eval_jaxpr/shbk,sbhe->skhe/dot_general | solution.py:110
  1010.7 12.4 %add_bitcast_fusion = f32[1,1024,1024]{1,2,0:T(8,128)} fusion(f32[1024,1024]{0,1:T(8,128)} %copy-done.19, f32[1024]{0:T(1024)S(1)} %copy-done.72, bf16[1,1024,1024]{1,2,0:T(8,128)(2,1)} %bitcast.386, bf16[1,1024,1024]{1,2,0:T(8,128)(2,1)S(1)} %bitcast.385, bf16[1,1024,1024]{1,2,0:T(8,128)(2,1)} %reshape_transpose.3, ...), kind=kOutput, calls=%fused_computation.181 | convolution fusion | flops 6463422464 | bytes 20975616 | tf_op jit(solution)/shard_map/dot_general | solution.py:28
  1027.8 5.6 copy.71
  1036.0 39.3 %all-reduce = (f32[512]{0:T(512)S(1)}, f32[1024]{0:T(1024)S(1)}, f32[1024]{0:T(1024)S(1)}, f32[1024]{0:T(1024)S(1)}) all-reduce(f32[512]{0:T(512)S(1)} %copy-done.65, f32[1024]{0:T(1024)S(1)} %copy-done.57, f32[1024]{0:T(1024)S(1)} %copy-done.56, f32[1024]{0:T(1024)S(1)} %copy-done.67), channel_id=1, replica_groups=mesh['fsdp'=16,'dp'=2] {'fsdp','dp'}, use_global_device_ids=true, to_apply=%region_32.33 | all-reduce | flops 3584 | bytes 28672 | tf_op jit(solution)/shard_map/psum | solution.py:297
  1077.1 10.0 fusion.163
  1087.1 64.5 %all-reduce.4.cloned.1.call-done = (f32[1024,512]{1,0:T(8,128)}, f32[512,1024]{1,0:T(8,128)}) async-done(((f32[1024,512]{1,0:T(8,128)}, f32[512,1024]{1,0:T(8,128)}), (f32[1024,512]{1,0:T(8,128)}, f32[512,1024]{1,0:T(8,128)})) %all-reduce.4.cloned.1.call-update) | async-done | bytes 4194320 | tf_op jit(solution)/shard_map/psum | solution.py:297
  (305 shorter events, 143.5 us)
Async XLA Ops:
  7.2 273.9 %copy-start = (bf16[1,1024,1024]{2,1,0:T(8,128)(2,1)S(1)}, bf16[1,1024,1024]{2,1,0:T(8,128)(2,1)}, u32[]{:S(2)}) copy-start(bf16[1,1024,1024]{2,1,0:T(8,128)(2,1)} %param.30) | copy-start | bytes 6291460
  7.2 9.1 copy-start.63
  7.2 9.7 copy-start.64
  7.2 106.6 %all-gather.5.cloned.1.call-start = ((), (), s32[]{:S(2)}) async-start(), calls=%async_computation | async-start | bytes 13369344 | tf_op jit(solution)/shard_map/all_gather | solution.py:177
  7.9 248.2 %all-gather.7.cloned.1.call-start = ((), (), s32[]{:S(2)}) async-start(), calls=%async_computation.1 | async-start | bytes 4456448 | tf_op jit(solution)/shard_map/all_gather | solution.py:178
  8.7 403.6 %all-gather.9.cloned.1.call-start = ((), (), s32[]{:S(2)}) async-start(), calls=%async_computation.2 | async-start | bytes 8912896 | tf_op jit(solution)/shard_map/all_gather | solution.py:179
  9.4 449.6 %all-gather.11.cloned.1.call-start = ((), (), s32[]{:S(2)}) async-start(), calls=%async_computation.3 | async-start | bytes 8912896 | tf_op jit(solution)/shard_map/all_gather | solution.py:180
  10.0 1141.6 %all-reduce.4.cloned.1.call-start = ((), (), s32[]{:S(2)}) async-start(), calls=%async_computation.4 | async-start | bytes 8388608 | tf_op jit(solution)/shard_map/psum | solution.py:297
  169.2 15.4 %copy-start.9 = (bf16[1,1024,16,64]{1,3,2,0:T(8,128)(2,1)S(1)}, bf16[1,1024,16,64]{1,3,2,0:T(8,128)(2,1)}, u32[]{:S(2)}) copy-start(bf16[1,1024,16,64]{1,3,2,0:T(8,128)(2,1)} %get-tuple-element.858) | copy-start | bytes 6291460 | tf_op jit(solution)/shard_map/while
  219.2 15.5 %copy-start.9 = (bf16[1,1024,16,64]{1,3,2,0:T(8,128)(2,1)S(1)}, bf16[1,1024,16,64]{1,3,2,0:T(8,128)(2,1)}, u32[]{:S(2)}) copy-start(bf16[1,1024,16,64]{1,3,2,0:T(8,128)(2,1)} %get-tuple-element.858) | copy-start | bytes 6291460 | tf_op jit(solution)/shard_map/while
  250.4 5.7 copy-start.28
  250.4 5.7 copy-start.30
  250.4 5.7 copy-start.70
  315.5 14.8 %copy-start.10 = (bf16[1,1024,16,64]{1,3,2,0:T(8,128)(2,1)S(1)}, bf16[1,1024,16,64]{1,3,2,0:T(8,128)(2,1)}, u32[]{:S(2)}) copy-start(bf16[1,1024,16,64]{1,3,2,0:T(8,128)(2,1)} %get-tuple-element.892) | copy-start | bytes 6291460 | tf_op jit(solution)/shard_map/while
  363.0 14.8 %copy-start.10 = (bf16[1,1024,16,64]{1,3,2,0:T(8,128)(2,1)S(1)}, bf16[1,1024,16,64]{1,3,2,0:T(8,128)(2,1)}, u32[]{:S(2)}) copy-start(bf16[1,1024,16,64]{1,3,2,0:T(8,128)(2,1)} %get-tuple-element.892) | copy-start | bytes 6291460 | tf_op jit(solution)/shard_map/while
  392.4 5.2 copy-start.4
  392.4 5.2 copy-start.26
  392.4 5.2 copy-start.14
  392.4 5.2 copy-start.46
  392.4 5.2 copy-start.59
  392.4 5.2 copy-start.68
  392.4 5.2 copy-start.75
  392.4 5.2 copy-start.77
  402.4 7.9 copy-start.6
  402.4 7.8 copy-start.32
  402.9 7.3 copy-start.34
  403.2 2.9 copy-start.54
  403.2 2.9 copy-start.66
  403.9 3.8 copy-start.40
  407.6 4.6 copy-start.22
  459.0 20.7 %copy-start.7 = (f32[1024,1024]{0,1:T(8,128)S(1)}, f32[1024,1024]{0,1:T(8,128)}, u32[]{:S(2)}) copy-start(f32[1024,1024]{0,1:T(8,128)} %copy-done.6) | copy-start | bytes 12582916
  459.0 20.7 %copy-start.24 = (f32[1024,512]{1,0:T(8,128)S(1)}, f32[1024,512]{1,0:T(8,128)}, u32[]{:S(2)}) copy-start(f32[1024,512]{1,0:T(8,128)} %fusion.225) | copy-start | bytes 6291460
  459.0 20.7 %copy-start.33 = (f32[1024]{0:T(1024)S(1)}, f32[1024]{0:T(1024)}, u32[]{:S(2)}) copy-start(f32[1024]{0:T(1024)} %copy-done.32) | copy-start | bytes 12292
  459.0 20.7 %copy-start.35 = (f32[1024]{0:T(1024)S(1)}, f32[1024]{0:T(1024)}, u32[]{:S(2)}) copy-start(f32[1024]{0:T(1024)} %copy-done.34) | copy-start | bytes 12292
  459.1 20.7 %copy-start.37 = (f32[1,1024]{1,0:T(1,128)S(1)}, f32[1,1024]{1,0:T(1,128)}, u32[]{:S(2)}) copy-start(f32[1,1024]{1,0:T(1,128)} %get-tuple-element.556) | copy-start | bytes 12292
  459.1 20.7 %copy-start.39 = (f32[1,1024]{1,0:T(1,128)S(1)}, f32[1,1024]{1,0:T(1,128)}, u32[]{:S(2)}) copy-start(f32[1,1024]{1,0:T(1,128)} %get-tuple-element.559) | copy-start | bytes 12292
  459.1 20.7 %copy-start.78 = (f32[512]{0:T(512)S(1)}, f32[512]{0:T(512)}, u32[]{:S(2)}) copy-start(f32[512]{0:T(512)} %param.45) | copy-start | bytes 6148
  459.1 20.7 %copy-start.81 = (bf16[512,1024]{1,0:T(8,128)(2,1)S(1)}, bf16[512,1024]{1,0:T(8,128)(2,1)}, u32[]{:S(2)}) copy-start(bf16[512,1024]{1,0:T(8,128)(2,1)} %param.46) | copy-start | bytes 3145732
  459.1 20.7 %copy-start.85 = (f32[1024]{0:T(1024)S(1)}, f32[1024]{0:T(1024)}, u32[]{:S(2)}) copy-start(f32[1024]{0:T(1024)} %param.47) | copy-start | bytes 12292
  459.1 20.7 %copy-start.86 = (f32[1024]{0:T(1024)S(1)}, f32[1024]{0:T(1024)}, u32[]{:S(2)}) copy-start(f32[1024]{0:T(1024)} %param.40) | copy-start | bytes 12292
  479.8 4.9 copy-start.12
  479.8 4.9 copy-start.42
  494.0 4.3 copy-start.23
  503.6 16.7 %copy-start.8 = (f32[1024,1024]{0,1:T(8,128)S(1)}, f32[1024,1024]{0,1:T(8,128)}, u32[]{:S(2)}) copy-start(f32[1024,1024]{0,1:T(8,128)} %copy-done.6) | copy-start | bytes 12582916
  503.6 16.7 %copy-start.44 = (f32[1024]{0:T(1024)S(1)}, f32[1024]{0:T(1024)}, u32[]{:S(2)}) copy-start(f32[1024]{0:T(1024)} %copy-done.43) | copy-start | bytes 12292
  525.0 27.1 %copy-start.51 = (f32[1024]{0:T(1024)S(1)}, f32[1024]{0:T(1024)}, u32[]{:S(2)}) copy-start(f32[1024]{0:T(1024)} %copy-done.50) | copy-start | bytes 12292
  552.1 5.4 copy-start.79
  563.8 7.2 copy-start.5
  563.8 7.2 copy-start.27
  769.5 4.5 copy-start.47
  769.6 4.5 copy-start.15
  769.6 4.5 copy-start.21
  774.1 4.5 copy-start.49
  774.1 4.5 copy-start.60
  778.6 3.6 copy-start.80
  788.5 7.2 copy-start.3
  788.5 7.2 copy-start.29
  788.6 7.2 copy-start.31
  1005.6 3.4 copy-start.17
  1010.7 12.4 %copy-start.2 = (f32[1,1024,16,64]{1,3,2,0:T(8,128)S(1)}, f32[1,1024,16,64]{1,3,2,0:T(8,128)}, u32[]{:S(2)}) copy-start(f32[1,1024,16,64]{1,3,2,0:T(8,128)} %get-tuple-element.231) | copy-start | bytes 12582916
  1023.2 3.0 copy-start.18
  1027.8 5.6 copy-start.16
  1151.6 3.4 copy-start.25
  1151.6 5.0 copy-start.1
  (30 other events, 52.9 us)
Sparse Core Ops, SparseCore 0:
  10.3 103.4 all-gather.4
  116.0 48.7 all-gather.6
  166.9 73.3 all-gather.8
  242.4 73.1 all-gather.10
  1010.8 140.7 all-reduce.3
where the time goes:
time: 1170 us; the launch traced here: 1160 us
  matrix products  605 us (52%)
  other arithmetic  204 us (17%)
  waiting for transfers between devices  159 us (14%)
  local copies, waits for them, and re-layouts  120 us (10%)
  blocking collectives  39.3 us (3%)
  loops' own time  20 us (2%)
  between operations  15.9 us (1%)
    dot_general x8, matrix products, block_scores(): jnp.einsum('sbhe,skhe->shbk', query_block, key_heads, preferred_element_t...  146 us
    dot_general x9, matrix products, matmul(): return jnp.dot(left, right, preferred_element_type=jnp.float32)  107 us
    another operation x8, other arithmetic  96.8 us
    all_gather x1, waiting for transfers between devices, local(): lax.all_gather(attn_in, 'fsdp', axis=0, tiled=True)  91.6 us
    dot_general x9, matrix products, matmul_right_t(): lax.dot_general(left, right, (((1,), (1,)), ((), ())), preferred_element_...  81.1 us
    dot_general x4, matrix products, one_block(): jnp.einsum('shbk,sbhe->skhe', probability.astype(jnp.bfloat16), grad_bloc...  71.5 us
    psum x1, waiting for transfers between devices, local(): lax.psum((grad_down, grad_down_bias, grad_up, grad_up_bias, grad_gain, gr...  64.5 us
    reduce_sum x4, other arithmetic, one_block(): row_total = jnp.sum(expo, -1, keepdims=True)  60.2 us
  transfers between devices with their start and end apart: 5, of which 2 were waited for; matrix products, arithmetic and copies ran while one was open for 33% of the time, Pallas kernels for 0%

commit v1 on v0

v1 whole, which is shorter than its diff:
```python
import functools
import math

import jax
import jax.numpy as jnp
from jax import lax
from jax.experimental import pallas as pl
from jax.experimental.pallas import tpu as pltpu
from jax.sharding import PartitionSpec as P

HEADS = 16
RAMP = 1000
EPS = 1e-05
F32 = jnp.float32
BF16 = jnp.bfloat16
VMEM_LIMIT = 58 * 2**20


def dot(left, right, left_dim, right_dim):
    return lax.dot_general(
        left, right, (((left_dim,), (right_dim,)), ((), ())), preferred_element_type=F32
    )


def call(kernel, name, grid, in_specs, out_specs, out_shape, flops, moved, exps=0, scratch=()):
    return pl.pallas_call(
        kernel,
        name=name,
        grid=grid,
        in_specs=in_specs,
        out_specs=out_specs,
        out_shape=out_shape,
        scratch_shapes=scratch,
        compiler_params=pltpu.CompilerParams(vmem_limit_bytes=VMEM_LIMIT),
        cost_estimate=pl.CostEstimate(
            flops=int(flops), bytes_accessed=int(moved), transcendentals=int(exps)
        ),
    )


def whole(shape):
    return pl.BlockSpec(shape, lambda *_: (0,) * len(shape))


def rows_block(rows, width):
    return pl.BlockSpec((rows, width), lambda i: (i, 0))


def normalize(values):
    center = values - jnp.mean(values, -1, keepdims=True)
    scale = lax.rsqrt(jnp.mean(center * center, -1, keepdims=True) + EPS)
    return center * scale, scale


def normalize_back(normal, scale, grad):
    return scale * (
        grad
        - jnp.mean(grad, -1, keepdims=True)
        - normal * jnp.mean(grad * normal, -1, keepdims=True)
    )


def split_three(values):
    high = values.astype(BF16).astype(F32)
    middle = (values - high).astype(BF16).astype(F32)
    return high, middle, values - high - middle


def key_extra(live):
    lane = jnp.arange(128) % 64
    bias = jnp.where(live, 0.0, -1e30)[:, None]
    ones = jnp.where((lane >= 1) & (lane <= 3), 1.0, 0.0)[None]
    return jnp.where(lane[None] == 0, bias, ones).astype(BF16)


def attend_forward_kernel(causal, chunk, ahead, q_ref, k_ref, v_ref, extra_ref, out_ref, lse_ref):
    rows, width = q_ref.shape
    keys, half = k_ref.shape[0], width // 2
    lane = lax.broadcasted_iota(jnp.int32, (rows, width), 1)
    key_lane = lax.broadcasted_iota(jnp.int32, (keys, width), 1)
    queries = q_ref[...] * jnp.asarray(half**-0.5, BF16)
    picks = jnp.where(lane % half == 0, 1.0, 0.0).astype(BF16)
    key_rows, extra, value_rows = k_ref[...], extra_ref[...], v_ref[...]
    one = jnp.asarray(1.0, BF16)
    head_q = [jnp.where(lane < half, queries, picks), jnp.where(lane < half, picks, queries)]
    head_k = [
        jnp.where(key_lane < half, key_rows, extra),
        jnp.where(key_lane < half, extra, key_rows),
    ]
    head_v = [
        jnp.where(key_lane < half, value_rows, one),
        jnp.where(key_lane < half, one, value_rows),
    ]

    def scores(at, head):
        low, high = at * chunk, (at + 1) * chunk
        live = high if causal else keys
        found = dot(head_q[head][low:high], head_k[head][:live], 1, 1)
        if not causal:
            return found
        query_at = lax.broadcasted_iota(jnp.int32, (chunk, chunk), 0)
        key_at = lax.broadcasted_iota(jnp.int32, (chunk, chunk), 1)
        edge = jnp.where(key_at <= query_at, found[:, low:high], -1e30)
        return jnp.concatenate([found[:, :low], edge], 1) if low else edge

    def mix(head, found):
        top = jnp.max(found, 1, keepdims=True)
        expo = jnp.exp(found - top).astype(BF16)
        mixed = dot(expo, head_v[head][: found.shape[1]], 1, 0)
        return mixed / pltpu.roll(mixed, half, 1), top + jnp.log(mixed)

    units = [(at, head) for at in range(rows // chunk) for head in range(2)]
    done, waiting = {}, []
    for unit in units:
        waiting.append((unit, scores(*unit)))
        if len(waiting) > ahead:
            first, found = waiting.pop(0)
            done[first] = mix(first[1], found)
    for first, found in waiting:
        done[first] = mix(first[1], found)
    left = lane[:chunk] < half
    place = lane[:chunk] % half
    for at in range(rows // chunk):
        low, high = at * chunk, (at + 1) * chunk
        out_ref[low:high, :] = jnp.where(left, done[at, 0][0], done[at, 1][0]).astype(BF16)
        parts = split_three(-jnp.where(left, done[at, 1][1], done[at, 0][1]))
        packed = jnp.where(place == 0, 1.0, 0.0)
        for index, part in enumerate(parts):
            packed = jnp.where(place == index + 1, part, packed)
        lse_ref[low:high, :] = packed.astype(BF16)


def attend_backward_kernel(
    causal, chunk, q_ref, k_ref, v_ref, out_ref, grad_ref, lse_ref, extra_ref,
    dq_ref, dk_ref, dv_ref, p_scr, s_scr,
):
    rows, width = q_ref.shape
    keys, half = k_ref.shape[0], width // 2
    scale = half**-0.5
    count = rows // chunk
    lane = lax.broadcasted_iota(jnp.int32, (rows, width), 1)
    key_lane = lax.broadcasted_iota(jnp.int32, (keys, width), 1)
    queries = q_ref[...] * jnp.asarray(scale, BF16)
    lse, extra = lse_ref[...], extra_ref[...]
    key_rows, value_rows, grads = k_ref[...], v_ref[...], grad_ref[...]
    place = key_lane % half
    ones = jnp.where((place >= 1) & (place <= 3), 1.0, 0.0).astype(BF16)
    products = grads.astype(F32) * out_ref[...].astype(F32)
    queries_t, grads_t = queries.T, grads.T
    grad_q = [[None] * count, [None] * count]
    grad_k_t, grad_v_t = [], []
    for head in range(2):
        mine = (lane < half) if head == 0 else (lane >= half)
        key_mine = (key_lane < half) if head == 0 else (key_lane >= half)
        base = half if head == 0 else 0
        head_q = jnp.where(mine, queries, lse)
        head_k = jnp.where(key_mine, key_rows, extra)
        head_v = jnp.where(key_mine, value_rows, ones)
        head_g = grads.astype(F32)
        dots = split_three(-jnp.sum(jnp.where(mine, products, 0.0), 1, keepdims=True))
        head_g = jnp.where(mine, head_g, 0.0)
        for index, part in enumerate(dots):
            head_g = jnp.where(lane == base + index + 1, part, head_g)
        head_g = head_g.astype(BF16)
        span = slice(head * half, (head + 1) * half)
        for at in range(count):
            low, high = at * chunk, (at + 1) * chunk
            live = high if causal else keys
            probs = jnp.exp(dot(head_q[low:high], head_k[:live], 1, 1))
            if causal:
                query_at = lax.broadcasted_iota(jnp.int32, (chunk, chunk), 0)
                key_at = lax.broadcasted_iota(jnp.int32, (chunk, chunk), 1)
                edge = jnp.where(key_at <= query_at, probs[:, low:high], 0.0)
                probs = jnp.concatenate([probs[:, :low], edge], 1) if low else edge
            grad_s = (probs * dot(head_g[low:high], head_v[:live], 1, 1)).astype(BF16)
            p_scr[head, low:high, :live] = probs.astype(BF16)
            s_scr[head, low:high, :live] = grad_s
            grad_q[head][at] = dot(grad_s, key_rows[:live], 1, 0)
        if causal:
            for total, source, saved in (
                (grad_v_t, grads_t, p_scr),
                (grad_k_t, queries_t, s_scr),
            ):
                total.append(
                    jnp.concatenate(
                        [
                            dot(
                                source[span, at * chunk :],
                                saved[head, at * chunk :, at * chunk : (at + 1) * chunk],
                                1,
                                0,
                            )
                            for at in range(count)
                        ],
                        1,
                    )
                )
        else:
            grad_v_t.append(dot(grads_t[span], p_scr[head], 1, 0))
            grad_k_t.append(dot(queries_t[span], s_scr[head], 1, 0))
    for at in range(count):
        low, high = at * chunk, (at + 1) * chunk
        both = jnp.where(lane[low:high] < half, grad_q[0][at], grad_q[1][at])
        dq_ref[low:high, :] = (both * scale).astype(BF16)
    dk_ref[...] = jnp.concatenate(grad_k_t, 0).T.astype(BF16)
    dv_ref[...] = jnp.concatenate(grad_v_t, 0).T.astype(BF16)


def attend_forward(queries, q_at, key_rows, k_at, value_rows, v_at, extra, width, causal):
    rows, keys = queries.shape[0], key_rows.shape[0]

    def pair(count, first):
        return pl.BlockSpec((count, 128), lambda i: (0, i + first))

    return call(
        functools.partial(attend_forward_kernel, causal, 256, 2),
        "self_forward" if causal else "cross_forward",
        (width // 128,),
        [pair(rows, q_at), pair(keys, k_at), pair(keys, v_at), whole((keys, 128))],
        [pair(rows, 0), pair(rows, 0)],
        [jax.ShapeDtypeStruct((rows, width), BF16)] * 2,
        4 * rows * keys * width,
        12 * rows * width,
        rows * keys * HEADS,
    )(queries, key_rows, value_rows, extra)


def attend_backward(
    queries, q_at, key_rows, k_at, value_rows, v_at, mixed, grads, lse, extra, width, causal
):
    rows, keys = queries.shape[0], key_rows.shape[0]

    def pair(count, first):
        return pl.BlockSpec((count, 128), lambda i: (0, i + first))

    return call(
        functools.partial(attend_backward_kernel, causal, 256),
        "self_backward" if causal else "cross_backward",
        (width // 128,),
        [pair(rows, q_at), pair(keys, k_at), pair(keys, v_at)]
        + [pair(rows, 0)] * 3
        + [whole((keys, 128))],
        [pair(rows, 0), pair(keys, 0), pair(keys, 0)],
        [
            jax.ShapeDtypeStruct((rows, width), BF16),
            jax.ShapeDtypeStruct((keys, width), BF16),
            jax.ShapeDtypeStruct((keys, width), BF16),
        ],
        10 * rows * keys * width,
        18 * rows * width,
        rows * keys * HEADS,
        [pltpu.VMEM((2, rows, keys), BF16)] * 2,
    )(queries, key_rows, value_rows, mixed, grads, lse, extra)


def project_kernel(x_ref, w_ref, bias_ref, out_ref):
    out_ref[...] = (dot(x_ref[...], w_ref[...], 1, 0) + bias_ref[...]).astype(BF16)


def project(values, weight, first, columns, bias, name):
    rows, depth = values.shape
    step = 512
    return call(
        project_kernel,
        name,
        (columns // step,),
        [
            whole((rows, depth)),
            pl.BlockSpec((depth, step), lambda i: (0, i + first // step)),
            pl.BlockSpec((1, step), lambda i: (0, i)),
        ],
        pl.BlockSpec((rows, step), lambda i: (0, i)),
        jax.ShapeDtypeStruct((rows, columns), BF16),
        2 * rows * depth * columns,
        2 * (rows * depth + depth * columns + rows * columns),
    )(values, weight, bias)


def post_self_kernel(
    x_ref, ctx_ref, wo_ref, wq_ref, bo_ref, gain_ref, shift_ref, bq_ref, normal_ref, scale_ref, q_ref
):
    part = 256
    spans = [slice(at, at + part) for at in range(0, x_ref.shape[0], part)]
    sums = [
        x_ref[span].astype(F32) + dot(ctx_ref[span], wo_ref[...], 1, 0) + bo_ref[...]
        for span in spans
    ]
    for span, total in zip(spans, sums):
        normal, scale = normalize(total)
        normal_ref[span] = normal
        scale_ref[span] = jnp.broadcast_to(scale, (part, 128))
        hidden = (normal * gain_ref[...] + shift_ref[...]).astype(BF16)
        q_ref[span] = (dot(hidden, wq_ref[...], 1, 0) + bq_ref[...]).astype(BF16)


def post_self(values, context, weights, wo_at, wq_at, out_bias, gain, shift, q_bias):
    rows, width = values.shape
    step = 512
    vector = whole((1, width))
    return call(
        post_self_kernel,
        "post_self",
        (rows // step,),
        [
            rows_block(step, width),
            rows_block(step, width),
            pl.BlockSpec((width, width), lambda i: (0, wo_at)),
            pl.BlockSpec((width, width), lambda i: (0, wq_at)),
        ]
        + [vector] * 4,
        [rows_block(step, width), rows_block(step, 128), rows_block(step, width)],
        [
            jax.ShapeDtypeStruct((rows, width), F32),
            jax.ShapeDtypeStruct((rows, 128), F32),
            jax.ShapeDtypeStruct((rows, width), BF16),
        ],
        4 * rows * width * width,
        rows * width * 10 + 4 * width * width,
    )(values, context, weights, weights, out_bias, gain, shift, q_bias)


def post_cross_kernel(
    n1_ref, ctx_ref, wo_ref, bo_ref, gain_ref, shift_ref, gain2_ref, shift2_ref,
    normal_ref, scale_ref, hidden_ref,
):
    part = 256
    spans = [slice(at, at + part) for at in range(0, n1_ref.shape[0], part)]
    sums = [
        n1_ref[span] * gain_ref[...]
        + shift_ref[...]
        + dot(ctx_ref[span], wo_ref[...], 1, 0)
        + bo_ref[...]
        for span in spans
    ]
    for span, total in zip(spans, sums):
        normal, scale = normalize(total)
        normal_ref[span] = normal
        scale_ref[span] = jnp.broadcast_to(scale, (part, 128))
        hidden_ref[span] = (normal * gain2_ref[...] + shift2_ref[...]).astype(BF16)


def post_cross(normal, context, weights, wo_at, out_bias, gain, shift, gain2, shift2):
    rows, width = normal.shape
    step = 512
    vector = whole((1, width))
    return call(
        post_cross_kernel,
        "post_cross",
        (rows // step,),
        [
            rows_block(step, width),
            rows_block(step, width),
            pl.BlockSpec((width, width), lambda i: (0, wo_at)),
        ]
        + [vector] * 5,
        [rows_block(step, width), rows_block(step, 128), rows_block(step, width)],
        [
            jax.ShapeDtypeStruct((rows, width), F32),
            jax.ShapeDtypeStruct((rows, 128), F32),
            jax.ShapeDtypeStruct((rows, width), BF16),
        ],
        2 * rows * width * width,
        rows * width * 12 + 2 * width * width,
    )(normal, context, weights, out_bias, gain, shift, gain2, shift2)


def second_block(w_ref, held, width):
    pieces = []
    for at in range(0, w_ref.shape[0], held):
        for group in range(w_ref.shape[1] // width):
            pieces.append(w_ref[at : at + held, group * width : (group + 1) * width])
    return jnp.concatenate(pieces, 0)


def ffn_forward_kernel(held, h_ref, w1_ref, w2_ref, b1_ref, b2_ref, out_ref, slope_ref):
    rows, width = h_ref.shape
    part = 256
    second = second_block(w2_ref, held, width)

    @pl.when(pl.program_id(0) == 0)
    def _():
        out_ref[...] = jnp.broadcast_to(b2_ref[...], out_ref.shape)

    def first(at):
        return dot(h_ref[at : at + part], w1_ref[...], 1, 0) + b1_ref[...]

    def finish(at, pre):
        phi = 0.5 + 0.5 * lax.erf(pre * (0.5**0.5))
        act = (pre * phi).astype(BF16)
        slope = phi + pre * (jnp.exp(pre * pre * -0.5) * (1.0 / math.sqrt(2.0 * math.pi)))
        slope_ref[at : at + part] = slope.astype(BF16)
        out_ref[at : at + part] += dot(act, second, 1, 0)

    waiting = None
    for at in range(0, rows, part):
        pre = first(at)
        if waiting is not None:
            finish(*waiting)
        waiting = (at, pre)
    finish(*waiting)


def ffn_forward(hidden, weights, w2_at, w1_at, first_bias, second_bias, held):
    rows, width = hidden.shape
    wide = first_bias.shape[1]
    step = 512
    groups = wide // width
    return call(
        functools.partial(ffn_forward_kernel, held),
        "ffn_forward",
        (wide // step,),
        [
            whole((rows, width)),
            pl.BlockSpec((width, step), lambda i: (0, i + w1_at // step)),
            pl.BlockSpec((step // groups, wide), lambda i: (i, w2_at // wide)),
            pl.BlockSpec((1, step), lambda i: (0, i)),
            whole((1, width)),
        ],
        [whole((rows, width)), pl.BlockSpec((rows, step), lambda i: (0, i))],
        [jax.ShapeDtypeStruct((rows, width), F32), jax.ShapeDtypeStruct((rows, wide), BF16)],
        4 * rows * width * wide,
        6 * rows * width + 4 * width * wide + 2 * rows * wide,
        2 * rows * wide,
    )(hidden, weights, weights, first_bias, second_bias)


def ffn_backward_kernel(held, g_ref, w1_ref, w2_ref, slope_ref, start_ref, out_ref):
    rows, width = g_ref.shape
    part = 256
    second = second_block(w2_ref, held, width)

    @pl.when(pl.program_id(0) == 0)
    def _():
        out_ref[...] = start_ref[...]

    def finish(at, grad_act):
        grad_pre = (slope_ref[at : at + part].astype(F32) * grad_act).astype(BF16)
        out_ref[at : at + part] += dot(grad_pre, w1_ref[...], 1, 1)

    waiting = None
    for at in range(0, rows, part):
        grad_act = dot(g_ref[at : at + part], second, 1, 1)
        if waiting is not None:
            finish(*waiting)
        waiting = (at, grad_act)
    finish(*waiting)


def ffn_backward(grads, weights, w2_at, w1_at, slope, start, held):
    rows, width = grads.shape
    wide = slope.shape[1]
    step = 512
    groups = wide // width
    return call(
        functools.partial(ffn_backward_kernel, held),
        "ffn_backward",
        (wide // step,),
        [
            whole((rows, width)),
            pl.BlockSpec((width, step), lambda i: (0, i + w1_at // step)),
            pl.BlockSpec((step // groups, wide), lambda i: (i, w2_at // wide)),
            pl.BlockSpec((rows, step), lambda i: (0, i)),
            whole((rows, width)),
        ],
        whole((rows, width)),
        jax.ShapeDtypeStruct((rows, width), F32),
        4 * rows * width * wide,
        10 * rows * width + 4 * width * wide + 2 * rows * wide,
    )(grads, weights, weights, slope, start)


def adapter_kernel(
    ramp_ref, n2_ref, ffn_ref, go_ref, down_ref, up_ref, gain2_ref, shift2_ref, gain3_ref, shift3_ref,
    gain_a_ref, shift_a_ref, down_b_ref, up_b_ref,
    out_ref, gffn_ref, rest_ref, grad_down_ref, grad_up_ref, small_ref,
):
    ramp = ramp_ref[0]

    @pl.when(pl.program_id(0) == 0)
    def _():
        grad_down_ref[...] = jnp.zeros_like(grad_down_ref)
        grad_up_ref[...] = jnp.zeros_like(grad_up_ref)
        small_ref[...] = jnp.zeros_like(small_ref)

    hidden = n2_ref[...] * gain2_ref[...] + shift2_ref[...]
    normal_a, scale_a = normalize(hidden)
    adapt_in = (normal_a * gain_a_ref[...] + shift_a_ref[...]).astype(BF16)
    lower = dot(adapt_in, down_ref[...], 1, 0) + down_b_ref[...]
    gate = 1.0 / (1.0 + jnp.exp(-lower))
    adapt_act = (lower * gate).astype(BF16)
    branch = dot(adapt_act, up_ref[...], 1, 0) + up_b_ref[...]
    normal, scale = normalize(hidden + ffn_ref[...] + ramp * branch)
    out_ref[...] = (normal * gain3_ref[...] + shift3_ref[...]).astype(BF16)
    grad_sum = normalize_back(normal, scale, gain3_ref[...] * go_ref[...].astype(F32))
    gffn_ref[...] = grad_sum.astype(BF16)
    grad_branch = (ramp * grad_sum).astype(BF16)
    grad_up_ref[...] += dot(adapt_act, grad_branch, 0, 0)
    grad_act = dot(grad_branch, up_ref[...], 1, 1).astype(BF16).astype(F32)
    grad_lower = (gate * (1.0 + lower * (1.0 - gate)) * grad_act).astype(BF16)
    grad_down_ref[...] += dot(adapt_in, grad_lower, 0, 0)
    grad_adapt = dot(grad_lower, down_ref[...], 1, 1)
    rest_ref[...] = grad_sum + normalize_back(normal_a, scale_a, gain_a_ref[...] * grad_adapt)
    hidden_units = lower.shape[1]
    small_ref[0:1, 0:hidden_units] += jnp.sum(grad_lower.astype(F32), 0, keepdims=True)
    small_ref[1:2] += jnp.sum(grad_branch.astype(F32), 0, keepdims=True)
    small_ref[2:3] += jnp.sum(grad_adapt * normal_a, 0, keepdims=True)
    small_ref[3:4] += jnp.sum(grad_adapt, 0, keepdims=True)


def adapter(ramp, normal2, ffn, grad_out, down, up, vectors, down_bias):
    rows, width = normal2.shape
    units = down.shape[1]
    step = 256
    vector = whole((1, width))
    gain2, shift2, gain3, shift3, gain_a, shift_a, up_bias = vectors
    return call(
        adapter_kernel,
        "adapter",
        (rows // step,),
        [pl.BlockSpec(memory_space=pltpu.SMEM)]
        + [rows_block(step, width)] * 3
        + [whole(down.shape), whole(up.shape)]
        + [vector] * 6
        + [whole((1, units)), vector],
        [rows_block(step, width)] * 3 + [whole(down.shape), whole(up.shape), whole((8, width))],
        [
            jax.ShapeDtypeStruct((rows, width), BF16),
            jax.ShapeDtypeStruct((rows, width), BF16),
            jax.ShapeDtypeStruct((rows, width), F32),
            jax.ShapeDtypeStruct(down.shape, F32),
            jax.ShapeDtypeStruct(up.shape, F32),
            jax.ShapeDtypeStruct((8, width), F32),
        ],
        12 * rows * width * units,
        18 * rows * width + 12 * width * units,
        rows * units,
    )(
        ramp, normal2, ffn, grad_out, down, up, gain2, shift2, gain3, shift3, gain_a, shift_a,
        down_bias, up_bias,
    )


def norm_back_kernel(g_ref, normal_ref, scale_ref, gain_ref, wo_ref, sum_ref, ctx_ref):
    part = 256
    for at in range(0, g_ref.shape[0], part):
        span = slice(at, at + part)
        grad = normalize_back(normal_ref[span], scale_ref[span, 0:1], gain_ref[...] * g_ref[span])
        sum_ref[span] = grad
        ctx_ref[span] = dot(grad.astype(BF16), wo_ref[...], 1, 1).astype(BF16)


def norm_back_query_kernel(
    g_ref, dq_ref, wq_ref, normal_ref, scale_ref, gain_ref, wo_ref, sum_ref, ctx_ref
):
    part = 256
    spans = [slice(at, at + part) for at in range(0, g_ref.shape[0], part)]
    totals = [g_ref[span] + dot(dq_ref[span], wq_ref[...], 1, 1) for span in spans]
    for span, total in zip(spans, totals):
        grad = normalize_back(normal_ref[span], scale_ref[span, 0:1], gain_ref[...] * total)
        sum_ref[span] = grad
        ctx_ref[span] = dot(grad.astype(BF16), wo_ref[...], 1, 1).astype(BF16)


def norm_back(grads, normal, scale, gain, weights, wo_at, query_grads=None, wq_at=None):
    rows, width = grads.shape
    step = 512
    block = rows_block(step, width)
    with_query = query_grads is not None
    extra_specs = [block, pl.BlockSpec((width, width), lambda i: (0, wq_at))] if with_query else []
    extra = [query_grads, weights] if with_query else []
    return call(
        norm_back_query_kernel if with_query else norm_back_kernel,
        "norm_one_back" if with_query else "norm_two_back",
        (rows // step,),
        [block]
        + extra_specs
        + [
            block,
            rows_block(step, 128),
            whole((1, width)),
            pl.BlockSpec((width, width), lambda i: (0, wo_at)),
        ],
        [block, block],
        [jax.ShapeDtypeStruct((rows, width), F32), jax.ShapeDtypeStruct((rows, width), BF16)],
        (4 if with_query else 2) * rows * width * width,
        16 * rows * width + 4 * width * width,
    )(grads, *extra, normal, scale, gain, weights)


def back_project_kernel(count, with_start, *refs):
    grads, rest = refs[:count], refs[count:]
    weights, rest = rest[:count], rest[count:]
    total = sum(dot(g[...], w[...], 1, 1) for g, w in zip(grads, weights))
    if with_start:
        total = total + rest[0][...]
    rest[-1][...] = total


def back_project(grads, weights, first, start, name):
    rows, width = grads[0].shape
    step = 256
    count = len(grads)
    column = pl.BlockSpec((rows, step), lambda i: (0, i))

    def row_of(at):
        return pl.BlockSpec((step, width), lambda i: (i, at))

    return call(
        functools.partial(back_project_kernel, count, start is not None),
        name,
        (width // step,),
        [whole((rows, width))] * count
        + [row_of(first + at) for at in range(count)]
        + ([column] if start is not None else []),
        column,
        jax.ShapeDtypeStruct((rows, width), F32),
        2 * rows * width * width * count,
        rows * width * (2 * count + 8) + 2 * count * width * width,
    )(*grads, *([weights] * count), *([start] if start is not None else []))


def local(
    inputs,
    encoder,
    grad_out,
    target_mask,
    source_lengths,
    step,
    attn_in,
    attn_out,
    ffn_in,
    ffn_in_bias,
    ffn_out,
    ffn_out_bias,
    attn_bias,
    norm_gain,
    norm_shift,
    adapter_down,
    adapter_down_bias,
    adapter_up,
    adapter_up_bias,
    adapter_gain,
    adapter_shift,
):
    sequences, row_count, width = inputs.shape
    source_count = encoder.shape[1]
    held = attn_in.shape[0]
    groups = ffn_out.shape[0] // held
    wide = ffn_in.shape[1]
    self_w = lax.all_gather(attn_in[:, 0 : 3 * width], "fsdp", axis=0, tiled=True)
    rest_w = jnp.concatenate(
        [ffn_out[at * held : (at + 1) * held] for at in range(groups)]
        + [ffn_in, attn_in[:, 3 * width :], attn_out],
        1,
    )
    rest_w = lax.all_gather(rest_w, "fsdp", axis=0, tiled=True)
    w1_at, w2_at = wide, 0
    cq_at = 2 * wide // width
    ck_at, so_at, co_at = cq_at + 1, cq_at + 3, cq_at + 4

    ramp = (4.0 * step.astype(F32) / RAMP).reshape(1)
    bias = [attn_bias[at : at + 1] for at in range(6)]
    gain = [norm_gain[at : at + 1] for at in range(3)]
    shift = [norm_shift[at : at + 1] for at in range(3)]
    none = jnp.zeros((1, width), F32)
    tokens, states = inputs.reshape(-1, width), encoder.reshape(-1, width)
    self_extra = key_extra(target_mask.reshape(-1) > 0)
    cross_extra = key_extra(jnp.arange(source_count, dtype=jnp.int32) < source_lengths[0])
    per = width // 128

    qkv = project(
        tokens, self_w, 0, 3 * width, jnp.concatenate([bias[0], none, bias[1]], 1), "self_project"
    )
    self_ctx, self_lse = attend_forward(
        qkv, 0, qkv, per, qkv, 2 * per, self_extra, width, True
    )
    normal1, scale1, cross_q = post_self(
        tokens, self_ctx, rest_w, so_at, cq_at, bias[2], gain[0], shift[0], bias[3]
    )
    cross_kv = project(
        states, rest_w, ck_at * width, 2 * width, jnp.concatenate([none, bias[4]], 1), "cross_project"
    )
    cross_ctx, cross_lse = attend_forward(
        cross_q, 0, cross_kv, 0, cross_kv, per, cross_extra, width, False
    )
    normal2, scale2, hidden2 = post_cross(
        normal1, cross_ctx, rest_w, co_at, bias[5], gain[0], shift[0], gain[1], shift[1]
    )
    ffn, slope = ffn_forward(
        hidden2, rest_w, w2_at, w1_at, ffn_in_bias[None], ffn_out_bias[None], held
    )
    layer_out, grad_ffn, grad_rest, grad_down, grad_up, small = adapter(
        ramp,
        normal2,
        ffn,
        grad_out.reshape(-1, width),
        adapter_down,
        adapter_up,
        (
            gain[1], shift[1], gain[2], shift[2], adapter_gain[None], adapter_shift[None],
            adapter_up_bias[None],
        ),
        adapter_down_bias[None],
    )
    grad_down, grad_up, small = lax.psum((grad_down, grad_up, small), ("fsdp", "dp"))
    grad_hidden2 = ffn_backward(grad_ffn, rest_w, w2_at, w1_at, slope, grad_rest, held)
    grad_sum2, grad_cross = norm_back(grad_hidden2, normal2, scale2, gain[1], rest_w, co_at)
    cross_dq, cross_dk, cross_dv = attend_backward(
        cross_q, 0, cross_kv, 0, cross_kv, per, cross_ctx, grad_cross, cross_lse, cross_extra,
        width, False,
    )
    grad_encoder = back_project((cross_dk, cross_dv), rest_w, ck_at, None, "encoder_back")
    grad_sum1, grad_self = norm_back(
        grad_sum2, normal1, scale1, gain[0], rest_w, so_at, cross_dq, cq_at
    )
    self_grads = attend_backward(
        qkv, 0, qkv, per, qkv, 2 * per, self_ctx, grad_self, self_lse, self_extra, width, True
    )
    grad_input = back_project(self_grads, self_w, 0, grad_sum1, "input_back")

    token_total = sequences * row_count * lax.axis_size("fsdp") * lax.axis_size("dp")
    factor = 1.0 / math.sqrt(token_total)
    units = adapter_down.shape[1]
    return (
        layer_out.reshape(inputs.shape),
        grad_input.reshape(inputs.shape),
        grad_encoder.reshape(encoder.shape),
        grad_down * factor,
        small[0, :units] * factor,
        grad_up * factor,
        small[1] * factor,
        small[2] * factor,
        small[3] * factor,
    )


def solution(mesh):
    batch = P(("fsdp", "dp"), None, None)
    split = P("fsdp", None)
    placed = (
        (batch,) * 3
        + (P(("fsdp", "dp"), None), P(("fsdp", "dp")), P())
        + (split, split, split, P(), split)
        + (P(),) * 10
    )
    return jax.shard_map(
        local,
        mesh=mesh,
        in_specs=placed,
        out_specs=(batch,) * 3 + (P(),) * 6,
        check_vma=False,
    )
```

time: 1170 us -> 594 us (0.51)
  matrix products: 605 us -> 0 us
  Pallas kernels: 0 us -> 267 us
  other arithmetic: 204 us -> 7.81 us
  local copies, waits for them, and re-layouts: 120 us -> 8.7 us
  waiting for transfers between devices: 159 us -> 246 us
  loops' own time: 20 us -> 0 us
    dot_general x48 -> x0, matrix products: 605 us -> none  [the longest x8 146 us: block_scores(): jnp.einsum('sbhe,skhe->shbk', query_block, key_heads, preferred_element_t...]
    pallas_call x0 -> x15, Pallas kernels: none -> 267 us  [the longest x2 74.1 us: attend_backward(): call(functools.partial(attend_backward_kernel, causal, 256), 'self_backwa...]
    another operation x9 -> x0, other arithmetic: 98.8 us -> none
    reduce_sum x15 -> x0, other arithmetic: 80.3 us -> none  [the longest x4 60.2 us: one_block(): row_total = jnp.sum(expo, -1, keepdims=True)]
    all_gather x4 -> x2, waiting for transfers between devices: 91.6 us -> 167 us  [the longest x1 109 us: local(): rest_w = lax.all_gather(rest_w, 'fsdp', axis=0, tiled=True)]
    unnamed x181 -> x22, local copies, waits for them, and re-layouts: 50.4 us -> 6.84 us
    another operation x11 -> x0, local copies, waits for them, and re-layouts: 29.5 us -> none  [the longest x2 12.7 us: attend_forward(): split_heads(queries)]
    another operation x4 -> x0, loops' own time: 20 us -> none  [the longest x2 10.2 us: attend_backward(): lax.scan(one_block, (empty, empty), (jnp.arange(block_count), log_totals))]
  transfers between devices with their start and end apart: 5 -> 3, of which waited for: 2 -> 3; matrix products, arithmetic and copies ran while one was open for 33% -> 1% of each run, Pallas kernels for 0% -> 16%
where the time goes in v1:
time: 594 us; the launch traced here: 585 us
  Pallas kernels  267 us (45%)
  waiting for transfers between devices  246 us (41%)
  blocking collectives  40.4 us (7%)
  between operations  15.4 us (3%)
  local copies, waits for them, and re-layouts  8.7 us (1%)
  other arithmetic  7.81 us (1%)
    all_gather x1, waiting for transfers between devices, local(): rest_w = lax.all_gather(rest_w, 'fsdp', axis=0, tiled=True)  109 us
    psum x1, waiting for transfers between devices, local(): lax.psum((grad_down, grad_up, small), ('fsdp', 'dp'))  78.5 us
    pallas_call x2, Pallas kernels, attend_backward(): call(functools.partial(attend_backward_kernel, causal, 256), 'self_backwa...  74.1 us
    all_gather x1, waiting for transfers between devices, local(): self_w = lax.all_gather(attn_in[:, 0:3 * width], 'fsdp', axis=0, tiled=True)  58.4 us
    pallas_call x2, Pallas kernels, attend_forward(): call(functools.partial(attend_forward_kernel, causal, 256, 2), 'self_forw...  43.9 us
    psum x1, blocking collectives, local(): lax.psum((grad_down, grad_up, small), ('fsdp', 'dp'))  40.4 us
    pallas_call x1, Pallas kernels, ffn_forward(): call(functools.partial(ffn_forward_kernel, held), 'ffn_forward', (wide //...  27 us
    pallas_call x1, Pallas kernels, ffn_backward(): call(functools.partial(ffn_backward_kernel, held), 'ffn_backward', (wide...  26.2 us
  transfers between devices with their start and end apart: 3, of which 3 were waited for; matrix products, arithmetic and copies ran while one was open for 1% of the time, Pallas kernels for 16%

profile of v1, /device:TPU:0, one launch (start us, length us, event | category | flops | bytes accessed | tf_op | source)
XLA Modules:
  0.0 585.0 jit_solution(857377796136634376)
XLA Ops:
  7.2 0.0 copy-start.2
  7.2 0.0 copy-start.3
  7.2 0.0 all-gather.3.cloned.1.call-start
  7.2 1.0 slice_dynamic-update-slice_fusion.4
  8.2 0.9 slice_dynamic-update-slice_fusion.3
  9.2 0.9 slice_dynamic-update-slice_fusion.2
  10.1 0.9 slice_dynamic-update-slice_fusion.1
  11.0 1.1 constant_dynamic-update-slice_fusion.1
  12.1 0.0 copy-done.2
  12.1 0.0 copy-start.4
  12.1 0.0 copy-start.7
  12.1 0.0 copy-start.5
  12.1 0.0 copy-start.6
  12.1 0.8 slice_dynamic-update-slice_fusion
  12.9 0.0 all-gather.3.cloned.1.call-update
  13.0 0.0 all-gather.5.cloned.1.call-start
  13.0 0.0 copy-done.3
  13.0 0.0 copy-start.1
  13.1 1.2 copy-done.1
  14.2 0.0 all-gather.5.cloned.1.call-update
  14.3 0.0 all-reduce.4.cloned.1.call-start
  15.6 0.0 copy-done.4
  15.6 0.6 fusion.1
  16.2 0.6 concatenate.11.bias_ref
  16.9 0.0 copy-done.7
  16.9 0.0 copy-done.5
  16.9 0.0 copy-done.6
  16.9 0.6 fusion.2
  17.5 1.1 select_convert_fusion
  18.7 0.6 pad_maximum_fusion.bias_ref
  19.3 58.4 %all-gather.3.cloned.1.call-done.w_ref.refs_3_.refs_4_.refs_5_ = bf16[1024,3072]{1,0:T(8,128)(2,1)} async-done(((bf16[64,3072]{1,0:T(8,128)(2,1)}), bf16[1024,3072]{1,0:T(8,128)(2,1)}) %all-gather.3.cloned.1.call-update) | async-done | bytes 6291472 | tf_op jit(solution)/shard_map/all_gather | solution.py:650
  77.7 11.5 %self_project.1.q_ref.k_ref.v_ref = bf16[1024,3072]{1,0:T(8,128)(2,1)} custom-call(bf16[1024,1024]{1,0:T(8,128)(2,1)} %bitcast.22, bf16[1024,3072]{1,0:T(8,128)(2,1)} %all-gather.3.cloned.1.call-done.w_ref.refs_3_.refs_4_.refs_5_, f32[1,3072]{1,0:T(1,128)} %pad_maximum_fusion.bias_ref), custom_call_target="tpu_custom_call" | custom-call | flops 6442450944 | bytes 14680064 | tf_op jit(solution)/shard_map/self_project/pallas_call | solution.py:263
  89.2 19.1 %self_forward.1 = (bf16[1024,1024]{1,0:T(8,128)(2,1)}, bf16[1024,1024]{1,0:T(8,128)(2,1)}) custom-call(bf16[1024,3072]{1,0:T(8,128)(2,1)} %self_project.1.q_ref.k_ref.v_ref, bf16[1024,3072]{1,0:T(8,128)(2,1)} %self_project.1.q_ref.k_ref.v_ref, bf16[1024,3072]{1,0:T(8,128)(2,1)} %self_project.1.q_ref.k_ref.v_ref, bf16[1024,128]{1,0:T(8,128)(2,1)} %get-tuple-element.85.extra_ref), custom_call_target="tpu_custom_call" | custom-call | flops 4294967296 | bytes 12582912 | tf_op jit(solution)/shard_map/self_forward/pallas_call | solution.py:215
  108.3 108.7 %all-gather.5.cloned.1.call-done.wo_ref.wq_ref.w_ref.w1_ref.w2_ref.refs_2_.refs_3_ = bf16[1024,13312]{1,0:T(8,128)(2,1)} async-done(((bf16[64,13312]{1,0:T(8,128)(2,1)}), bf16[1024,13312]{1,0:T(8,128)(2,1)}) %all-gather.5.cloned.1.call-update) | async-done | bytes 27262992 | tf_op jit(solution)/shard_map/all_gather | solution.py:656
  216.9 8.4 %cross_project.1.k_ref.v_ref = bf16[1024,2048]{1,0:T(8,128)(2,1)} custom-call(bf16[1024,1024]{1,0:T(8,128)(2,1)} %bitcast.21, bf16[1024,13312]{1,0:T(8,128)(2,1)} %all-gather.5.cloned.1.call-done.wo_ref.wq_ref.w_ref.w1_ref.w2_ref.refs_2_.refs_3_, f32[1,2048]{1,0:T(1,128)} %concatenate.11.bias_ref), custom_call_target="tpu_custom_call" | custom-call | flops 4294967296 | bytes 10485760 | tf_op jit(solution)/shard_map/cross_project/pallas_call | solution.py:263
  225.3 9.0 %post_self.1 = (f32[1024,1024]{1,0:T(8,128)}, f32[1024,128]{1,0:T(8,128)}, bf16[1024,1024]{1,0:T(8,128)(2,1)}) custom-call(bf16[1024,1024]{1,0:T(8,128)(2,1)} %bitcast.23, bf16[1024,1024]{1,0:T(8,128)(2,1)} %get-tuple-element.37.ctx_ref.out_ref, bf16[1024,13312]{1,0:T(8,128)(2,1)} %all-gather.5.cloned.1.call-done.wo_ref.wq_ref.w_ref.w1_ref.w2_ref.refs_2_.refs_3_, ...), custom_call_target="tpu_custom_call" | custom-call | flops 4294967296 | bytes 14680064 | tf_op jit(solution)/shard_map/post_self/pallas_call | solution.py:300
  234.3 24.8 %cross_forward.1 = (bf16[1024,1024]{1,0:T(8,128)(2,1)}, bf16[1024,1024]{1,0:T(8,128)(2,1)}) custom-call(bf16[1024,1024]{1,0:T(8,128)(2,1)} %get-tuple-element.39.q_ref, bf16[1024,2048]{1,0:T(8,128)(2,1)} %cross_project.1.k_ref.v_ref, bf16[1024,2048]{1,0:T(8,128)(2,1)} %cross_project.1.k_ref.v_ref, bf16[1024,128]{1,0:T(8,128)(2,1)} %get-tuple-element.84.extra_ref), custom_call_target="tpu_custom_call" | custom-call | flops 4294967296 | bytes 12582912 | tf_op jit(solution)/shard_map/cross_forward/pallas_call | solution.py:215
  259.1 7.8 %post_cross.1 = (f32[1024,1024]{1,0:T(8,128)}, f32[1024,128]{1,0:T(8,128)}, bf16[1024,1024]{1,0:T(8,128)(2,1)}) custom-call(f32[1024,1024]{1,0:T(8,128)} %get-tuple-element.38.n1_ref.normal_ref, bf16[1024,1024]{1,0:T(8,128)(2,1)} %get-tuple-element.40.ctx_ref.out_ref, ...), custom_call_target="tpu_custom_call" | custom-call | flops 2147483648 | bytes 14680064 | tf_op jit(solution)/shard_map/post_cross/pallas_call | solution.py:346
  266.9 27.0 %ffn_forward.1 = (f32[1024,1024]{1,0:T(8,128)}, bf16[1024,4096]{1,0:T(8,128)(2,1)}) custom-call(bf16[1024,1024]{1,0:T(8,128)(2,1)} %get-tuple-element.42.h_ref, bf16[1024,13312]{1,0:T(8,128)(2,1)} %all-gather.5.cloned.1.call-done.wo_ref.wq_ref.w_ref.w1_ref.w2_ref.refs_2_.refs_3_, ...), custom_call_target="tpu_custom_call" | custom-call | flops 17179869184 | bytes 31457280 | tf_op jit(solution)/shard_map/ffn_forward/pallas_call | solution.py:408
  293.8 18.6 %adapter.1 = (bf16[1024,1024]{1,0:T(8,128)(2,1)}, bf16[1024,1024]{1,0:T(8,128)(2,1)}, f32[1024,1024]{1,0:T(8,128)}, f32[1024,512]{1,0:T(8,128)}, f32[512,1024]{1,0:T(8,128)}, /*index=5*/f32[8,1024]{1,0:T(8,128)}) custom-call(f32[1]{0:T(128)S(6)} %div.3.ramp_ref, f32[1024,1024]{1,0:T(8,128)} %get-tuple-element.41.n2_ref.normal_ref, ...), custom_call_target="tpu_custom_call" | custom-call | flops 6442450944 | bytes 25165824 | tf_op jit(solution)/shard_map/adapter/pallas_call | solution.py:516
  312.4 40.4 %psum.22 = f32[8,1024]{1,0:T(8,128)S(1)} all-reduce(f32[8,1024]{1,0:T(8,128)} %get-tuple-element.63), channel_id=1, replica_groups=mesh['fsdp'=16,'dp'=2] {'fsdp','dp'}, use_global_device_ids=true, to_apply=%region_1.2 | all-reduce | flops 8192 | bytes 65536 | tf_op jit(solution)/shard_map/psum | solution.py:705
  352.8 0.6 slice_multiply_fusion
  353.5 26.2 %ffn_backward.1.g_ref = f32[1024,1024]{1,0:T(8,128)} custom-call(bf16[1024,1024]{1,0:T(8,128)(2,1)} %get-tuple-element.45.g_ref, bf16[1024,13312]{1,0:T(8,128)(2,1)} %all-gather.5.cloned.1.call-done.wo_ref.wq_ref.w_ref.w1_ref.w2_ref.refs_2_.refs_3_, bf16[1024,13312]{1,0:T(8,128)(2,1)} %all-gather.5.cloned.1.call-done.wo_ref.wq_ref.w_ref.w1_ref.w2_ref.refs_2_.refs_3_, ...), custom_call_target="tpu_custom_call" | custom-call | flops 17179869184 | bytes 35651584 | tf_op jit(solution)/shard_map/ffn_backward/pallas_call | solution.py:454
  379.6 8.0 %norm_two_back.1 = (f32[1024,1024]{1,0:T(8,128)}, bf16[1024,1024]{1,0:T(8,128)(2,1)}) custom-call(f32[1024,1024]{1,0:T(8,128)} %ffn_backward.1.g_ref, f32[1024,1024]{1,0:T(8,128)} %get-tuple-element.41.n2_ref.normal_ref, f32[1024,128]{1,0:T(8,128)} %get-tuple-element.48.scale_ref, f32[1,1024]{1,0:T(1,128)} %get-tuple-element.86.gain2_ref.gain_ref, ...), custom_call_target="tpu_custom_call" | custom-call | flops 2147483648 | bytes 20971520 | tf_op jit(solution)/shard_map/norm_two_back/pallas_call | solution.py:571
  387.6 43.6 %cross_backward.1 = (bf16[1024,1024]{1,0:T(8,128)(2,1)}, bf16[1024,1024]{1,0:T(8,128)(2,1)}, bf16[1024,1024]{1,0:T(8,128)(2,1)}) custom-call(bf16[1024,1024]{1,0:T(8,128)(2,1)} %get-tuple-element.39.q_ref, bf16[1024,2048]{1,0:T(8,128)(2,1)} %cross_project.1.k_ref.v_ref, bf16[1024,2048]{1,0:T(8,128)(2,1)} %cross_project.1.k_ref.v_ref, ...), custom_call_target="tpu_custom_call" | custom-call | flops 10737418240 | bytes 18874368 | tf_op jit(solution)/shard_map/cross_backward/pallas_call | solution.py:236
  431.2 0.0 all-reduce.4.cloned.1.call-update
  431.3 9.2 %encoder_back.1 = f32[1024,1024]{1,0:T(8,128)} custom-call(bf16[1024,1024]{1,0:T(8,128)(2,1)} %get-tuple-element.60.refs_0_, bf16[1024,1024]{1,0:T(8,128)(2,1)} %get-tuple-element.61.refs_1_, bf16[1024,13312]{1,0:T(8,128)(2,1)} %all-gather.5.cloned.1.call-done.wo_ref.wq_ref.w_ref.w1_ref.w2_ref.refs_2_.refs_3_, ...), custom_call_target="tpu_custom_call" | custom-call | flops 4294967296 | bytes 16777216 | tf_op jit(solution)/shard_map/encoder_back/pallas_call | solution.py:608
  440.4 0.6 slice_multiply_fusion.3
  441.0 10.9 %norm_one_back.1 = (f32[1024,1024]{1,0:T(8,128)}, bf16[1024,1024]{1,0:T(8,128)(2,1)}) custom-call(f32[1024,1024]{1,0:T(8,128)} %get-tuple-element.49.g_ref, bf16[1024,1024]{1,0:T(8,128)(2,1)} %get-tuple-element.52.dq_ref, bf16[1024,13312]{1,0:T(8,128)(2,1)} %all-gather.5.cloned.1.call-done.wo_ref.wq_ref.w_ref.w1_ref.w2_ref.refs_2_.refs_3_, ...), custom_call_target="tpu_custom_call" | custom-call | flops 4294967296 | bytes 20971520 | tf_op jit(solution)/shard_map/norm_one_back/pallas_call | solution.py:571
  451.9 30.5 %self_backward.1 = (bf16[1024,1024]{1,0:T(8,128)(2,1)}, bf16[1024,1024]{1,0:T(8,128)(2,1)}, bf16[1024,1024]{1,0:T(8,128)(2,1)}) custom-call(bf16[1024,3072]{1,0:T(8,128)(2,1)} %self_project.1.q_ref.k_ref.v_ref, bf16[1024,3072]{1,0:T(8,128)(2,1)} %self_project.1.q_ref.k_ref.v_ref, bf16[1024,3072]{1,0:T(8,128)(2,1)} %self_project.1.q_ref.k_ref.v_ref, ...), custom_call_target="tpu_custom_call" | custom-call | flops 10737418240 | bytes 18874368 | tf_op jit(solution)/shard_map/self_backward/pallas_call | solution.py:236
  482.4 12.5 %input_back.1 = f32[1024,1024]{1,0:T(8,128)} custom-call(bf16[1024,1024]{1,0:T(8,128)(2,1)} %get-tuple-element.56.refs_0_, bf16[1024,1024]{1,0:T(8,128)(2,1)} %get-tuple-element.57.refs_1_, bf16[1024,1024]{1,0:T(8,128)(2,1)} %get-tuple-element.58.refs_2_, bf16[1024,3072]{1,0:T(8,128)(2,1)} %all-gather.3.cloned.1.call-done.w_ref.refs_3_.refs_4_.refs_5_, ...), custom_call_target="tpu_custom_call" | custom-call | flops 6442450944 | bytes 20971520 | tf_op jit(solution)/shard_map/input_back/pallas_call | solution.py:608
  494.9 78.5 %all-reduce.4.cloned.1.call-done = (f32[1024,512]{1,0:T(8,128)}, f32[512,1024]{1,0:T(8,128)}) async-done(((f32[1024,512]{1,0:T(8,128)}, f32[512,1024]{1,0:T(8,128)}), (f32[1024,512]{1,0:T(8,128)}, f32[512,1024]{1,0:T(8,128)})) %all-reduce.4.cloned.1.call-update) | async-done | bytes 4194320 | tf_op jit(solution)/shard_map/psum | solution.py:705
  573.4 0.0 copy-start
  573.4 3.3 broadcast_multiply_fusion.1
  576.7 0.0 copy-done
  576.7 1.5 broadcast_multiply_fusion
  (6 shorter events, 0.0 us)
Async XLA Ops:
  7.2 4.9 copy-start.2
  7.2 5.8 copy-start.3
  7.2 70.5 %all-gather.3.cloned.1.call-start = ((), (), s32[]{:S(2)}) async-start(), calls=%async_computation | async-start | bytes 6684672 | tf_op jit(solution)/shard_map/all_gather | solution.py:650
  12.1 3.5 copy-start.4
  12.1 4.8 copy-start.7
  12.1 4.8 copy-start.5
  12.1 4.8 copy-start.6
  13.0 204.0 %all-gather.5.cloned.1.call-start = ((), (), s32[]{:S(2)}) async-start(), calls=%async_computation.1 | async-start | bytes 28966912 | tf_op jit(solution)/shard_map/all_gather | solution.py:656
  13.0 1.2 copy-start.1
  14.3 559.2 %all-reduce.4.cloned.1.call-start = ((), (), s32[]{:S(2)}) async-start(), calls=%async_computation.2 | async-start | bytes 8388608 | tf_op jit(solution)/shard_map/psum | solution.py:705
  573.4 3.3 copy-start
Sparse Core Ops, SparseCore 0:
  13.1 64.5 all-gather.2
  79.8 137.0 all-gather.4
  431.4 142.0 all-reduce.3

commit v2 on v1

--- a/solution.py
+++ b/solution.py
@@ -470,17 +470,16 @@
 
 
 def adapter_kernel(
-    ramp_ref, n2_ref, ffn_ref, go_ref, down_ref, up_ref, gain2_ref, shift2_ref, gain3_ref, shift3_ref,
+    factor, ramp_ref, n2_ref, ffn_ref, go_ref, down_ref, up_ref, gain2_ref, shift2_ref, gain3_ref, shift3_ref,
     gain_a_ref, shift_a_ref, down_b_ref, up_b_ref,
-    out_ref, gffn_ref, rest_ref, grad_down_ref, grad_up_ref, small_ref,
+    out_ref, gffn_ref, rest_ref, grads_ref,
 ):
     ramp = ramp_ref[0]
+    width, units = down_ref.shape
 
     @pl.when(pl.program_id(0) == 0)
     def _():
-        grad_down_ref[...] = jnp.zeros_like(grad_down_ref)
-        grad_up_ref[...] = jnp.zeros_like(grad_up_ref)
-        small_ref[...] = jnp.zeros_like(small_ref)
+        grads_ref[...] = jnp.zeros_like(grads_ref)
 
     hidden = n2_ref[...] * gain2_ref[...] + shift2_ref[...]
     normal_a, scale_a = normalize(hidden)
@@ -494,27 +493,35 @@
     grad_sum = normalize_back(normal, scale, gain3_ref[...] * go_ref[...].astype(F32))
     gffn_ref[...] = grad_sum.astype(BF16)
     grad_branch = (ramp * grad_sum).astype(BF16)
-    grad_up_ref[...] += dot(adapt_act, grad_branch, 0, 0)
+    grads_ref[0:units] += dot(adapt_act, grad_branch, 0, 0)
     grad_act = dot(grad_branch, up_ref[...], 1, 1).astype(BF16).astype(F32)
     grad_lower = (gate * (1.0 + lower * (1.0 - gate)) * grad_act).astype(BF16)
-    grad_down_ref[...] += dot(adapt_in, grad_lower, 0, 0)
+    for at in range(0, width, units):
+        grads_ref[units : 2 * units, at : at + units] += dot(
+            adapt_in[:, at : at + units], grad_lower, 0, 0
+        )
     grad_adapt = dot(grad_lower, down_ref[...], 1, 1)
     rest_ref[...] = grad_sum + normalize_back(normal_a, scale_a, gain_a_ref[...] * grad_adapt)
-    hidden_units = lower.shape[1]
-    small_ref[0:1, 0:hidden_units] += jnp.sum(grad_lower.astype(F32), 0, keepdims=True)
-    small_ref[1:2] += jnp.sum(grad_branch.astype(F32), 0, keepdims=True)
-    small_ref[2:3] += jnp.sum(grad_adapt * normal_a, 0, keepdims=True)
-    small_ref[3:4] += jnp.sum(grad_adapt, 0, keepdims=True)
-
-
-def adapter(ramp, normal2, ffn, grad_out, down, up, vectors, down_bias):
+    for at, row in enumerate(
+        (grad_branch.astype(F32), grad_adapt * normal_a, grad_adapt, grad_lower.astype(F32))
+    ):
+        grads_ref[2 * units + at : 2 * units + at + 1, 0 : row.shape[1]] += jnp.sum(
+            row, 0, keepdims=True
+        )
+
+    @pl.when(pl.program_id(0) == pl.num_programs(0) - 1)
+    def _():
+        grads_ref[...] *= factor
+
+
+def adapter(ramp, normal2, ffn, grad_out, down, up, vectors, down_bias, extra, factor):
     rows, width = normal2.shape
     units = down.shape[1]
     step = 256
     vector = whole((1, width))
     gain2, shift2, gain3, shift3, gain_a, shift_a, up_bias = vectors
     return call(
-        adapter_kernel,
+        functools.partial(adapter_kernel, factor),
         "adapter",
         (rows // step,),
         [pl.BlockSpec(memory_space=pltpu.SMEM)]
@@ -522,14 +529,12 @@
         + [whole(down.shape), whole(up.shape)]
         + [vector] * 6
         + [whole((1, units)), vector],
-        [rows_block(step, width)] * 3 + [whole(down.shape), whole(up.shape), whole((8, width))],
+        [rows_block(step, width)] * 3 + [whole((2 * units + extra, width))],
         [
             jax.ShapeDtypeStruct((rows, width), BF16),
             jax.ShapeDtypeStruct((rows, width), BF16),
             jax.ShapeDtypeStruct((rows, width), F32),
-            jax.ShapeDtypeStruct(down.shape, F32),
-            jax.ShapeDtypeStruct(up.shape, F32),
-            jax.ShapeDtypeStruct((8, width), F32),
+            jax.ShapeDtypeStruct((2 * units + extra, width), F32),
         ],
         12 * rows * width * units,
         18 * rows * width + 12 * width * units,
@@ -617,6 +622,20 @@
         2 * rows * width * width * count,
         rows * width * (2 * count + 8) + 2 * count * width * width,
     )(*grads, *([weights] * count), *([start] if start is not None else []))
+
+
+def gather(shard):
+    return lax.all_gather(shard, "fsdp", axis=0, tiled=True)
+
+
+def total_sum(part):
+    count = lax.axis_size("dp")
+    mine = lax.psum_scatter(part, "fsdp", scatter_dimension=0, tiled=True)
+    total, travel = mine, mine
+    for _ in range(count - 1):
+        travel = lax.ppermute(travel, "dp", [(at, (at + 1) % count) for at in range(count)])
+        total = total + travel
+    return gather(total)
 
 
 def local(
@@ -647,16 +666,14 @@
     held = attn_in.shape[0]
     groups = ffn_out.shape[0] // held
     wide = ffn_in.shape[1]
-    self_w = lax.all_gather(attn_in[:, 0 : 3 * width], "fsdp", axis=0, tiled=True)
-    rest_w = jnp.concatenate(
-        [ffn_out[at * held : (at + 1) * held] for at in range(groups)]
-        + [ffn_in, attn_in[:, 3 * width :], attn_out],
-        1,
-    )
-    rest_w = lax.all_gather(rest_w, "fsdp", axis=0, tiled=True)
+    pad = jnp.zeros((held, 128), BF16)
+    attn_w = gather(jnp.concatenate([attn_in, attn_out, pad], 1))
+    ffn_w = jnp.concatenate(
+        [ffn_out[at * held : (at + 1) * held] for at in range(groups)] + [ffn_in, pad], 1
+    )
+    ffn_w = gather(ffn_w)
     w1_at, w2_at = wide, 0
-    cq_at = 2 * wide // width
-    ck_at, so_at, co_at = cq_at + 1, cq_at + 3, cq_at + 4
+    cq_at, ck_at, so_at, co_at = 3, 4, 6, 7
 
     ramp = (4.0 * step.astype(F32) / RAMP).reshape(1)
     bias = [attn_bias[at : at + 1] for at in range(6)]
@@ -669,27 +686,28 @@
     per = width // 128
 
     qkv = project(
-        tokens, self_w, 0, 3 * width, jnp.concatenate([bias[0], none, bias[1]], 1), "self_project"
+        tokens, attn_w, 0, 3 * width, jnp.concatenate([bias[0], none, bias[1]], 1), "self_project"
     )
     self_ctx, self_lse = attend_forward(
         qkv, 0, qkv, per, qkv, 2 * per, self_extra, width, True
     )
     normal1, scale1, cross_q = post_self(
-        tokens, self_ctx, rest_w, so_at, cq_at, bias[2], gain[0], shift[0], bias[3]
+        tokens, self_ctx, attn_w, so_at, cq_at, bias[2], gain[0], shift[0], bias[3]
     )
     cross_kv = project(
-        states, rest_w, ck_at * width, 2 * width, jnp.concatenate([none, bias[4]], 1), "cross_project"
+        states, attn_w, ck_at * width, 2 * width, jnp.concatenate([none, bias[4]], 1), "cross_project"
     )
     cross_ctx, cross_lse = attend_forward(
         cross_q, 0, cross_kv, 0, cross_kv, per, cross_extra, width, False
     )
     normal2, scale2, hidden2 = post_cross(
-        normal1, cross_ctx, rest_w, co_at, bias[5], gain[0], shift[0], gain[1], shift[1]
+        normal1, cross_ctx, attn_w, co_at, bias[5], gain[0], shift[0], gain[1], shift[1]
     )
     ffn, slope = ffn_forward(
-        hidden2, rest_w, w2_at, w1_at, ffn_in_bias[None], ffn_out_bias[None], held
-    )
-    layer_out, grad_ffn, grad_rest, grad_down, grad_up, small = adapter(
+        hidden2, ffn_w, w2_at, w1_at, ffn_in_bias[None], ffn_out_bias[None], held
+    )
+    token_total = sequences * row_count * lax.axis_size("fsdp") * lax.axis_size("dp")
+    layer_out, grad_ffn, grad_rest, adapter_grads = adapter(
         ramp,
         normal2,
         ffn,
@@ -701,36 +719,38 @@
             adapter_up_bias[None],
         ),
         adapter_down_bias[None],
-    )
-    grad_down, grad_up, small = lax.psum((grad_down, grad_up, small), ("fsdp", "dp"))
-    grad_hidden2 = ffn_backward(grad_ffn, rest_w, w2_at, w1_at, slope, grad_rest, held)
-    grad_sum2, grad_cross = norm_back(grad_hidden2, normal2, scale2, gain[1], rest_w, co_at)
+        8 * lax.axis_size("fsdp"),
+        1.0 / math.sqrt(token_total),
+    )
+    adapter_grads = total_sum(adapter_grads)
+    grad_hidden2 = ffn_backward(grad_ffn, ffn_w, w2_at, w1_at, slope, grad_rest, held)
+    grad_sum2, grad_cross = norm_back(grad_hidden2, normal2, scale2, gain[1], attn_w, co_at)
     cross_dq, cross_dk, cross_dv = attend_backward(
         cross_q, 0, cross_kv, 0, cross_kv, per, cross_ctx, grad_cross, cross_lse, cross_extra,
         width, False,
     )
-    grad_encoder = back_project((cross_dk, cross_dv), rest_w, ck_at, None, "encoder_back")
+    grad_encoder = back_project((cross_dk, cross_dv), attn_w, ck_at, None, "encoder_back")
     grad_sum1, grad_self = norm_back(
-        grad_sum2, normal1, scale1, gain[0], rest_w, so_at, cross_dq, cq_at
+        grad_sum2, normal1, scale1, gain[0], attn_w, so_at, cross_dq, cq_at
     )
     self_grads = attend_backward(
         qkv, 0, qkv, per, qkv, 2 * per, self_ctx, grad_self, self_lse, self_extra, width, True
     )
-    grad_input = back_project(self_grads, self_w, 0, grad_sum1, "input_back")
-
-    token_total = sequences * row_count * lax.axis_size("fsdp") * lax.axis_size("dp")
-    factor = 1.0 / math.sqrt(token_total)
+    grad_input = back_project(self_grads, attn_w, 0, grad_sum1, "input_back")
+
     units = adapter_down.shape[1]
+    grad_down = [adapter_grads[units : 2 * units, at : at + units] for at in range(0, width, units)]
+    small = adapter_grads[2 * units :]
     return (
         layer_out.reshape(inputs.shape),
         grad_input.reshape(inputs.shape),
         grad_encoder.reshape(encoder.shape),
-        grad_down * factor,
-        small[0, :units] * factor,
-        grad_up * factor,
-        small[1] * factor,
-        small[2] * factor,
-        small[3] * factor,
+        jnp.concatenate(grad_down, 0),
+        small[3, :units],
+        adapter_grads[:units],
+        small[0],
+        small[1],
+        small[2],
     )
 
 

time: 594 us -> 494 us (0.83)
  waiting for transfers between devices: 246 us -> 180 us
  blocking collectives: 40.4 us -> 0 us
    psum x1 -> x0, waiting for transfers between devices: 78.5 us -> none  [local(): lax.psum((grad_down, grad_up, small), ('fsdp', 'dp'))]
    reduce_scatter x0 -> x1, waiting for transfers between devices: none -> 75.6 us  [total_sum(): mine = lax.psum_scatter(part, 'fsdp', scatter_dimension=0, tiled=True)]
    all_gather x2 -> x3, waiting for transfers between devices: 167 us -> 98.1 us  [gather(): return lax.all_gather(shard, 'fsdp', axis=0, tiled=True)]
    psum x1 -> x0, blocking collectives: 40.4 us -> none  [local(): lax.psum((grad_down, grad_up, small), ('fsdp', 'dp'))]
    slice x0 -> x4, local copies, waits for them, and re-layouts: none -> 7.64 us  [the longest x1 3.16 us: local(): adapter_grads[:units]]
    ppermute x0 -> x1, waiting for transfers between devices: none -> 6.53 us  [total_sum(): lax.ppermute(travel, 'dp', [(at, (at + 1) % count) for at in range(count)])]
    mul x4 -> x0, other arithmetic: 6.03 us -> none  [the longest x1 3.3 us: local(): grad_down * factor]
  transfers between devices with their start and end apart: 3 -> 5, of which waited for: 3 -> 4; matrix products, arithmetic and copies ran while one was open for 1% -> 1% of each run, Pallas kernels for 16% -> 46%
where the time goes in v2:
time: 494 us; the launch traced here: 485 us
  Pallas kernels  269 us (54%)
  waiting for transfers between devices  180 us (36%)
  between operations  15.7 us (3%)
  local copies, waits for them, and re-layouts  10.6 us (2%)
  other arithmetic  7.33 us (1%)
    all_gather x3, waiting for transfers between devices, gather(): return lax.all_gather(shard, 'fsdp', axis=0, tiled=True)  98.1 us
    reduce_scatter x1, waiting for transfers between devices, total_sum(): mine = lax.psum_scatter(part, 'fsdp', scatter_dimension=0, tiled=True)  75.6 us
    pallas_call x2, Pallas kernels, attend_backward(): call(functools.partial(attend_backward_kernel, causal, 256), 'self_backwa...  74 us
    pallas_call x2, Pallas kernels, attend_forward(): call(functools.partial(attend_forward_kernel, causal, 256, 2), 'self_forw...  44 us
    pallas_call x1, Pallas kernels, ffn_forward(): call(functools.partial(ffn_forward_kernel, held), 'ffn_forward', (wide //...  26.4 us
    pallas_call x1, Pallas kernels, ffn_backward(): call(functools.partial(ffn_backward_kernel, held), 'ffn_backward', (wide...  26.1 us
    pallas_call x2, Pallas kernels, back_project(): call(functools.partial(back_project_kernel, count, start is not None), na...  21.6 us
    pallas_call x1, Pallas kernels, adapter(): call(functools.partial(adapter_kernel, factor), 'adapter', (rows // step,...  21.1 us
  transfers between devices with their start and end apart: 5, of which 4 were waited for; matrix products, arithmetic and copies ran while one was open for 1% of the time, Pallas kernels for 46%

profile of v2, /device:TPU:0, one launch (start us, length us, event | category | flops | bytes accessed | tf_op | source)
XLA Modules:
  0.0 484.8 jit_solution(7042017347196467908)
XLA Ops:
  7.2 0.0 copy-start.1
  7.2 0.0 all-gather.4.cloned.1.call-start
  7.2 0.0 copy-start.2
  7.3 2.3 pad_maximum_fusion.1
  9.6 0.0 copy-start.3
  9.6 0.0 copy-start.6
  9.6 0.0 copy-start.4
  9.6 0.0 copy-start.5
  9.6 0.0 all-gather.4.cloned.1.call-update
  9.6 0.0 all-gather.6.cloned.1.call-start
  9.7 0.0 copy-done.1
  9.8 0.0 copy-done.2
  9.8 0.0 copy-start
  9.8 1.0 copy-done
  10.8 0.0 all-gather.6.cloned.1.call-update
  10.9 0.0 reduce-scatter.2.cloned.1.call-start
  12.2 0.0 copy-done.3
  12.2 0.6 fusion.3
  12.8 0.6 concatenate.17.bias_ref
  13.5 0.0 copy-done.6
  13.5 0.0 copy-done.4
  13.5 0.0 copy-done.5
  13.5 0.6 fusion.4
  14.1 1.1 select_convert_fusion
  15.3 0.6 pad_maximum_fusion.2.bias_ref
  15.9 87.3 %all-gather.4.cloned.1.call-done.w_ref.wo_ref.wq_ref.refs_3_.refs_4_.refs_5_.refs_2_ = bf16[1024,8320]{1,0:T(8,128)(2,1)} async-done(((bf16[64,8320]{1,0:T(8,128)(2,1)}), bf16[1024,8320]{1,0:T(8,128)(2,1)}) %all-gather.4.cloned.1.call-update) | async-done | bytes 17039376 | tf_op jit(solution)/shard_map/all_gather | solution.py:628
  103.2 11.6 %self_project.1.q_ref.k_ref.v_ref = bf16[1024,3072]{1,0:T(8,128)(2,1)} custom-call(bf16[1024,1024]{1,0:T(8,128)(2,1)} %bitcast.19, bf16[1024,8320]{1,0:T(8,128)(2,1)} %all-gather.4.cloned.1.call-done.w_ref.wo_ref.wq_ref.refs_3_.refs_4_.refs_5_.refs_2_, f32[1,3072]{1,0:T(1,128)} %pad_maximum_fusion.2.bias_ref), custom_call_target="tpu_custom_call" | custom-call | flops 6442450944 | bytes 14680064 | tf_op jit(solution)/shard_map/self_project/pallas_call | solution.py:263
  114.8 19.1 %self_forward.1 = (bf16[1024,1024]{1,0:T(8,128)(2,1)}, bf16[1024,1024]{1,0:T(8,128)(2,1)}) custom-call(bf16[1024,3072]{1,0:T(8,128)(2,1)} %self_project.1.q_ref.k_ref.v_ref, bf16[1024,3072]{1,0:T(8,128)(2,1)} %self_project.1.q_ref.k_ref.v_ref, bf16[1024,3072]{1,0:T(8,128)(2,1)} %self_project.1.q_ref.k_ref.v_ref, bf16[1024,128]{1,0:T(8,128)(2,1)} %get-tuple-element.79.extra_ref), custom_call_target="tpu_custom_call" | custom-call | flops 4294967296 | bytes 12582912 | tf_op jit(solution)/shard_map/self_forward/pallas_call | solution.py:215
  133.9 8.6 %cross_project.1.k_ref.v_ref = bf16[1024,2048]{1,0:T(8,128)(2,1)} custom-call(bf16[1024,1024]{1,0:T(8,128)(2,1)} %bitcast.23, bf16[1024,8320]{1,0:T(8,128)(2,1)} %all-gather.4.cloned.1.call-done.w_ref.wo_ref.wq_ref.refs_3_.refs_4_.refs_5_.refs_2_, f32[1,2048]{1,0:T(1,128)} %concatenate.17.bias_ref), custom_call_target="tpu_custom_call" | custom-call | flops 4294967296 | bytes 10485760 | tf_op jit(solution)/shard_map/cross_project/pallas_call | solution.py:263
  142.5 9.2 %post_self.1 = (f32[1024,1024]{1,0:T(8,128)}, f32[1024,128]{1,0:T(8,128)}, bf16[1024,1024]{1,0:T(8,128)(2,1)}) custom-call(bf16[1024,1024]{1,0:T(8,128)(2,1)} %bitcast.20, bf16[1024,1024]{1,0:T(8,128)(2,1)} %get-tuple-element.35.ctx_ref.out_ref, bf16[1024,8320]{1,0:T(8,128)(2,1)} %all-gather.4.cloned.1.call-done.w_ref.wo_ref.wq_ref.refs_3_.refs_4_.refs_5_.refs_2_, ...), custom_call_target="tpu_custom_call" | custom-call | flops 4294967296 | bytes 14680064 | tf_op jit(solution)/shard_map/post_self/pallas_call | solution.py:300
  151.7 24.8 %cross_forward.1 = (bf16[1024,1024]{1,0:T(8,128)(2,1)}, bf16[1024,1024]{1,0:T(8,128)(2,1)}) custom-call(bf16[1024,1024]{1,0:T(8,128)(2,1)} %get-tuple-element.37.q_ref, bf16[1024,2048]{1,0:T(8,128)(2,1)} %cross_project.1.k_ref.v_ref, bf16[1024,2048]{1,0:T(8,128)(2,1)} %cross_project.1.k_ref.v_ref, bf16[1024,128]{1,0:T(8,128)(2,1)} %get-tuple-element.78.extra_ref), custom_call_target="tpu_custom_call" | custom-call | flops 4294967296 | bytes 12582912 | tf_op jit(solution)/shard_map/cross_forward/pallas_call | solution.py:215
  176.5 7.9 %post_cross.1 = (f32[1024,1024]{1,0:T(8,128)}, f32[1024,128]{1,0:T(8,128)}, bf16[1024,1024]{1,0:T(8,128)(2,1)}) custom-call(f32[1024,1024]{1,0:T(8,128)} %get-tuple-element.36.n1_ref.normal_ref, bf16[1024,1024]{1,0:T(8,128)(2,1)} %get-tuple-element.38.ctx_ref.out_ref, ...), custom_call_target="tpu_custom_call" | custom-call | flops 2147483648 | bytes 14680064 | tf_op jit(solution)/shard_map/post_cross/pallas_call | solution.py:346
  184.5 10.7 %all-gather.6.cloned.1.call-done.w1_ref.w2_ref = bf16[1024,8320]{1,0:T(8,128)(2,1)} async-done(((bf16[64,8320]{1,0:T(8,128)(2,1)}), bf16[1024,8320]{1,0:T(8,128)(2,1)}) %all-gather.6.cloned.1.call-update) | async-done | bytes 17039376 | tf_op jit(solution)/shard_map/all_gather | solution.py:628
  195.2 26.4 %ffn_forward.1 = (f32[1024,1024]{1,0:T(8,128)}, bf16[1024,4096]{1,0:T(8,128)(2,1)}) custom-call(bf16[1024,1024]{1,0:T(8,128)(2,1)} %get-tuple-element.40.h_ref, bf16[1024,8320]{1,0:T(8,128)(2,1)} %all-gather.6.cloned.1.call-done.w1_ref.w2_ref, bf16[1024,8320]{1,0:T(8,128)(2,1)} %all-gather.6.cloned.1.call-done.w1_ref.w2_ref, f32[1,4096]{1,0:T(1,128)} %bitcast.30, ...), custom_call_target="tpu_custom_call" | custom-call | flops 17179869184 | bytes 31457280 | tf_op jit(solution)/shard_map/ffn_forward/pallas_call | solution.py:408
  221.6 21.1 %adapter.1 = (bf16[1024,1024]{1,0:T(8,128)(2,1)}, bf16[1024,1024]{1,0:T(8,128)(2,1)}, f32[1024,1024]{1,0:T(8,128)}, f32[1152,1024]{1,0:T(8,128)}) custom-call(f32[1]{0:T(128)S(6)} %div.3.ramp_ref, f32[1024,1024]{1,0:T(8,128)} %get-tuple-element.39.n2_ref.normal_ref, f32[1024,1024]{1,0:T(8,128)} %get-tuple-element.41.ffn_ref, bf16[1024,1024]{1,0:T(8,128)(2,1)} %bitcast.29, ...), custom_call_target="tpu_custom_call" | custom-call | flops 6442450944 | bytes 25165824 | tf_op jit(solution)/shard_map/adapter/pallas_call | solution.py:523
  242.7 0.0 reduce-scatter.2.cloned.1.call-update
  242.7 0.0 all-gather.8.cloned.1.call-start
  242.7 75.6 %reduce-scatter.2.cloned.1.call-done = f32[72,1024]{1,0:T(8,128)} async-done(((f32[1152,1024]{1,0:T(8,128)}), f32[72,1024]{1,0:T(8,128)}) %reduce-scatter.2.cloned.1.call-update) | async-done | bytes 294928 | tf_op jit(solution)/shard_map/reduce_scatter | solution.py:633
  318.3 1.5 collective-permute-start
  319.8 6.5 %collective-permute-done = f32[72,1024]{1,0:T(8,128)S(1)} collective-permute-done((f32[72,1024]{1,0:T(8,128)}, f32[72,1024]{1,0:T(8,128)S(1)}, u32[]{:S(2)}, u32[]{:S(2)}) %collective-permute-start) | collective-permute-done | bytes 294944 | tf_op jit(solution)/shard_map/ppermute | solution.py:636
  326.3 1.7 add.29
  328.1 0.0 all-gather.8.cloned.1.call-update
  328.1 26.1 %ffn_backward.1.g_ref = f32[1024,1024]{1,0:T(8,128)} custom-call(bf16[1024,1024]{1,0:T(8,128)(2,1)} %get-tuple-element.43.g_ref, bf16[1024,8320]{1,0:T(8,128)(2,1)} %all-gather.6.cloned.1.call-done.w1_ref.w2_ref, bf16[1024,8320]{1,0:T(8,128)(2,1)} %all-gather.6.cloned.1.call-done.w1_ref.w2_ref, bf16[1024,4096]{1,0:T(8,128)(2,1)} %get-tuple-element.44.slope_ref, ...), custom_call_target="tpu_custom_call" | custom-call | flops 17179869184 | bytes 35651584 | tf_op jit(solution)/shard_map/ffn_backward/pallas_call | solution.py:454
  354.3 8.1 %norm_two_back.1 = (f32[1024,1024]{1,0:T(8,128)}, bf16[1024,1024]{1,0:T(8,128)(2,1)}) custom-call(f32[1024,1024]{1,0:T(8,128)} %ffn_backward.1.g_ref, f32[1024,1024]{1,0:T(8,128)} %get-tuple-element.39.n2_ref.normal_ref, f32[1024,128]{1,0:T(8,128)} %get-tuple-element.46.scale_ref, f32[1,1024]{1,0:T(1,128)} %get-tuple-element.80.gain2_ref.gain_ref, ...), custom_call_target="tpu_custom_call" | custom-call | flops 2147483648 | bytes 20971520 | tf_op jit(solution)/shard_map/norm_two_back/pallas_call | solution.py:576
  362.3 43.6 %cross_backward.1 = (bf16[1024,1024]{1,0:T(8,128)(2,1)}, bf16[1024,1024]{1,0:T(8,128)(2,1)}, bf16[1024,1024]{1,0:T(8,128)(2,1)}) custom-call(bf16[1024,1024]{1,0:T(8,128)(2,1)} %get-tuple-element.37.q_ref, bf16[1024,2048]{1,0:T(8,128)(2,1)} %cross_project.1.k_ref.v_ref, bf16[1024,2048]{1,0:T(8,128)(2,1)} %cross_project.1.k_ref.v_ref, ...), custom_call_target="tpu_custom_call" | custom-call | flops 10737418240 | bytes 18874368 | tf_op jit(solution)/shard_map/cross_backward/pallas_call | solution.py:236
  405.9 9.1 %encoder_back.1 = f32[1024,1024]{1,0:T(8,128)} custom-call(bf16[1024,1024]{1,0:T(8,128)(2,1)} %get-tuple-element.58.refs_0_, bf16[1024,1024]{1,0:T(8,128)(2,1)} %get-tuple-element.59.refs_1_, bf16[1024,8320]{1,0:T(8,128)(2,1)} %all-gather.4.cloned.1.call-done.w_ref.wo_ref.wq_ref.refs_3_.refs_4_.refs_5_.refs_2_, ...), custom_call_target="tpu_custom_call" | custom-call | flops 4294967296 | bytes 16777216 | tf_op jit(solution)/shard_map/encoder_back/pallas_call | solution.py:613
  415.0 10.8 %norm_one_back.1 = (f32[1024,1024]{1,0:T(8,128)}, bf16[1024,1024]{1,0:T(8,128)(2,1)}) custom-call(f32[1024,1024]{1,0:T(8,128)} %get-tuple-element.47.g_ref, bf16[1024,1024]{1,0:T(8,128)(2,1)} %get-tuple-element.50.dq_ref, bf16[1024,8320]{1,0:T(8,128)(2,1)} %all-gather.4.cloned.1.call-done.w_ref.wo_ref.wq_ref.refs_3_.refs_4_.refs_5_.refs_2_, ...), custom_call_target="tpu_custom_call" | custom-call | flops 4294967296 | bytes 20971520 | tf_op jit(solution)/shard_map/norm_one_back/pallas_call | solution.py:576
  425.8 30.5 %self_backward.1 = (bf16[1024,1024]{1,0:T(8,128)(2,1)}, bf16[1024,1024]{1,0:T(8,128)(2,1)}, bf16[1024,1024]{1,0:T(8,128)(2,1)}) custom-call(bf16[1024,3072]{1,0:T(8,128)(2,1)} %self_project.1.q_ref.k_ref.v_ref, bf16[1024,3072]{1,0:T(8,128)(2,1)} %self_project.1.q_ref.k_ref.v_ref, bf16[1024,3072]{1,0:T(8,128)(2,1)} %self_project.1.q_ref.k_ref.v_ref, ...), custom_call_target="tpu_custom_call" | custom-call | flops 10737418240 | bytes 18874368 | tf_op jit(solution)/shard_map/self_backward/pallas_call | solution.py:236
  456.2 12.5 %input_back.1 = f32[1024,1024]{1,0:T(8,128)} custom-call(bf16[1024,1024]{1,0:T(8,128)(2,1)} %get-tuple-element.54.refs_0_, bf16[1024,1024]{1,0:T(8,128)(2,1)} %get-tuple-element.55.refs_1_, bf16[1024,1024]{1,0:T(8,128)(2,1)} %get-tuple-element.56.refs_2_, bf16[1024,8320]{1,0:T(8,128)(2,1)} %all-gather.4.cloned.1.call-done.w_ref.wo_ref.wq_ref.refs_3_.refs_4_.refs_5_.refs_2_, ...), custom_call_target="tpu_custom_call" | custom-call | flops 6442450944 | bytes 20971520 | tf_op jit(solution)/shard_map/input_back/pallas_call | solution.py:613
  468.7 0.0 all-gather.8.cloned.1.call-done
  468.7 1.7 fusion.2
  470.4 1.5 pad_maximum_fusion
  471.9 1.3 slice.99
  473.2 1.5 fusion.1
  474.7 3.2 slice.100
  (12 shorter events, 0.1 us)
Async XLA Ops:
  7.2 2.5 copy-start.1
  7.2 96.0 %all-gather.4.cloned.1.call-start = ((), (), s32[]{:S(2)}) async-start(), calls=%async_computation.1 | async-start | bytes 18104320 | tf_op jit(solution)/shard_map/all_gather | solution.py:628
  7.2 2.5 copy-start.2
  9.6 2.6 copy-start.3
  9.6 3.9 copy-start.6
  9.6 3.9 copy-start.4
  9.6 3.9 copy-start.5
  9.6 185.5 %all-gather.6.cloned.1.call-start = ((), (), s32[]{:S(2)}) async-start(), calls=%async_computation.2 | async-start | bytes 18104320 | tf_op jit(solution)/shard_map/all_gather | solution.py:628
  9.8 1.0 copy-start
  10.9 307.5 %reduce-scatter.2.cloned.1.call-start = ((), (), s32[]{:S(2)}) async-start(), calls=%async_computation.3 | async-start | bytes 5013504 | tf_op jit(solution)/shard_map/reduce_scatter | solution.py:633
  242.7 226.0 %all-gather.8.cloned.1.call-start = ((), (), s32[]{:S(2)}) async-start(), calls=%async_computation.4 | async-start | bytes 5013504 | tf_op jit(solution)/shard_map/all_gather | solution.py:628
  318.3 8.0 %collective-permute-start = (f32[72,1024]{1,0:T(8,128)}, f32[72,1024]{1,0:T(8,128)S(1)}, u32[]{:S(2)}, u32[]{:S(2)}) collective-permute-start(f32[72,1024]{1,0:T(8,128)} %reduce-scatter.2.cloned.1.call-done), channel_id=1, source_target_pairs={{0,1},{1,0},{2,3},{3,2},{4,5},{5,4},{6,7},{7,6},{8,9},{9,8},{10,11... | collective-permute-start | bytes 884744 | tf_op jit(solution)/shard_map/ppermute | solution.py:636
Sparse Core Ops, SparseCore 0:
  10.2 93.0 all-gather.3
  104.8 90.2 all-gather.5
  242.8 75.4 reduce-scatter.1
  328.2 52.1 all-gather.7

commit v3 on v0

v3 whole, which is shorter than its diff:
```python
import functools
import math

import jax
import jax.numpy as jnp
from jax import lax
from jax.experimental import pallas as pl
from jax.experimental.pallas import tpu as pltpu
from jax.sharding import PartitionSpec as P

HEADS = 16
RAMP = 1000
EPS = 1e-05
F32 = jnp.float32
BF16 = jnp.bfloat16
VMEM_LIMIT = 58 * 2**20


def dot(left, right, left_dim, right_dim):
    return lax.dot_general(
        left, right, (((left_dim,), (right_dim,)), ((), ())), preferred_element_type=F32
    )


def call(kernel, name, grid, in_specs, out_specs, out_shape, flops, moved, exps=0, scratch=()):
    return pl.pallas_call(
        kernel,
        name=name,
        grid=grid,
        in_specs=in_specs,
        out_specs=out_specs,
        out_shape=out_shape,
        scratch_shapes=scratch,
        compiler_params=pltpu.CompilerParams(vmem_limit_bytes=VMEM_LIMIT),
        cost_estimate=pl.CostEstimate(
            flops=int(flops), bytes_accessed=int(moved), transcendentals=int(exps)
        ),
    )


def whole(shape):
    return pl.BlockSpec(shape, lambda *_: (0,) * len(shape), pipeline_mode=pl.Buffered(1))


def columns(rows, width, first=0):
    return pl.BlockSpec((rows, width), lambda i: (0, i + first))


def square(width, at):
    return pl.BlockSpec((width, width), lambda i: (0, at), pipeline_mode=pl.Buffered(1))


def normalize(values):
    center = values - jnp.mean(values, -1, keepdims=True)
    scale = lax.rsqrt(jnp.mean(center * center, -1, keepdims=True) + EPS)
    return center * scale, scale


def normalize_back(normal, scale, grad):
    return scale * (
        grad
        - jnp.mean(grad, -1, keepdims=True)
        - normal * jnp.mean(grad * normal, -1, keepdims=True)
    )


def split_three(values):
    high = values.astype(BF16).astype(F32)
    middle = (values - high).astype(BF16).astype(F32)
    return high, middle, values - high - middle


GROUP = 4
CHUNK = 256
SIZE = 64


def attend_forward(causal, ahead, q_ref, k_ref, v_ref, length, ctx_ref, expo_ref, inverse_ref):
    rows, keys = q_ref.shape[0], k_ref.shape[0]
    width = 2 * SIZE
    lane = lax.broadcasted_iota(jnp.int32, (rows, width), 1)
    key_lane = lax.broadcasted_iota(jnp.int32, (keys, width), 1)
    key_row = lax.broadcasted_iota(jnp.int32, (keys, width), 0)
    picks = jnp.where(lane % SIZE == 0, 1.0, 0.0).astype(BF16)
    extra = jnp.where(key_row < length, 0.0, -1e30).astype(BF16)
    one = jnp.asarray(1.0, BF16)
    left = lane[:CHUNK] < SIZE
    head_q, head_k, head_v = [], [], []
    for at in range(0, q_ref.shape[1], width):
        queries = q_ref[:, at : at + width]
        key_rows, value_rows = k_ref[:, at : at + width], v_ref[:, at : at + width]
        head_q += [jnp.where(lane < SIZE, queries, picks), jnp.where(lane < SIZE, picks, queries)]
        head_k += [
            jnp.where(key_lane < SIZE, key_rows, extra),
            jnp.where(key_lane < SIZE, extra, key_rows),
        ]
        head_v += [
            jnp.where(key_lane < SIZE, value_rows, one),
            jnp.where(key_lane < SIZE, one, value_rows),
        ]

    def scores(at, head):
        low, high = at * CHUNK, (at + 1) * CHUNK
        live = high if causal else keys
        found = dot(head_q[head][low:high], head_k[head][:live], 1, 1)
        if not causal:
            return found
        query_at = lax.broadcasted_iota(jnp.int32, (CHUNK, CHUNK), 0)
        key_at = lax.broadcasted_iota(jnp.int32, (CHUNK, CHUNK), 1)
        edge = jnp.where(key_at <= query_at, found[:, low:high], -1e30)
        return jnp.concatenate([found[:, :low], edge], 1) if low else edge

    done, waiting = {}, []

    def finish(at, head, found):
        low, high = at * CHUNK, (at + 1) * CHUNK
        live = found.shape[1]
        top = jnp.max(found, 1, keepdims=True)
        expo = jnp.exp(found - top).astype(BF16)
        expo_ref[head, low:high, :live] = expo
        done[head] = dot(expo, head_v[head][:live], 1, 0)
        if head % 2:
            first, second = done[head - 1], done[head]
            inverse = 1.0 / jnp.where(left, pltpu.roll(first, SIZE, 1), pltpu.roll(second, SIZE, 1))
            span = slice(head // 2 * width, (head // 2 + 1) * width)
            inverse_ref[low:high, span] = inverse
            ctx_ref[low:high, span] = (jnp.where(left, first, second) * inverse).astype(BF16)

    for pair in range(len(head_q) // 2):
        for at in range(rows // CHUNK):
            for head in (2 * pair, 2 * pair + 1):
                waiting.append((at, head, scores(at, head)))
                if len(waiting) > ahead:
                    finish(*waiting.pop(0))
    for unit in waiting:
        finish(*unit)


def attend_backward(
    causal, q_ref, k_ref, v_ref, ctx_ref, grad_ref, expo_ref, inverse_ref, dq_ref, dk_ref, dv_ref, s_scr,
    before, after,
):
    rows, keys = q_ref.shape[0], k_ref.shape[0]
    width = 2 * SIZE
    count = rows // CHUNK
    lane = lax.broadcasted_iota(jnp.int32, (rows, width), 1)
    key_lane = lax.broadcasted_iota(jnp.int32, (keys, width), 1)
    place = key_lane % SIZE
    ones = jnp.where((place >= 1) & (place <= 3), 1.0, 0.0).astype(BF16)
    for pair in range(q_ref.shape[1] // width):
        span = slice(pair * width, (pair + 1) * width)
        key_rows, value_rows = k_ref[:, span], v_ref[:, span]
        grads = (grad_ref[:, span].astype(F32) * inverse_ref[:, span]).astype(BF16)
        wide = grads.astype(F32)
        products = wide * ctx_ref[:, span].astype(F32)
        queries_t, grads_t = q_ref[:, span].T, grads.T
        head_g, head_v = [], []
        for head in range(2):
            mine = (lane < SIZE) if head == 0 else (lane >= SIZE)
            key_mine = (key_lane < SIZE) if head == 0 else (key_lane >= SIZE)
            base = SIZE if head == 0 else 0
            head_v.append(jnp.where(key_mine, value_rows, ones))
            dots = split_three(-jnp.sum(jnp.where(mine, products, 0.0), 1, keepdims=True))
            grad = jnp.where(mine, wide, 0.0)
            for index, part in enumerate(dots):
                grad = jnp.where(lane == base + index + 1, part, grad)
            head_g.append(grad.astype(BF16))

        grad_q, waiting = {}, []
        before(pair)

        def finish(at, head, grad_p, pair=pair, span=span, key_rows=key_rows, grad_q=grad_q):
            low, high = at * CHUNK, (at + 1) * CHUNK
            live = grad_p.shape[1]
            expo = expo_ref[2 * pair + head, low:high, :live]
            grad_s = (expo.astype(F32) * grad_p).astype(BF16)
            s_scr[head, low:high, :live] = grad_s
            grad_q[head] = dot(grad_s, key_rows[:live], 1, 0)
            if head:
                both = jnp.where(lane[low:high] < SIZE, grad_q[0], grad_q[1])
                dq_ref[low:high, span] = (both * SIZE**-0.5).astype(BF16)

        for at in range(count):
            for head in range(2):
                low, high = at * CHUNK, (at + 1) * CHUNK
                live = high if causal else keys
                waiting.append((at, head, dot(head_g[head][low:high], head_v[head][:live], 1, 1)))
                if len(waiting) > 1:
                    finish(*waiting.pop(0))
        for unit in waiting:
            finish(*unit)
        step = CHUNK if causal else keys
        for source, saved, first, to in (
            (grads_t, expo_ref, 2 * pair, dv_ref),
            (queries_t, s_scr, 0, dk_ref),
        ):
            for low in range(0, keys, step):
                start = low if causal else 0
                parts = [
                    dot(
                        source[head * SIZE : (head + 1) * SIZE, start:],
                        saved[first + head, start:, low : low + step],
                        1,
                        0,
                    )
                    for head in range(2)
                ]
                to[low : low + step, span] = jnp.concatenate(parts, 0).T.astype(BF16)
        after(pair)


def parts_of(rows):
    return [slice(at, at + CHUNK) for at in range(0, rows, CHUNK)]


def wide_scale(scale):
    return jnp.broadcast_to(scale, (scale.shape[0], 128))


def self_forward_kernel(
    length_ref, x_ref, wq_ref, wk_ref, wv_ref, bq_ref, bv_ref,
    q_ref, k_ref, v_ref, ctx_ref, expo_ref, inverse_ref,
):
    scale = jnp.asarray(SIZE**-0.5, BF16)
    for span in parts_of(x_ref.shape[0]):
        rows = x_ref[span]
        q_ref[span] = (dot(rows, wq_ref[...], 1, 0) + bq_ref[...]).astype(BF16) * scale
        k_ref[span] = dot(rows, wk_ref[...], 1, 0).astype(BF16)
        v_ref[span] = (dot(rows, wv_ref[...], 1, 0) + bv_ref[...]).astype(BF16)
    attend_forward(
        True, 2, q_ref, k_ref, v_ref, length_ref[0], ctx_ref, expo_ref, inverse_ref
    )


def anywhere():
    return pl.BlockSpec(memory_space=pl.ANY)


def scalar():
    return pl.BlockSpec(memory_space=pltpu.SMEM)


def attend_out(rows, keys, width):
    group = GROUP * SIZE
    heads = width // SIZE
    specs = (
        [columns(rows, group)]
        + [columns(keys, group)] * 2
        + [columns(rows, group)]
        + [pl.BlockSpec((GROUP, rows, keys), lambda i: (i, 0, 0)), columns(rows, group)]
    )
    shapes = (
        [jax.ShapeDtypeStruct((rows, width), BF16)]
        + [jax.ShapeDtypeStruct((keys, width), BF16)] * 2
        + [jax.ShapeDtypeStruct((rows, width), BF16)]
        + [
            jax.ShapeDtypeStruct((heads, rows, keys), BF16),
            jax.ShapeDtypeStruct((rows, width), F32),
        ]
    )
    return specs, shapes


def self_forward(length, values, weights, q_bias, v_bias):
    rows, width = values.shape
    group = GROUP * SIZE
    per = width // group
    specs, shapes = attend_out(rows, rows, width)
    return call(
        self_forward_kernel,
        "self_forward",
        (per,),
        [scalar(), whole((rows, width))]
        + [columns(width, group, at * per) for at in range(3)]
        + [columns(1, group)] * 2,
        specs,
        shapes,
        6 * rows * width * width + 4 * rows * rows * width,
        18 * rows * width + 6 * width * width + 32 * rows * rows,
        rows * rows * HEADS,
    )(length, values, weights, weights, weights, q_bias, v_bias)


def cross_forward_kernel(
    length_ref, x_ref, sctx_ref, states_ref, wo_ref, wq_ref, wk_ref, wv_ref,
    bo_ref, gain_ref, shift_ref, bq_ref, bv_ref,
    normal_ref, scale_ref, q_ref, k_ref, v_ref, ctx_ref, expo_ref, inverse_ref, hidden_scr,
):
    spans = parts_of(x_ref.shape[0])

    @pl.when(pl.program_id(0) == 0)
    def _():
        sums = [
            x_ref[span].astype(F32) + dot(sctx_ref[span], wo_ref[...], 1, 0) + bo_ref[...]
            for span in spans
        ]
        for span, total in zip(spans, sums):
            normal, scale = normalize(total)
            normal_ref[span] = normal
            scale_ref[span] = wide_scale(scale)
            hidden_scr[span] = (normal * gain_ref[...] + shift_ref[...]).astype(BF16)

    size = jnp.asarray(SIZE**-0.5, BF16)
    for span in parts_of(states_ref.shape[0]):
        rows = states_ref[span]
        k_ref[span] = dot(rows, wk_ref[...], 1, 0).astype(BF16)
        v_ref[span] = (dot(rows, wv_ref[...], 1, 0) + bv_ref[...]).astype(BF16)
    for span in spans:
        q_ref[span] = (dot(hidden_scr[span], wq_ref[...], 1, 0) + bq_ref[...]).astype(BF16) * size
    attend_forward(
        False, 2, q_ref, k_ref, v_ref, length_ref[0], ctx_ref, expo_ref, inverse_ref
    )


def cross_forward(length, values, context, states, weights, at, vectors):
    rows, width = values.shape
    keys = states.shape[0]
    group = GROUP * SIZE
    per = width // group
    specs, shapes = attend_out(rows, keys, width)
    return call(
        cross_forward_kernel,
        "cross_forward",
        (per,),
        [scalar(), whole((rows, width)), whole((rows, width)), whole((keys, width))]
        + [square(width, at[0])]
        + [columns(width, group, first * per) for first in at[1:]]
        + [whole((1, width))] * 3
        + [columns(1, group)] * 2,
        [whole((rows, width)), whole((rows, 128))] + specs,
        [jax.ShapeDtypeStruct((rows, width), F32), jax.ShapeDtypeStruct((rows, 128), F32)] + shapes,
        8 * rows * width * width + 4 * rows * keys * width,
        26 * rows * width + 8 * width * width + 32 * rows * keys,
        rows * keys * HEADS,
        [pltpu.VMEM((rows, width), BF16)],
    )(length, values, context, states, weights, weights, weights, weights, *vectors)


def second_block(w_ref, held, width):
    pieces = []
    for at in range(0, w_ref.shape[0], held):
        for group in range(w_ref.shape[1] // width):
            pieces.append(w_ref[at : at + held, group * width : (group + 1) * width])
    return jnp.concatenate(pieces, 0)


def middle_kernel(
    held, factor, ramp_ref, n1_ref, ctx_ref, wo_ref, w1_ref, w2_ref, b1_ref, go_ref, down_ref, up_ref,
    bo_ref, gain1_ref, shift1_ref, gain2_ref, shift2_ref, gain3_ref, shift3_ref, b2_ref,
    gain_a_ref, shift_a_ref, up_b_ref, down_b_ref,
    normal_out, scale_ref, slope_ref, out_out, gffn_out, rest_out, grads_out,
    hidden_scr, act_scr, branch_scr, lower_scr,
    normal_ref, out_ref, gffn_ref, rest_ref, grads_ref, go_scr, down_scr, up_scr, in_sems, out_sems,
):
    rows, width = ctx_ref.shape
    units = down_ref.shape[1]
    spans = parts_of(rows)
    step = pl.program_id(0)
    first_load, *loads = moved(
        [(n1_ref, normal_ref), (go_ref, go_scr), (down_ref, down_scr), (up_ref, up_scr)], in_sems
    )
    keep = pltpu.make_async_copy(normal_ref, normal_out, out_sems.at[0])

    @pl.when(step == 0)
    def _():
        first_load.start()
        start_all(loads)
        sums = [dot(ctx_ref[span], wo_ref[...], 1, 0) + bo_ref[...] for span in spans]
        first_load.wait()
        for span, total in zip(spans, sums):
            normal, scale = normalize(
                total + (normal_ref[span] * gain1_ref[...] + shift1_ref[...])
            )
            normal_ref[span] = normal
            scale_ref[span] = wide_scale(scale)
            hidden = normal * gain2_ref[...] + shift2_ref[...]
            hidden_scr[span] = hidden.astype(BF16)
            rest_ref[span] = hidden + b2_ref[...]
        keep.start()

    second = second_block(w2_ref, held, width)

    def first(span):
        return dot(hidden_scr[span], w1_ref[...], 1, 0) + b1_ref[...]

    def finish(span, pre):
        phi = 0.5 + 0.5 * lax.erf(pre * (0.5**0.5))
        act = (pre * phi).astype(BF16)
        slope = phi + pre * (jnp.exp(pre * pre * -0.5) * (1.0 / math.sqrt(2.0 * math.pi)))
        slope_ref[span] = slope.astype(BF16)
        rest_ref[span] += dot(act, second, 1, 0)

    waiting = None
    for span in spans:
        pre = first(span)
        if waiting is not None:
            finish(*waiting)
        waiting = (span, pre)
    finish(*waiting)

    @pl.when(step == pl.num_programs(0) - 1)
    def _():
        ramp = ramp_ref[0]
        wait_all(loads)
        outs = moved(
            [(normal_ref, normal_out), (out_ref, out_out), (gffn_ref, gffn_out), (grads_ref, grads_out)],
            out_sems,
        )
        sums = [jnp.zeros((1, width), F32)] * 3 + [jnp.zeros((1, units), F32)]
        kept = []
        for span in spans:
            hidden = normal_ref[span] * gain2_ref[...] + shift2_ref[...]
            mean_a = jnp.mean(hidden, -1, keepdims=True)
            normal_a, scale_a = normalize(hidden)
            hidden_scr[span] = (normal_a * gain_a_ref[...] + shift_a_ref[...]).astype(BF16)
            kept.append([scale_a, mean_a])
        for span, keep in zip(spans, kept):
            lower = dot(hidden_scr[span], down_scr[...], 1, 0) + down_b_ref[...]
            gate = 1.0 / (1.0 + jnp.exp(-lower))
            act_scr[span] = (lower * gate).astype(BF16)
            keep.append(gate * (1.0 + lower * (1.0 - gate)))
        for span, keep in zip(spans, kept):
            branch = dot(act_scr[span], up_scr[...], 1, 0) + up_b_ref[...]
            normal, scale = normalize(rest_ref[span] + ramp * branch)
            out_ref[span] = (normal * gain3_ref[...] + shift3_ref[...]).astype(BF16)
            grad = normalize_back(normal, scale, gain3_ref[...] * go_scr[span].astype(F32))
            gffn_ref[span] = grad.astype(BF16)
            rest_ref[span] = grad
            grad_branch = (ramp * grad).astype(BF16)
            branch_scr[span] = grad_branch
            sums[0] = sums[0] + jnp.sum(grad_branch.astype(F32), 0, keepdims=True)
        start_all(outs[1:3])
        for span, keep in zip(spans, kept):
            grad_act = dot(branch_scr[span], up_scr[...], 1, 1).astype(BF16).astype(F32)
            grad_lower = (keep[2] * grad_act).astype(BF16)
            lower_scr[span] = grad_lower
            sums[3] = sums[3] + jnp.sum(grad_lower.astype(F32), 0, keepdims=True)
        for at, (span, keep) in enumerate(zip(spans, kept)):
            grad_adapt = dot(lower_scr[span], down_scr[...], 1, 1)
            hidden = normal_ref[span] * gain2_ref[...] + shift2_ref[...]
            normal_a = (hidden - keep[1]) * keep[0]
            rest_ref[span] += normalize_back(normal_a, keep[0], gain_a_ref[...] * grad_adapt)
            outs.append(
                pltpu.make_async_copy(rest_ref.at[span], rest_out.at[span], out_sems.at[4 + at])
            )
            outs[-1].start()
            sums[1] = sums[1] + jnp.sum(grad_adapt * normal_a, 0, keepdims=True)
            sums[2] = sums[2] + jnp.sum(grad_adapt, 0, keepdims=True)
        kind = grads_ref.dtype
        grads_ref[0:units] = (dot(act_scr[...], branch_scr[...], 0, 0) * factor).astype(kind)
        for at in range(0, width, units):
            grads_ref[units : 2 * units, at : at + units] = (
                dot(hidden_scr[:, at : at + units], lower_scr[...], 0, 0) * factor
            ).astype(kind)
        sums[3] = jnp.concatenate([sums[3], jnp.zeros((1, width - units), F32)], 1)
        small = jnp.concatenate([*sums, jnp.zeros((grads_ref.shape[0] - 2 * units - 4, width), F32)], 0)
        grads_ref[2 * units :] = (small * factor).astype(kind)
        outs[3].start()
        wait_all(outs)


def middle(
    ramp, normal1, context, attn_w, wo_at, ffn_w, w2_at, w1_at, first_bias, grad_out, down, up, vectors,
    down_bias, held, extra, factor,
):
    rows, width = normal1.shape
    wide = first_bias.shape[1]
    units = down.shape[1]
    step = 512
    groups = wide // width
    block = whole((rows, width))
    return call(
        functools.partial(middle_kernel, held, factor),
        "middle",
        (wide // step,),
        [
            scalar(),
            anywhere(),
            block,
            square(width, wo_at),
            columns(width, step, w1_at // step),
            pl.BlockSpec((step // groups, wide), lambda i: (i, w2_at // wide)),
            columns(1, step),
            anywhere(),
            anywhere(),
            anywhere(),
        ]
        + [whole((1, width))] * 11
        + [whole((1, units))],
        [anywhere(), whole((rows, 128)), columns(rows, step)] + [anywhere()] * 4,
        [
            jax.ShapeDtypeStruct((rows, width), F32),
            jax.ShapeDtypeStruct((rows, 128), F32),
            jax.ShapeDtypeStruct((rows, wide), BF16),
            jax.ShapeDtypeStruct((rows, width), BF16),
            jax.ShapeDtypeStruct((rows, width), BF16),
            jax.ShapeDtypeStruct((rows, width), F32),
            jax.ShapeDtypeStruct((2 * units + extra, width), BF16),
        ],
        4 * rows * width * wide + 2 * rows * width * width + 12 * rows * width * units,
        22 * rows * width + 4 * width * wide + 2 * rows * wide + 12 * width * units,
        2 * rows * wide + rows * units,
        [
            pltpu.VMEM((rows, width), BF16),
            pltpu.VMEM((rows, units), BF16),
            pltpu.VMEM((rows, width), BF16),
            pltpu.VMEM((rows, units), BF16),
            pltpu.VMEM((rows, width), F32),
            pltpu.VMEM((rows, width), BF16),
            pltpu.VMEM((rows, width), BF16),
            pltpu.VMEM((rows, width), F32),
            pltpu.VMEM((2 * units + extra, width), BF16),
            pltpu.VMEM((rows, width), BF16),
            pltpu.VMEM(down.shape, BF16),
            pltpu.VMEM(up.shape, BF16),
            pltpu.SemaphoreType.DMA((4,)),
            pltpu.SemaphoreType.DMA((4 + rows // CHUNK,)),
        ],
    )(
        ramp, normal1, context, attn_w, ffn_w, ffn_w, first_bias, grad_out, down, up, *vectors, down_bias
    )


def moved(pairs, sems):
    return [
        pltpu.make_async_copy(source, target, sems.at[at])
        for at, (source, target) in enumerate(pairs)
    ]


def start_all(copies):
    for copy in copies:
        copy.start()


def wait_all(copies):
    for copy in copies:
        copy.wait()


def norm_back_out(
    spans, grads, start_scr, normal_scr, scale_ref, gain_ref, low_scr, out_ref, low_ref, sems
):
    outs = []
    for at, span in enumerate(spans):
        grad = normalize_back(
            normal_scr[span], scale_ref[span, 0:1], gain_ref[...] * (grads[span] + start_scr[span])
        )
        start_scr[span] = grad
        low_scr[span] = grad.astype(BF16)
        outs += moved(
            [(start_scr.at[span], out_ref.at[span]), (low_scr.at[span], low_ref.at[span])],
            sems.at[pl.ds(2 * at, 2)],
        )
        start_all(outs[-2:])
    return outs


def ffn_backward_kernel(
    held, g_ref, w1_ref, w2_ref, slope_ref, start_ref, normal_ref, scale_ref, gain_ref,
    out_ref, low_ref, sum_scr, start_scr, normal_scr, low_scr, in_sems, out_sems,
):
    rows, width = g_ref.shape
    second = second_block(w2_ref, held, width)
    spans = parts_of(rows)
    step = pl.program_id(0)
    loads = moved([(start_ref, start_scr), (normal_ref, normal_scr)], in_sems)

    @pl.when(step == 0)
    def _():
        start_all(loads)
        sum_scr[...] = jnp.zeros_like(sum_scr)

    def finish(span, grad_act):
        grad_pre = (slope_ref[span].astype(F32) * grad_act).astype(BF16)
        sum_scr[span] += dot(grad_pre, w1_ref[...], 1, 1)

    waiting = None
    for span in spans:
        grad_act = dot(g_ref[span], second, 1, 1)
        if waiting is not None:
            finish(*waiting)
        waiting = (span, grad_act)
    finish(*waiting)

    @pl.when(step == pl.num_programs(0) - 1)
    def _():
        wait_all(loads)
        outs = norm_back_out(
            spans, sum_scr, start_scr, normal_scr, scale_ref, gain_ref, low_scr, out_ref, low_ref, out_sems
        )
        wait_all(outs)


def ffn_backward(grads, weights, w2_at, w1_at, slope, start, normal, scale, gain, held):
    rows, width = grads.shape
    wide = slope.shape[1]
    step = 512
    groups = wide // width
    return call(
        functools.partial(ffn_backward_kernel, held),
        "ffn_backward",
        (wide // step,),
        [
            whole((rows, width)),
            columns(width, step, w1_at // step),
            pl.BlockSpec((step // groups, wide), lambda i: (i, w2_at // wide)),
            columns(rows, step),
            anywhere(),
            anywhere(),
            whole((rows, 128)),
            whole((1, width)),
        ],
        [anywhere()] * 2,
        [jax.ShapeDtypeStruct((rows, width), F32), jax.ShapeDtypeStruct((rows, width), BF16)],
        4 * rows * width * wide,
        16 * rows * width + 4 * width * wide + 2 * rows * wide,
        0,
        [pltpu.VMEM((rows, width), F32)] * 3
        + [
            pltpu.VMEM((rows, width), BF16),
            pltpu.SemaphoreType.DMA((2,)),
            pltpu.SemaphoreType.DMA((2 * rows // CHUNK,)),
        ],
    )(grads, weights, weights, slope, start, normal, scale, gain)


def expo_loads(expo_ref, expo_scr, sems):
    step, count = pl.program_id(0), pl.num_programs(0)

    def load(group, pair):
        heads = pl.ds(group * GROUP + 2 * pair, 2)
        return pltpu.make_async_copy(
            expo_ref.at[heads], expo_scr.at[pl.ds(2 * pair, 2)], sems.at[pair]
        )

    def begin():
        for pair in range(GROUP // 2):
            load(0, pair).start()

    def before(pair):
        load(step, pair).wait()

    def after(pair):
        @pl.when(step < count - 1)
        def _():
            load(step + 1, pair).start()

    return begin, before, after


def cross_backward_kernel(
    g_ref, low_ref, normal_ref, scale_ref, gain_ref, wo_ref, wq_ref, wk_ref, wv_ref,
    q_ref, k_ref, v_ref, ctx_ref, expo_ref, inverse_ref,
    states_ref, sum_ref, sum_low_ref,
    total_scr, states_scr, start_scr, normal_scr, low_scr, grad_scr, dq_scr, dk_scr, dv_scr, s_scr, expo_scr,
    in_sems, out_sems, expo_sems,
):
    spans = parts_of(low_ref.shape[0])
    step = pl.program_id(0)
    loads = moved([(g_ref, start_scr), (normal_ref, normal_scr)], in_sems)
    begin, before, after = expo_loads(expo_ref, expo_scr, expo_sems)

    @pl.when(step == 0)
    def _():
        begin()
        start_all(loads)
        total_scr[...] = jnp.zeros_like(total_scr)
        states_scr[...] = jnp.zeros_like(states_scr)

    for span in spans:
        grad_scr[span] = dot(low_ref[span], wo_ref[...], 1, 1).astype(BF16)
    attend_backward(
        False, q_ref, k_ref, v_ref, ctx_ref, grad_scr, expo_scr, inverse_ref, dq_scr, dk_scr, dv_scr, s_scr,
        before, after,
    )
    for span in parts_of(states_ref.shape[0]):
        states_scr[span] += dot(dk_scr[span], wk_ref[...], 1, 1) + dot(dv_scr[span], wv_ref[...], 1, 1)
    for span in spans:
        total_scr[span] += dot(dq_scr[span], wq_ref[...], 1, 1)

    @pl.when(step == pl.num_programs(0) - 1)
    def _():
        states = pltpu.make_async_copy(states_scr, states_ref, out_sems.at[2 * len(spans)])
        states.start()
        wait_all(loads)
        outs = norm_back_out(
            spans, total_scr, start_scr, normal_scr, scale_ref, gain_ref, low_scr, sum_ref, sum_low_ref,
            out_sems,
        )
        wait_all([states, *outs])


def self_backward_kernel(
    g_ref, low_ref, wo_ref, wq_ref, wk_ref, wv_ref, q_ref, k_ref, v_ref, ctx_ref, expo_ref, inverse_ref,
    out_ref, total_scr, start_scr, grad_scr, dq_scr, dk_scr, dv_scr, s_scr, expo_scr,
    in_sems, out_sems, expo_sems,
):
    spans = parts_of(low_ref.shape[0])
    step = pl.program_id(0)
    load = pltpu.make_async_copy(g_ref, start_scr, in_sems.at[0])
    begin, before, after = expo_loads(expo_ref, expo_scr, expo_sems)

    @pl.when(step == 0)
    def _():
        begin()
        load.start()
        total_scr[...] = jnp.zeros_like(total_scr)

    for span in spans:
        grad_scr[span] = dot(low_ref[span], wo_ref[...], 1, 1).astype(BF16)
    attend_backward(
        True, q_ref, k_ref, v_ref, ctx_ref, grad_scr, expo_scr, inverse_ref, dq_scr, dk_scr, dv_scr, s_scr,
        before, after,
    )

    def back(span):
        return (
            dot(dq_scr[span], wq_ref[...], 1, 1)
            + dot(dk_scr[span], wk_ref[...], 1, 1)
            + dot(dv_scr[span], wv_ref[...], 1, 1)
        )

    last = step == pl.num_programs(0) - 1

    @pl.when(jnp.logical_not(last))
    def _():
        for span in spans:
            total_scr[span] += back(span)

    @pl.when(last)
    def _():
        load.wait()
        outs = []
        for at, span in enumerate(spans):
            total_scr[span] += start_scr[span] + back(span)
            outs.append(
                pltpu.make_async_copy(total_scr.at[span], out_ref.at[span], out_sems.at[at])
            )
            outs[-1].start()
        wait_all(outs)


def attend_in(rows, keys, width, at):
    group = GROUP * SIZE
    per = width // group
    weights = [pl.BlockSpec((group, width), lambda i: (i, at[0]))] + [
        columns(width, group, first * per) for first in at[1:]
    ]
    return weights + [
        columns(rows, group),
        columns(keys, group),
        columns(keys, group),
        columns(rows, group),
        anywhere(),
        columns(rows, group),
    ]


def attend_scratch(rows, keys):
    group = GROUP * SIZE
    return [
        pltpu.VMEM((rows, group), BF16),
        pltpu.VMEM((rows, group), BF16),
        pltpu.VMEM((keys, group), BF16),
        pltpu.VMEM((keys, group), BF16),
        pltpu.VMEM((2, rows, keys), BF16),
        pltpu.VMEM((GROUP, rows, keys), BF16),
        pltpu.SemaphoreType.DMA((2,)),
        pltpu.SemaphoreType.DMA((2 * rows // CHUNK + 1,)),
        pltpu.SemaphoreType.DMA((GROUP // 2,)),
    ]


def cross_backward(grads, low, normal, scale, gain, weights, at, saved):
    rows, width = grads.shape
    keys = saved[1].shape[0]
    return call(
        cross_backward_kernel,
        "cross_backward",
        (width // (GROUP * SIZE),),
        [anywhere(), whole((rows, width)), anywhere(), whole((rows, 128)), whole((1, width))]
        + attend_in(rows, keys, width, at),
        [anywhere()] * 3,
        [
            jax.ShapeDtypeStruct((keys, width), F32),
            jax.ShapeDtypeStruct((rows, width), F32),
            jax.ShapeDtypeStruct((rows, width), BF16),
        ],
        8 * rows * width * width + 8 * rows * keys * width,
        32 * rows * width + 8 * width * width + 32 * rows * keys,
        0,
        [
            pltpu.VMEM((rows, width), F32),
            pltpu.VMEM((keys, width), F32),
            pltpu.VMEM((rows, width), F32),
            pltpu.VMEM((rows, width), F32),
            pltpu.VMEM((rows, width), BF16),
        ]
        + attend_scratch(rows, keys),
    )(grads, low, normal, scale, gain, weights, weights, weights, weights, *saved)


def self_backward(grads, low, weights, at, saved):
    rows, width = grads.shape
    return call(
        self_backward_kernel,
        "self_backward",
        (width // (GROUP * SIZE),),
        [anywhere(), whole((rows, width))] + attend_in(rows, rows, width, at),
        anywhere(),
        jax.ShapeDtypeStruct((rows, width), F32),
        8 * rows * width * width + 4 * rows * rows * width,
        20 * rows * width + 8 * width * width + 32 * rows * rows,
        0,
        [pltpu.VMEM((rows, width), F32)] * 2 + attend_scratch(rows, rows),
    )(grads, low, weights, weights, weights, weights, *saved)


def unpack_kernel(all_ref, down_ref, down_b_ref, up_ref, up_b_ref, gain_ref, shift_ref):
    width, units = down_ref.shape
    up_ref[...] = all_ref[0:units].astype(F32)
    for at in range(0, width, units):
        down_ref[at : at + units] = all_ref[units : 2 * units, at : at + units].astype(F32)
    last = 2 * units
    small = all_ref[last : last + 16].astype(F32)
    up_b_ref[...] = small[0:1]
    gain_ref[...] = small[1:2]
    shift_ref[...] = small[2:3]
    down_b_ref[...] = small[3:4, 0:units]


def unpack(grads, down_shape):
    width, units = down_shape
    shapes = [(width, units), (1, units), (units, width)] + [(1, width)] * 3
    return call(
        unpack_kernel,
        "unpack",
        (),
        [whole(grads.shape)],
        [whole(shape) for shape in shapes],
        [jax.ShapeDtypeStruct(shape, F32) for shape in shapes],
        0,
        16 * width * units,
    )(grads)


def gather(shard):
    return lax.all_gather(shard, "fsdp", axis=0, tiled=True)


def sum_over(part, axis):
    count = lax.axis_size(axis)
    total, travel = part.astype(F32), part
    for _ in range(count - 1):
        travel = lax.ppermute(travel, axis, [(at, (at + 1) % count) for at in range(count)])
        total = total + travel.astype(F32)
    return total.astype(part.dtype)


def local(
    inputs,
    encoder,
    grad_out,
    target_mask,
    source_lengths,
    step,
    attn_in,
    attn_out,
    ffn_in,
    ffn_in_bias,
    ffn_out,
    ffn_out_bias,
    attn_bias,
    norm_gain,
    norm_shift,
    adapter_down,
    adapter_down_bias,
    adapter_up,
    adapter_up_bias,
    adapter_gain,
    adapter_shift,
):
    sequences, row_count, width = inputs.shape
    held = attn_in.shape[0]
    groups = ffn_out.shape[0] // held
    wide = ffn_in.shape[1]
    pad = jnp.zeros((held, 128), BF16)
    attn_w = gather(jnp.concatenate([attn_in, attn_out, pad], 1))
    ffn_w = jnp.concatenate(
        [ffn_out[at * held : (at + 1) * held] for at in range(groups)] + [ffn_in, pad], 1
    )
    ffn_w = gather(ffn_w)
    w1_at, w2_at = wide, 0
    self_at, cross_at = (6, 0, 1, 2), (7, 3, 4, 5)

    ramp = (4.0 * step.astype(F32) / RAMP).reshape(1)
    bias = [attn_bias[at : at + 1] for at in range(6)]
    gain = [norm_gain[at : at + 1] for at in range(3)]
    shift = [norm_shift[at : at + 1] for at in range(3)]
    tokens, states = inputs.reshape(-1, width), encoder.reshape(-1, width)
    target_length = jnp.sum((target_mask > 0).astype(jnp.int32)).reshape(1)

    *self_saved, self_ctx, self_expo, self_inverse = self_forward(
        target_length, tokens, attn_w, bias[0], bias[1]
    )
    normal1, scale1, *cross_saved, cross_ctx, cross_expo, cross_inverse = cross_forward(
        source_lengths,
        tokens,
        self_ctx,
        states,
        attn_w,
        self_at[:1] + cross_at[1:],
        (bias[2], gain[0], shift[0], bias[3], bias[4]),
    )
    token_total = sequences * row_count * lax.axis_size("fsdp") * lax.axis_size("dp")
    normal2, scale2, slope, layer_out, grad_ffn, grad_rest, adapter_grads = middle(
        ramp,
        normal1,
        cross_ctx,
        attn_w,
        cross_at[0],
        ffn_w,
        w2_at,
        w1_at,
        ffn_in_bias[None],
        grad_out.reshape(-1, width),
        adapter_down,
        adapter_up,
        (bias[5], gain[0], shift[0], gain[1], shift[1], gain[2], shift[2], ffn_out_bias[None])
        + (adapter_gain[None], adapter_shift[None], adapter_up_bias[None]),
        adapter_down_bias[None],
        held,
        16 * lax.axis_size("fsdp"),
        1.0 / math.sqrt(token_total),
    )
    scattered = lax.psum_scatter(adapter_grads, "fsdp", scatter_dimension=0, tiled=True)
    grad_sum2, low_sum2 = ffn_backward(
        grad_ffn, ffn_w, w2_at, w1_at, slope, grad_rest, normal2, scale2, gain[1], held
    )
    grad_encoder, grad_sum1, low_sum1 = cross_backward(
        grad_sum2,
        low_sum2,
        normal1,
        scale1,
        gain[0],
        attn_w,
        cross_at,
        (*cross_saved, cross_ctx, cross_expo, cross_inverse),
    )
    scattered, low_sum1 = lax.optimization_barrier((scattered, low_sum1))
    adapter_grads = gather(sum_over(scattered, "dp"))
    grad_input = self_backward(
        grad_sum1, low_sum1, attn_w, self_at, (*self_saved, self_ctx, self_expo, self_inverse)
    )
    grad_down, down_bias, grad_up, up_bias, grad_gain, grad_shift = unpack(
        adapter_grads, adapter_down.shape
    )
    return (
        layer_out.reshape(inputs.shape),
        grad_input.reshape(inputs.shape),
        grad_encoder.reshape(encoder.shape),
        grad_down,
        down_bias.reshape(-1),
        grad_up,
        up_bias.reshape(-1),
        grad_gain.reshape(-1),
        grad_shift.reshape(-1),
    )


def solution(mesh):
    batch = P(("fsdp", "dp"), None, None)
    split = P("fsdp", None)
    placed = (
        (batch,) * 3
        + (P(("fsdp", "dp"), None), P(("fsdp", "dp")), P())
        + (split, split, split, P(), split)
        + (P(),) * 10
    )
    return jax.shard_map(
        local,
        mesh=mesh,
        in_specs=placed,
        out_specs=(batch,) * 3 + (P(),) * 6,
        check_vma=False,
    )
```

time: 1170 us -> 389 us (0.33)
  matrix products: 605 us -> 0 us
  Pallas kernels: 0 us -> 239 us
  other arithmetic: 204 us -> 4.61 us
  local copies, waits for them, and re-layouts: 120 us -> 2.33 us
  blocking collectives: 39.3 us -> 0 us
  waiting for transfers between devices: 159 us -> 121 us
  loops' own time: 20 us -> 0 us
    dot_general x48 -> x0, matrix products: 605 us -> none  [the longest x8 146 us: block_scores(): jnp.einsum('sbhe,skhe->shbk', query_block, key_heads, preferred_element_t...]
    pallas_call x0 -> x7, Pallas kernels: none -> 239 us  [the longest x1 53.7 us: cross_backward(): call(cross_backward_kernel, 'cross_backward', (width // (GROUP * SIZE),),...]
    another operation x9 -> x0, other arithmetic: 98.8 us -> none
    reduce_sum x15 -> x1, other arithmetic: 80.3 us -> 0.64 us  [local(): target_length = jnp.sum((target_mask > 0).astype(jnp.int32)).reshape(1)]
    psum x1 -> x0, waiting for transfers between devices: 64.5 us -> none  [local(): lax.psum((grad_down, grad_down_bias, grad_up, grad_up_bias, grad_gain, gr...]
    unnamed x181 -> x19, local copies, waits for them, and re-layouts: 50.4 us -> 1.08 us
    psum x1 -> x0, blocking collectives: 39.3 us -> none  [local(): lax.psum((grad_down, grad_down_bias, grad_up, grad_up_bias, grad_gain, gr...]
    another operation x11 -> x0, local copies, waits for them, and re-layouts: 29.5 us -> none  [the longest x2 12.7 us: attend_forward(): split_heads(queries)]
  transfers between devices with their start and end apart: 5 -> 5, of which waited for: 2 -> 4; matrix products, arithmetic and copies ran while one was open for 33% -> 1% of each run, Pallas kernels for 0% -> 49%
where the time goes in v3:
time: 389 us; the launch traced here: 384 us
  Pallas kernels  239 us (61%)
  waiting for transfers between devices  121 us (31%)
  between operations  15.5 us (4%)
  other arithmetic  4.61 us (1%)
    all_gather x3, waiting for transfers between devices, gather(): return lax.all_gather(shard, 'fsdp', axis=0, tiled=True)  116 us
    pallas_call x1, Pallas kernels, cross_backward(): call(cross_backward_kernel, 'cross_backward', (width // (GROUP * SIZE),),...  53.7 us
    pallas_call x1, Pallas kernels, middle(): call(functools.partial(middle_kernel, held, factor), 'middle', (wide // s...  45.5 us
    pallas_call x1, Pallas kernels, cross_forward(): call(cross_forward_kernel, 'cross_forward', (per,), [scalar(), whole((row...  40.9 us
    pallas_call x1, Pallas kernels, self_backward(): call(self_backward_kernel, 'self_backward', (width // (GROUP * SIZE),), [...  38.4 us
    pallas_call x1, Pallas kernels, self_forward(): call(self_forward_kernel, 'self_forward', (per,), [scalar(), whole((rows,...  29.5 us
    pallas_call x1, Pallas kernels, ffn_backward(): call(functools.partial(ffn_backward_kernel, held), 'ffn_backward', (wide...  26.8 us
  transfers between devices with their start and end apart: 5, of which 4 were waited for; matrix products, arithmetic and copies ran while one was open for 1% of the time, Pallas kernels for 49%

profile of v3, /device:TPU:0, one launch (start us, length us, event | category | flops | bytes accessed | tf_op | source)
XLA Modules:
  0.0 384.2 jit_solution(4699880434534576959)
XLA Ops:
  7.2 0.0 copy-start.1
  7.2 0.0 all-gather.4.cloned.1.call-start
  7.2 0.0 copy-start.2
  7.3 2.3 pad_maximum_fusion
  9.6 0.0 copy-start.6
  9.6 0.0 copy-start.5
  9.6 0.0 copy-start.3
  9.6 0.0 copy-start.4
  9.6 0.0 all-gather.4.cloned.1.call-update
  9.6 0.0 all-gather.6.cloned.1.call-start
  9.7 0.0 copy-done.1
  9.8 0.0 copy-done.2
  9.8 0.0 copy-start
  9.8 1.0 copy-done
  10.8 0.0 all-gather.6.cloned.1.call-update
  10.8 0.0 reduce-scatter.2.cloned.1.call-start
  12.2 0.0 copy-done.6
  12.2 0.6 fusion
  12.8 0.0 copy-done.5
  12.8 0.6 fusion.3
  13.4 0.0 copy-done.3
  13.4 0.0 copy-done.4
  13.4 0.6 fusion.1
  14.1 89.2 %all-gather.4.cloned.1.call-done.wq_ref.wk_ref.wv_ref.wo_ref = bf16[1024,8320]{1,0:T(8,128)(2,1)} async-done(((bf16[64,8320]{1,0:T(8,128)(2,1)}), bf16[1024,8320]{1,0:T(8,128)(2,1)}) %all-gather.4.cloned.1.call-update) | async-done | bytes 17039376 | tf_op jit(solution)/shard_map/all_gather | solution.py:849
  103.2 29.5 %self_forward.1 = (bf16[1024,1024]{1,0:T(8,128)(2,1)}, bf16[1024,1024]{1,0:T(8,128)(2,1)}, bf16[1024,1024]{1,0:T(8,128)(2,1)}, bf16[1024,1024]{1,0:T(8,128)(2,1)...) custom-call(s32[1]{0:T(128)} %bitcast.1.length_ref, bf16[1024,1024]{1,0:T(8,128)(2,1)} %bitcast.17, ...), custom_call_target="tpu_custom_call" | custom-call | flops 10737418240 | bytes 58720256 | tf_op jit(solution)/shard_map/self_forward/pallas_call | solution.py:269
  132.8 40.9 %cross_forward.1 = (f32[1024,1024]{1,0:T(8,128)}, f32[1024,128]{1,0:T(8,128)}, bf16[1024,1024]{1,0:T(8,128)(2,1)}, bf16[1024,1024]{1,0:T(8,128)(2,1)}, bf16[1024...) custom-call(s32[1]{0:T(128)S(6)} %copy.35.length_ref, ...), custom_call_target="tpu_custom_call" | custom-call | flops 12884901888 | bytes 69206016 | tf_op jit(solution)/shard_map/cross_forward/pallas_call | solution.py:321
  173.7 22.1 %all-gather.6.cloned.1.call-done.w1_ref.w2_ref = bf16[1024,8320]{1,0:T(8,128)(2,1)} async-done(((bf16[64,8320]{1,0:T(8,128)(2,1)}), bf16[1024,8320]{1,0:T(8,128)(2,1)}) %all-gather.6.cloned.1.call-update) | async-done | bytes 17039376 | tf_op jit(solution)/shard_map/all_gather | solution.py:849
  195.7 45.5 %middle.1 = (f32[1024,1024]{1,0:T(8,128)}, f32[1024,128]{1,0:T(8,128)}, bf16[1024,4096]{1,0:T(8,128)(2,1)}, bf16[1024,1024]{1,0:T(8,128)(2,1)}, bf16[1024,1024]{...) custom-call(f32[1]{0:T(128)S(6)} %div.3.ramp_ref, f32[1024,1024]{1,0:T(8,128)} %get-tuple-element.44.n1_ref.normal_ref, ...), custom_call_target="tpu_custom_call" | custom-call | flops 25769803776 | bytes 54525952 | tf_op jit(solution)/shard_map/middle/pallas_call | solution.py:472
  241.3 0.0 reduce-scatter.2.cloned.1.call-update
  241.3 0.0 all-gather.8.cloned.1.call-start
  241.3 26.8 %ffn_backward.1 = (f32[1024,1024]{1,0:T(8,128)}, bf16[1024,1024]{1,0:T(8,128)(2,1)}) custom-call(bf16[1024,1024]{1,0:T(8,128)(2,1)} %get-tuple-element.47.g_ref, bf16[1024,8320]{1,0:T(8,128)(2,1)} %all-gather.6.cloned.1.call-done.w1_ref.w2_ref, bf16[1024,8320]{1,0:T(8,128)(2,1)} %all-gather.6.cloned.1.call-done.w1_ref.w2_ref, ...), custom_call_target="tpu_custom_call" | custom-call | flops 17179869184 | bytes 41943040 | tf_op jit(solution)/shard_map/ffn_backward/pallas_call | solution.py:600
  268.1 53.7 %cross_backward.1 = (f32[1024,1024]{1,0:T(8,128)}, f32[1024,1024]{1,0:T(8,128)}, bf16[1024,1024]{1,0:T(8,128)(2,1)}) custom-call(f32[1024,1024]{1,0:T(8,128)} %get-tuple-element.52.g_ref, bf16[1024,1024]{1,0:T(8,128)(2,1)} %get-tuple-element.53.low_ref, f32[1024,1024]{1,0:T(8,128)} %get-tuple-element.44.n1_ref.normal_ref, ...), custom_call_target="tpu_custom_call" | custom-call | flops 17179869184 | bytes 75497472 | tf_op jit(solution)/shard_map/cross_backward/pallas_call | solution.py:778
  321.9 0.0 reduce-scatter.2.cloned.1.call-done
  321.9 1.5 collective-permute-start
  323.4 5.1 %collective-permute-done = bf16[80,1024]{1,0:T(8,128)(2,1)S(1)} collective-permute-done((bf16[80,1024]{1,0:T(8,128)(2,1)}, bf16[80,1024]{1,0:T(8,128)(2,1)S(1)}, u32[]{:S(2)}, u32[]{:S(2)}) %collective-permute-start) | collective-permute-done | bytes 163872 | tf_op jit(solution)/shard_map/ppermute | solution.py:856
  328.5 1.6 add_convert_fusion
  330.2 0.0 all-gather.8.cloned.1.call-update
  330.2 38.4 %self_backward.1 = f32[1024,1024]{1,0:T(8,128)} custom-call(f32[1024,1024]{1,0:T(8,128)} %get-tuple-element.60.g_ref, bf16[1024,1024]{1,0:T(8,128)(2,1)} %get-tuple-element.63.low_ref, bf16[1024,8320]{1,0:T(8,128)(2,1)} %all-gather.4.cloned.1.call-done.wq_ref.wk_ref.wv_ref.wo_ref, ...), custom_call_target="tpu_custom_call" | custom-call | flops 12884901888 | bytes 62914560 | tf_op jit(solution)/shard_map/self_backward/pallas_call | solution.py:806
  368.6 5.0 %all-gather.8.cloned.1.call-done.all_ref = bf16[1280,1024]{1,0:T(8,128)(2,1)} async-done(((bf16[80,1024]{1,0:T(8,128)(2,1)}), bf16[1280,1024]{1,0:T(8,128)(2,1)}) %all-gather.8.cloned.1.call-update) | async-done | bytes 2621456 | tf_op jit(solution)/shard_map/all_gather | solution.py:849
  373.6 3.9 %unpack.1 = (f32[1024,512]{1,0:T(8,128)}, f32[1,512]{1,0:T(1,128)}, f32[512,1024]{1,0:T(8,128)}, f32[1,1024]{1,0:T(1,128)}, f32[1,1024]{1,0:T(1,128)}, /*index=5*/f32[1,1024]{1,0:T(1,128)}) custom-call(bf16[1280,1024]{1,0:T(8,128)(2,1)} %all-gather.8.cloned.1.call-done.all_ref), custom_call_target="tpu_custom_call" | custom-call | bytes 8388608 | tf_op jit(solution)/shard_map/unpack/pallas_call | solution.py:836
  (7 shorter events, 0.1 us)
Async XLA Ops:
  7.2 2.5 copy-start.1
  7.2 96.0 %all-gather.4.cloned.1.call-start = ((), (), s32[]{:S(2)}) async-start(), calls=%async_computation.1 | async-start | bytes 18104320 | tf_op jit(solution)/shard_map/all_gather | solution.py:849
  7.2 2.5 copy-start.2
  9.6 2.6 copy-start.6
  9.6 3.2 copy-start.5
  9.6 3.8 %copy-start.3 = (f32[6,1024]{1,0:T(8,128)S(1)}, f32[6,1024]{1,0:T(8,128)}, u32[]{:S(2)}) copy-start(f32[6,1024]{1,0:T(8,128)} %param.33) | copy-start | bytes 73732
  9.6 3.8 %copy-start.4 = (f32[3,1024]{1,0:T(4,128)S(1)}, f32[3,1024]{1,0:T(4,128)}, u32[]{:S(2)}) copy-start(f32[3,1024]{1,0:T(4,128)} %param.35) | copy-start | bytes 36868
  9.6 186.1 %all-gather.6.cloned.1.call-start = ((), (), s32[]{:S(2)}) async-start(), calls=%async_computation.2 | async-start | bytes 18104320 | tf_op jit(solution)/shard_map/all_gather | solution.py:849
  9.8 1.0 copy-start
  10.8 311.0 %reduce-scatter.2.cloned.1.call-start = ((), (), s32[]{:S(2)}) async-start(), calls=%async_computation.3 | async-start | bytes 2785280 | tf_op jit(solution)/shard_map/reduce_scatter | solution.py:937
  241.3 132.3 %all-gather.8.cloned.1.call-start = ((), (), s32[]{:S(2)}) async-start(), calls=%async_computation.4 | async-start | bytes 2785280 | tf_op jit(solution)/shard_map/all_gather | solution.py:849
  321.9 6.7 %collective-permute-start = (bf16[80,1024]{1,0:T(8,128)(2,1)}, bf16[80,1024]{1,0:T(8,128)(2,1)S(1)}, u32[]{:S(2)}, u32[]{:S(2)}) collective-permute-start(bf16[80,1024]{1,0:T(8,128)(2,1)} %reduce-scatter.2.cloned.1.call-done), channel_id=1, source_target_pairs={{0,1},{1,0},{2,3},{3,2},{4,5},{5,4},{6,7},{7,6},{8,9},{9,8},{10,11... | collective-permute-start | bytes 491528 | tf_op jit(solution)/shard_map/ppermute | solution.py:856
Sparse Core Ops, SparseCore 0:
  10.2 93.0 all-gather.3
  105.4 90.2 all-gather.5
  241.4 63.9 reduce-scatter.1
  330.3 43.1 all-gather.7

commit v4 on v3

--- a/solution.py
+++ b/solution.py
@@ -336,6 +336,9 @@
     )(length, values, context, states, weights, weights, weights, weights, *vectors)
 
 
+FFN_STEP = 1024
+
+
 def second_block(w_ref, held, width):
     pieces = []
     for at in range(0, w_ref.shape[0], held):
@@ -344,181 +347,219 @@
     return jnp.concatenate(pieces, 0)
 
 
+def in_turn(units, finish):
+    waiting = None
+    for first, span in units:
+        value = first(span)
+        if waiting is not None:
+            finish(*waiting)
+        waiting = (span, value)
+    finish(*waiting)
+
+
+def post_cross_kernel(
+    ramp_ref, n1_ref, ctx_ref, wo_ref, down_ref, up_ref,
+    bo_ref, gain1_ref, shift1_ref, gain2_ref, shift2_ref, b2_ref, gain_a_ref, shift_a_ref, up_b_ref,
+    down_b_ref,
+    normal_ref, hidden_ref, in_ref, act_ref, slope_ref, base_ref, stats_ref,
+):
+    spans = parts_of(n1_ref.shape[0])
+    sums = [dot(ctx_ref[span], wo_ref[...], 1, 0) + bo_ref[...] for span in spans]
+    for span, total in zip(spans, sums):
+        normal, scale = normalize(total + (n1_ref[span] * gain1_ref[...] + shift1_ref[...]))
+        normal_ref[span] = normal
+        hidden = normal * gain2_ref[...] + shift2_ref[...]
+        hidden_ref[span] = hidden.astype(BF16)
+        base_ref[span] = hidden + b2_ref[...] + ramp_ref[0] * up_b_ref[...]
+        mean_a = jnp.mean(hidden, -1, keepdims=True)
+        normal_a, scale_a = normalize(hidden)
+        in_ref[span] = (normal_a * gain_a_ref[...] + shift_a_ref[...]).astype(BF16)
+        for at, value in enumerate((scale, mean_a, scale_a)):
+            stats_ref[span, at * 128 : (at + 1) * 128] = wide_scale(value)
+    for span in spans:
+        lower = dot(in_ref[span], down_ref[...], 1, 0) + down_b_ref[...]
+        gate = 1.0 / (1.0 + jnp.exp(-lower))
+        act_ref[span] = (lower * gate).astype(BF16)
+        slope_ref[span] = gate * (1.0 + lower * (1.0 - gate))
+    for span in spans:
+        base_ref[span] += ramp_ref[0] * dot(act_ref[span], up_ref[...], 1, 0)
+
+
+def post_cross(ramp, normal1, context, weights, wo_at, down, up, vectors, down_bias):
+    rows, width = normal1.shape
+    units = down.shape[1]
+    step = 512
+
+    def block(wide):
+        return pl.BlockSpec((step, wide), lambda i: (i, 0))
+
+    return call(
+        post_cross_kernel,
+        "post_cross",
+        (rows // step,),
+        [scalar(), block(width), block(width), square(width, wo_at), whole(down.shape), whole(up.shape)]
+        + [whole((1, width))] * 9
+        + [whole((1, units))],
+        [block(width)] * 3 + [block(units)] * 2 + [block(width), block(384)],
+        [
+            jax.ShapeDtypeStruct((rows, width), F32),
+            jax.ShapeDtypeStruct((rows, width), BF16),
+            jax.ShapeDtypeStruct((rows, width), BF16),
+            jax.ShapeDtypeStruct((rows, units), BF16),
+            jax.ShapeDtypeStruct((rows, units), F32),
+            jax.ShapeDtypeStruct((rows, width), F32),
+            jax.ShapeDtypeStruct((rows, 384), F32),
+        ],
+        2 * rows * width * width + 4 * rows * width * units,
+        22 * rows * width,
+        rows * units,
+    )(ramp, normal1, context, weights, down, up, *vectors, down_bias)
+
+
 def middle_kernel(
-    held, factor, ramp_ref, n1_ref, ctx_ref, wo_ref, w1_ref, w2_ref, b1_ref, go_ref, down_ref, up_ref,
-    bo_ref, gain1_ref, shift1_ref, gain2_ref, shift2_ref, gain3_ref, shift3_ref, b2_ref,
-    gain_a_ref, shift_a_ref, up_b_ref, down_b_ref,
-    normal_out, scale_ref, slope_ref, out_out, gffn_out, rest_out, grads_out,
-    hidden_scr, act_scr, branch_scr, lower_scr,
-    normal_ref, out_ref, gffn_ref, rest_ref, grads_ref, go_scr, down_scr, up_scr, in_sems, out_sems,
+    held, factor, ramp_ref, hidden_ref, w1_ref, w2_ref, b1_ref, stats_ref,
+    gain2_ref, shift2_ref, gain3_ref, shift3_ref, gain_a_ref,
+    base_in, normal_in, in_in, act_in, slope_in, go_in, down_in, up_in,
+    slope_ref, out_out, gffn_out, rest_out, grads_out,
+    base_scr, normal_scr, in_scr, act_scr, slope_scr, go_scr, down_scr, up_scr,
+    total_scr, out_scr, gffn_scr, branch_scr, lower_scr, grads_scr, in_sems, out_sems,
 ):
-    rows, width = ctx_ref.shape
-    units = down_ref.shape[1]
+    rows, width = hidden_ref.shape
+    units = down_in.shape[1]
     spans = parts_of(rows)
     step = pl.program_id(0)
-    first_load, *loads = moved(
-        [(n1_ref, normal_ref), (go_ref, go_scr), (down_ref, down_scr), (up_ref, up_scr)], in_sems
-    )
-    keep = pltpu.make_async_copy(normal_ref, normal_out, out_sems.at[0])
+    loads = moved(
+        [
+            (base_in, base_scr), (normal_in, normal_scr), (in_in, in_scr), (act_in, act_scr),
+            (slope_in, slope_scr), (go_in, go_scr), (down_in, down_scr), (up_in, up_scr),
+        ],
+        in_sems,
+    )
 
     @pl.when(step == 0)
     def _():
-        first_load.start()
+        total_scr[...] = jnp.zeros_like(total_scr)
+
+    @pl.when(step == 1)
+    def _():
         start_all(loads)
-        sums = [dot(ctx_ref[span], wo_ref[...], 1, 0) + bo_ref[...] for span in spans]
-        first_load.wait()
-        for span, total in zip(spans, sums):
-            normal, scale = normalize(
-                total + (normal_ref[span] * gain1_ref[...] + shift1_ref[...])
-            )
-            normal_ref[span] = normal
-            scale_ref[span] = wide_scale(scale)
-            hidden = normal * gain2_ref[...] + shift2_ref[...]
-            hidden_scr[span] = hidden.astype(BF16)
-            rest_ref[span] = hidden + b2_ref[...]
-        keep.start()
-
-    second = second_block(w2_ref, held, width)
 
     def first(span):
-        return dot(hidden_scr[span], w1_ref[...], 1, 0) + b1_ref[...]
+        return dot(hidden_ref[span], w1_ref[...], 1, 0) + b1_ref[...]
 
     def finish(span, pre):
         phi = 0.5 + 0.5 * lax.erf(pre * (0.5**0.5))
         act = (pre * phi).astype(BF16)
         slope = phi + pre * (jnp.exp(pre * pre * -0.5) * (1.0 / math.sqrt(2.0 * math.pi)))
         slope_ref[span] = slope.astype(BF16)
-        rest_ref[span] += dot(act, second, 1, 0)
-
-    waiting = None
-    for span in spans:
-        pre = first(span)
-        if waiting is not None:
-            finish(*waiting)
-        waiting = (span, pre)
-    finish(*waiting)
+        total_scr[span] += dot(act, second_block(w2_ref, held, width), 1, 0)
+
+    in_turn([(first, span) for span in spans], finish)
 
     @pl.when(step == pl.num_programs(0) - 1)
     def _():
         ramp = ramp_ref[0]
         wait_all(loads)
-        outs = moved(
-            [(normal_ref, normal_out), (out_ref, out_out), (gffn_ref, gffn_out), (grads_ref, grads_out)],
-            out_sems,
-        )
+        outs = moved([(out_scr, out_out), (gffn_scr, gffn_out), (grads_scr, grads_out)], out_sems)
+        kind = grads_scr.dtype
         sums = [jnp.zeros((1, width), F32)] * 3 + [jnp.zeros((1, units), F32)]
-        kept = []
-        for span in spans:
-            hidden = normal_ref[span] * gain2_ref[...] + shift2_ref[...]
-            mean_a = jnp.mean(hidden, -1, keepdims=True)
-            normal_a, scale_a = normalize(hidden)
-            hidden_scr[span] = (normal_a * gain_a_ref[...] + shift_a_ref[...]).astype(BF16)
-            kept.append([scale_a, mean_a])
-        for span, keep in zip(spans, kept):
-            lower = dot(hidden_scr[span], down_scr[...], 1, 0) + down_b_ref[...]
-            gate = 1.0 / (1.0 + jnp.exp(-lower))
-            act_scr[span] = (lower * gate).astype(BF16)
-            keep.append(gate * (1.0 + lower * (1.0 - gate)))
-        for span, keep in zip(spans, kept):
-            branch = dot(act_scr[span], up_scr[...], 1, 0) + up_b_ref[...]
-            normal, scale = normalize(rest_ref[span] + ramp * branch)
-            out_ref[span] = (normal * gain3_ref[...] + shift3_ref[...]).astype(BF16)
+
+        def norm_three(span):
+            normal, scale = normalize(total_scr[span] + base_scr[span])
+            out_scr[span] = (normal * gain3_ref[...] + shift3_ref[...]).astype(BF16)
             grad = normalize_back(normal, scale, gain3_ref[...] * go_scr[span].astype(F32))
-            gffn_ref[span] = grad.astype(BF16)
-            rest_ref[span] = grad
+            gffn_scr[span] = grad.astype(BF16)
+            total_scr[span] = grad
             grad_branch = (ramp * grad).astype(BF16)
             branch_scr[span] = grad_branch
             sums[0] = sums[0] + jnp.sum(grad_branch.astype(F32), 0, keepdims=True)
-        start_all(outs[1:3])
-        for span, keep in zip(spans, kept):
+
+        def adapter_back(span):
             grad_act = dot(branch_scr[span], up_scr[...], 1, 1).astype(BF16).astype(F32)
-            grad_lower = (keep[2] * grad_act).astype(BF16)
+            grad_lower = (slope_scr[span] * grad_act).astype(BF16)
             lower_scr[span] = grad_lower
             sums[3] = sums[3] + jnp.sum(grad_lower.astype(F32), 0, keepdims=True)
-        for at, (span, keep) in enumerate(zip(spans, kept)):
+
+        for span in spans:
+            norm_three(span)
+            adapter_back(span)
+        start_all(outs[:2])
+        grads_scr[0:units, 0:width] = (dot(act_scr[...], branch_scr[...], 0, 0) * factor).astype(kind)
+        for at, span in enumerate(spans):
             grad_adapt = dot(lower_scr[span], down_scr[...], 1, 1)
-            hidden = normal_ref[span] * gain2_ref[...] + shift2_ref[...]
-            normal_a = (hidden - keep[1]) * keep[0]
-            rest_ref[span] += normalize_back(normal_a, keep[0], gain_a_ref[...] * grad_adapt)
+            hidden = normal_scr[span] * gain2_ref[...] + shift2_ref[...]
+            scale_a = stats_ref[span, 256:257]
+            normal_a = (hidden - stats_ref[span, 128:129]) * scale_a
+            total_scr[span] += normalize_back(normal_a, scale_a, gain_a_ref[...] * grad_adapt)
             outs.append(
-                pltpu.make_async_copy(rest_ref.at[span], rest_out.at[span], out_sems.at[4 + at])
+                pltpu.make_async_copy(total_scr.at[span], rest_out.at[span], out_sems.at[3 + at])
             )
             outs[-1].start()
             sums[1] = sums[1] + jnp.sum(grad_adapt * normal_a, 0, keepdims=True)
             sums[2] = sums[2] + jnp.sum(grad_adapt, 0, keepdims=True)
-        kind = grads_ref.dtype
-        grads_ref[0:units] = (dot(act_scr[...], branch_scr[...], 0, 0) * factor).astype(kind)
         for at in range(0, width, units):
-            grads_ref[units : 2 * units, at : at + units] = (
-                dot(hidden_scr[:, at : at + units], lower_scr[...], 0, 0) * factor
+            grads_scr[units : 2 * units, at : at + units] = (
+                dot(in_scr[:, at : at + units], lower_scr[...], 0, 0) * factor
             ).astype(kind)
-        sums[3] = jnp.concatenate([sums[3], jnp.zeros((1, width - units), F32)], 1)
-        small = jnp.concatenate([*sums, jnp.zeros((grads_ref.shape[0] - 2 * units - 4, width), F32)], 0)
-        grads_ref[2 * units :] = (small * factor).astype(kind)
-        outs[3].start()
+        vectors = []
+        for row in sums:
+            row = row * factor
+            vectors += [row[:, low : low + 128] for low in range(0, row.shape[1], 128)]
+        vectors += [jnp.zeros((1, 128), F32)] * (4 * width // 128 - len(vectors))
+        small = jnp.concatenate(vectors, 0).astype(kind)
+        lines = small.shape[0]
+        grads_scr[0:lines, width:] = small
+        grads_scr[lines:, width:] = jnp.zeros((2 * units - lines, 128), kind)
+        outs[2].start()
         wait_all(outs)
 
 
 def middle(
-    ramp, normal1, context, attn_w, wo_at, ffn_w, w2_at, w1_at, first_bias, grad_out, down, up, vectors,
-    down_bias, held, extra, factor,
+    ramp, hidden, ffn_w, w2_at, w1_at, first_bias, stats, vectors, late, held, factor
 ):
-    rows, width = normal1.shape
+    rows, width = hidden.shape
     wide = first_bias.shape[1]
+    down, up = late[-2:]
     units = down.shape[1]
-    step = 512
+    step = FFN_STEP
     groups = wide // width
-    block = whole((rows, width))
     return call(
         functools.partial(middle_kernel, held, factor),
         "middle",
         (wide // step,),
         [
             scalar(),
-            anywhere(),
-            block,
-            square(width, wo_at),
+            whole((rows, width)),
             columns(width, step, w1_at // step),
             pl.BlockSpec((step // groups, wide), lambda i: (i, w2_at // wide)),
             columns(1, step),
-            anywhere(),
-            anywhere(),
-            anywhere(),
+            whole((rows, 384)),
         ]
-        + [whole((1, width))] * 11
-        + [whole((1, units))],
-        [anywhere(), whole((rows, 128)), columns(rows, step)] + [anywhere()] * 4,
+        + [whole((1, width))] * 5
+        + [anywhere()] * len(late),
+        [columns(rows, step)] + [anywhere()] * 4,
         [
-            jax.ShapeDtypeStruct((rows, width), F32),
-            jax.ShapeDtypeStruct((rows, 128), F32),
             jax.ShapeDtypeStruct((rows, wide), BF16),
             jax.ShapeDtypeStruct((rows, width), BF16),
             jax.ShapeDtypeStruct((rows, width), BF16),
             jax.ShapeDtypeStruct((rows, width), F32),
-            jax.ShapeDtypeStruct((2 * units + extra, width), BF16),
+            jax.ShapeDtypeStruct((2 * units, width + 128), BF16),
         ],
-        4 * rows * width * wide + 2 * rows * width * width + 12 * rows * width * units,
+        4 * rows * width * wide + 8 * rows * width * units,
         22 * rows * width + 4 * width * wide + 2 * rows * wide + 12 * width * units,
-        2 * rows * wide + rows * units,
-        [
-            pltpu.VMEM((rows, width), BF16),
-            pltpu.VMEM((rows, units), BF16),
-            pltpu.VMEM((rows, width), BF16),
-            pltpu.VMEM((rows, units), BF16),
+        2 * rows * wide,
+        [pltpu.VMEM(value.shape, value.dtype) for value in late]
+        + [
             pltpu.VMEM((rows, width), F32),
             pltpu.VMEM((rows, width), BF16),
             pltpu.VMEM((rows, width), BF16),
-            pltpu.VMEM((rows, width), F32),
-            pltpu.VMEM((2 * units + extra, width), BF16),
             pltpu.VMEM((rows, width), BF16),
-            pltpu.VMEM(down.shape, BF16),
-            pltpu.VMEM(up.shape, BF16),
-            pltpu.SemaphoreType.DMA((4,)),
-            pltpu.SemaphoreType.DMA((4 + rows // CHUNK,)),
+            pltpu.VMEM((rows, units), BF16),
+            pltpu.VMEM((2 * units, width + 128), BF16),
+            pltpu.SemaphoreType.DMA((len(late),)),
+            pltpu.SemaphoreType.DMA((3 + rows // CHUNK,)),
         ],
-    )(
-        ramp, normal1, context, attn_w, ffn_w, ffn_w, first_bias, grad_out, down, up, *vectors, down_bias
-    )
+    )(ramp, hidden, ffn_w, ffn_w, first_bias, stats, *vectors, *late)
 
 
 def moved(pairs, sems):
@@ -539,21 +580,24 @@
 
 
 def norm_back_out(
-    spans, grads, start_scr, normal_scr, scale_ref, gain_ref, low_scr, out_ref, low_ref, sems
+    grads, start_scr, normal_scr, scale_ref, gain_ref, low_scr, out_ref, low_ref, sems
 ):
     outs = []
-    for at, span in enumerate(spans):
+
+    def back(span):
         grad = normalize_back(
             normal_scr[span], scale_ref[span, 0:1], gain_ref[...] * (grads[span] + start_scr[span])
         )
         start_scr[span] = grad
         low_scr[span] = grad.astype(BF16)
-        outs += moved(
+        copies = moved(
             [(start_scr.at[span], out_ref.at[span]), (low_scr.at[span], low_ref.at[span])],
-            sems.at[pl.ds(2 * at, 2)],
+            sems.at[pl.ds(len(outs), 2)],
         )
-        start_all(outs[-2:])
-    return outs
+        start_all(copies)
+        outs.extend(copies)
+
+    return outs, back
 
 
 def ffn_backward_kernel(
@@ -561,41 +605,54 @@
     out_ref, low_ref, sum_scr, start_scr, normal_scr, low_scr, in_sems, out_sems,
 ):
     rows, width = g_ref.shape
-    second = second_block(w2_ref, held, width)
     spans = parts_of(rows)
     step = pl.program_id(0)
     loads = moved([(start_ref, start_scr), (normal_ref, normal_scr)], in_sems)
 
     @pl.when(step == 0)
     def _():
+        sum_scr[...] = jnp.zeros_like(sum_scr)
+
+    @pl.when(step == 1)
+    def _():
         start_all(loads)
-        sum_scr[...] = jnp.zeros_like(sum_scr)
 
     def finish(span, grad_act):
         grad_pre = (slope_ref[span].astype(F32) * grad_act).astype(BF16)
         sum_scr[span] += dot(grad_pre, w1_ref[...], 1, 1)
 
-    waiting = None
-    for span in spans:
-        grad_act = dot(g_ref[span], second, 1, 1)
-        if waiting is not None:
-            finish(*waiting)
-        waiting = (span, grad_act)
-    finish(*waiting)
-
-    @pl.when(step == pl.num_programs(0) - 1)
+    def first(span):
+        return dot(g_ref[span], second_block(w2_ref, held, width), 1, 1)
+
+    last = step == pl.num_programs(0) - 1
+
+    @pl.when(jnp.logical_not(last))
+    def _():
+        in_turn([(first, span) for span in spans], finish)
+
+    @pl.when(last)
     def _():
         wait_all(loads)
-        outs = norm_back_out(
-            spans, sum_scr, start_scr, normal_scr, scale_ref, gain_ref, low_scr, out_ref, low_ref, out_sems
+        outs, back = norm_back_out(
+            sum_scr, start_scr, normal_scr, scale_ref, gain_ref, low_scr, out_ref, low_ref, out_sems
         )
+        held_act, done = None, []
+        for span in [*spans, None]:
+            grad_act = first(span) if span is not None else None
+            if held_act is not None:
+                finish(*held_act)
+                done.append(held_act[0])
+            held_act = (span, grad_act)
+            if len(done) > 1:
+                back(done.pop(0))
+        back(done.pop(0))
         wait_all(outs)
 
 
 def ffn_backward(grads, weights, w2_at, w1_at, slope, start, normal, scale, gain, held):
     rows, width = grads.shape
     wide = slope.shape[1]
-    step = 512
+    step = FFN_STEP
     groups = wide // width
     return call(
         functools.partial(ffn_backward_kernel, held),
@@ -608,7 +665,7 @@
             columns(rows, step),
             anywhere(),
             anywhere(),
-            whole((rows, 128)),
+            pl.BlockSpec((rows, 128), lambda i: (0, 0), pipeline_mode=pl.Buffered(1)),
             whole((1, width)),
         ],
         [anywhere()] * 2,
@@ -635,11 +692,15 @@
         )
 
     def begin():
-        for pair in range(GROUP // 2):
-            load(0, pair).start()
+        load(0, 0).start()
 
     def before(pair):
         load(step, pair).wait()
+
+        @pl.when(step == 0)
+        def _():
+            for later in range(pair + 1, min(pair + 2, GROUP // 2)):
+                load(0, later).start()
 
     def after(pair):
         @pl.when(step < count - 1)
@@ -664,9 +725,12 @@
     @pl.when(step == 0)
     def _():
         begin()
-        start_all(loads)
         total_scr[...] = jnp.zeros_like(total_scr)
         states_scr[...] = jnp.zeros_like(states_scr)
+
+    @pl.when(step == 1)
+    def _():
+        start_all(loads)
 
     for span in spans:
         grad_scr[span] = dot(low_ref[span], wo_ref[...], 1, 1).astype(BF16)
@@ -676,18 +740,30 @@
     )
     for span in parts_of(states_ref.shape[0]):
         states_scr[span] += dot(dk_scr[span], wk_ref[...], 1, 1) + dot(dv_scr[span], wv_ref[...], 1, 1)
-    for span in spans:
+
+    def add(span):
         total_scr[span] += dot(dq_scr[span], wq_ref[...], 1, 1)
 
-    @pl.when(step == pl.num_programs(0) - 1)
+    last = step == pl.num_programs(0) - 1
+
+    @pl.when(jnp.logical_not(last))
+    def _():
+        for span in spans:
+            add(span)
+
+    @pl.when(last)
     def _():
         states = pltpu.make_async_copy(states_scr, states_ref, out_sems.at[2 * len(spans)])
         states.start()
         wait_all(loads)
-        outs = norm_back_out(
-            spans, total_scr, start_scr, normal_scr, scale_ref, gain_ref, low_scr, sum_ref, sum_low_ref,
-            out_sems,
+        outs, back = norm_back_out(
+            total_scr, start_scr, normal_scr, scale_ref, gain_ref, low_scr, sum_ref, sum_low_ref, out_sems
         )
+        add(spans[0])
+        for before_span, span in zip(spans, spans[1:]):
+            add(span)
+            back(before_span)
+        back(spans[-1])
         wait_all([states, *outs])
 
 
@@ -704,8 +780,11 @@
     @pl.when(step == 0)
     def _():
         begin()
+        total_scr[...] = jnp.zeros_like(total_scr)
+
+    @pl.when(step == 1)
+    def _():
         load.start()
-        total_scr[...] = jnp.zeros_like(total_scr)
 
     for span in spans:
         grad_scr[span] = dot(low_ref[span], wo_ref[...], 1, 1).astype(BF16)
@@ -817,32 +896,57 @@
     )(grads, low, weights, weights, weights, weights, *saved)
 
 
-def unpack_kernel(all_ref, down_ref, down_b_ref, up_ref, up_b_ref, gain_ref, shift_ref):
-    width, units = down_ref.shape
-    up_ref[...] = all_ref[0:units].astype(F32)
-    for at in range(0, width, units):
-        down_ref[at : at + units] = all_ref[units : 2 * units, at : at + units].astype(F32)
-    last = 2 * units
-    small = all_ref[last : last + 16].astype(F32)
-    up_b_ref[...] = small[0:1]
-    gain_ref[...] = small[1:2]
-    shift_ref[...] = small[2:3]
-    down_b_ref[...] = small[3:4, 0:units]
+def unpack_kernel(up_in, down_in, small_in, down_ref, up_ref, up_b_ref, gain_ref, shift_ref, down_b_ref):
+    units = down_ref.shape[2]
+    up_ref[...] = up_in[...].astype(F32)
+    for at in range(down_ref.shape[0]):
+        down_ref[at] = down_in[:, at * units : (at + 1) * units].astype(F32)
+
+    @pl.when(pl.program_id(0) == 0)
+    def _():
+        small = small_in[...].astype(F32)
+        per = up_b_ref.shape[1] // 128
+        for at, ref in enumerate((up_b_ref, gain_ref, shift_ref, down_b_ref)):
+            for part in range(ref.shape[1] // 128):
+                row = at * per + part
+                ref[:, part * 128 : (part + 1) * 128] = small[row : row + 1]
 
 
 def unpack(grads, down_shape):
     width, units = down_shape
-    shapes = [(width, units), (1, units), (units, width)] + [(1, width)] * 3
-    return call(
+    halves = width // units
+    steps = 4
+    step = units // steps
+    small = 4 * width // 128
+
+    def fixed(shape):
+        return pl.BlockSpec(shape, lambda i: (0, 0))
+
+    down, *rest = call(
         unpack_kernel,
         "unpack",
-        (),
-        [whole(grads.shape)],
-        [whole(shape) for shape in shapes],
-        [jax.ShapeDtypeStruct(shape, F32) for shape in shapes],
+        (steps,),
+        [
+            pl.BlockSpec((step, width), lambda i: (i, 0)),
+            pl.BlockSpec((step, width), lambda i: (i + steps, 0)),
+            pl.BlockSpec((small, 128), lambda i: (0, width // 128)),
+        ],
+        [
+            pl.BlockSpec((halves, step, units), lambda i: (0, i, 0)),
+            pl.BlockSpec((step, width), lambda i: (i, 0)),
+        ]
+        + [fixed((1, width))] * 3
+        + [fixed((1, units))],
+        [
+            jax.ShapeDtypeStruct((halves, units, units), F32),
+            jax.ShapeDtypeStruct((units, width), F32),
+        ]
+        + [jax.ShapeDtypeStruct((1, width), F32)] * 3
+        + [jax.ShapeDtypeStruct((1, units), F32)],
         0,
         16 * width * units,
-    )(grads)
+    )(grads, grads, grads)
+    return down.reshape(down_shape), *rest
 
 
 def gather(shard):
@@ -914,29 +1018,35 @@
         (bias[2], gain[0], shift[0], bias[3], bias[4]),
     )
     token_total = sequences * row_count * lax.axis_size("fsdp") * lax.axis_size("dp")
-    normal2, scale2, slope, layer_out, grad_ffn, grad_rest, adapter_grads = middle(
+    normal2, hidden2, adapt_in, adapt_act, adapt_slope, base, stats = post_cross(
         ramp,
         normal1,
         cross_ctx,
         attn_w,
         cross_at[0],
+        adapter_down,
+        adapter_up,
+        (bias[5], gain[0], shift[0], gain[1], shift[1], ffn_out_bias[None])
+        + (adapter_gain[None], adapter_shift[None], adapter_up_bias[None]),
+        adapter_down_bias[None],
+    )
+    slope, layer_out, grad_ffn, grad_rest, adapter_grads = middle(
+        ramp,
+        hidden2,
         ffn_w,
         w2_at,
         w1_at,
         ffn_in_bias[None],
-        grad_out.reshape(-1, width),
-        adapter_down,
-        adapter_up,
-        (bias[5], gain[0], shift[0], gain[1], shift[1], gain[2], shift[2], ffn_out_bias[None])
-        + (adapter_gain[None], adapter_shift[None], adapter_up_bias[None]),
-        adapter_down_bias[None],
+        stats,
+        (gain[1], shift[1], gain[2], shift[2], adapter_gain[None]),
+        (base, normal2, adapt_in, adapt_act, adapt_slope)
+        + (grad_out.reshape(-1, width), adapter_down, adapter_up),
         held,
-        16 * lax.axis_size("fsdp"),
         1.0 / math.sqrt(token_total),
     )
     scattered = lax.psum_scatter(adapter_grads, "fsdp", scatter_dimension=0, tiled=True)
     grad_sum2, low_sum2 = ffn_backward(
-        grad_ffn, ffn_w, w2_at, w1_at, slope, grad_rest, normal2, scale2, gain[1], held
+        grad_ffn, ffn_w, w2_at, w1_at, slope, grad_rest, normal2, stats, gain[1], held
     )
     grad_encoder, grad_sum1, low_sum1 = cross_backward(
         grad_sum2,
@@ -953,7 +1063,7 @@
     grad_input = self_backward(
         grad_sum1, low_sum1, attn_w, self_at, (*self_saved, self_ctx, self_expo, self_inverse)
     )
-    grad_down, down_bias, grad_up, up_bias, grad_gain, grad_shift = unpack(
+    grad_down, grad_up, up_bias, grad_gain, grad_shift, down_bias = unpack(
         adapter_grads, adapter_down.shape
     )
     return (

time: 389 us -> 377 us (0.969)
  waiting for transfers between devices: 121 us -> 107 us
    all_gather x3, waiting for transfers between devices: 116 us -> 102 us  [gather(): return lax.all_gather(shard, 'fsdp', axis=0, tiled=True)]
    pallas_call x1 -> x2, Pallas kernels: 3.89 us -> 17.7 us  [the longest x1 13.5 us: post_cross(): call(post_cross_kernel, 'post_cross', (rows // step,), [scalar(), block(w...]
    pallas_call x1, Pallas kernels: 45.5 us -> 35.8 us  [middle(): call(functools.partial(middle_kernel, held, factor), 'middle', (wide // s...]
  transfers between devices with their start and end apart: 5 -> 5, of which waited for: 4 -> 4; matrix products, arithmetic and copies ran while one was open for 1% -> 1% of each run, Pallas kernels for 49% -> 54%
where the time goes in v4:
time: 377 us; the launch traced here: 372 us
  Pallas kernels  241 us (64%)
  waiting for transfers between devices  107 us (28%)
  between operations  15.7 us (4%)
  other arithmetic  4.58 us (1%)
    all_gather x3, waiting for transfers between devices, gather(): return lax.all_gather(shard, 'fsdp', axis=0, tiled=True)  102 us
    pallas_call x1, Pallas kernels, cross_backward(): call(cross_backward_kernel, 'cross_backward', (width // (GROUP * SIZE),),...  53.9 us
    pallas_call x1, Pallas kernels, cross_forward(): call(cross_forward_kernel, 'cross_forward', (per,), [scalar(), whole((row...  40.9 us
    pallas_call x1, Pallas kernels, self_backward(): call(self_backward_kernel, 'self_backward', (width // (GROUP * SIZE),), [...  38.4 us
    pallas_call x1, Pallas kernels, middle(): call(functools.partial(middle_kernel, held, factor), 'middle', (wide // s...  35.8 us
    pallas_call x1, Pallas kernels, self_forward(): call(self_forward_kernel, 'self_forward', (per,), [scalar(), whole((rows,...  29.5 us
    pallas_call x1, Pallas kernels, ffn_backward(): call(functools.partial(ffn_backward_kernel, held), 'ffn_backward', (wide...  24.6 us
    pallas_call x1, Pallas kernels, post_cross(): call(post_cross_kernel, 'post_cross', (rows // step,), [scalar(), block(w...  13.5 us
  transfers between devices with their start and end apart: 5, of which 4 were waited for; matrix products, arithmetic and copies ran while one was open for 1% of the time, Pallas kernels for 54%

profile of v4, /device:TPU:0, one launch (start us, length us, event | category | flops | bytes accessed | tf_op | source)
XLA Modules:
  0.0 371.7 jit_solution(9144234365023118517)
XLA Ops:
  7.2 0.0 copy-start.1
  7.2 0.0 all-gather.4.cloned.1.call-start
  7.2 0.0 copy-start.2
  7.3 2.3 pad_maximum_fusion
  9.6 0.0 copy-start.6
  9.6 0.0 copy-start.3
  9.6 0.0 copy-start.4
  9.6 0.0 copy-start.5
  9.6 0.0 all-gather.4.cloned.1.call-update
  9.6 0.0 all-gather.6.cloned.1.call-start
  9.7 0.0 copy-done.1
  9.8 0.0 copy-done.2
  9.8 0.0 copy-start
  9.8 1.0 copy-done
  10.8 0.0 all-gather.6.cloned.1.call-update
  10.8 0.0 reduce-scatter.2.cloned.1.call-start
  12.2 0.0 copy-done.6
  12.2 0.6 fusion
  12.8 0.0 copy-done.3
  12.8 0.6 fusion.1
  13.5 0.0 copy-done.4
  13.5 0.0 copy-done.5
  13.5 0.6 fusion.2
  14.1 89.1 %all-gather.4.cloned.1.call-done.wq_ref.wk_ref.wv_ref.wo_ref = bf16[1024,8320]{1,0:T(8,128)(2,1)} async-done(((bf16[64,8320]{1,0:T(8,128)(2,1)}), bf16[1024,8320]{1,0:T(8,128)(2,1)}) %all-gather.4.cloned.1.call-update) | async-done | bytes 17039376 | tf_op jit(solution)/shard_map/all_gather | solution.py:953
  103.2 29.5 %self_forward.1 = (bf16[1024,1024]{1,0:T(8,128)(2,1)}, bf16[1024,1024]{1,0:T(8,128)(2,1)}, bf16[1024,1024]{1,0:T(8,128)(2,1)}, bf16[1024,1024]{1,0:T(8,128)(2,1)...) custom-call(s32[1]{0:T(128)} %bitcast.1.length_ref, bf16[1024,1024]{1,0:T(8,128)(2,1)} %bitcast.18, ...), custom_call_target="tpu_custom_call" | custom-call | flops 10737418240 | bytes 58720256 | tf_op jit(solution)/shard_map/self_forward/pallas_call | solution.py:269
  132.8 40.9 %cross_forward.1 = (f32[1024,1024]{1,0:T(8,128)}, f32[1024,128]{1,0:T(8,128)}, bf16[1024,1024]{1,0:T(8,128)(2,1)}, bf16[1024,1024]{1,0:T(8,128)(2,1)}, bf16[1024...) custom-call(s32[1]{0:T(128)S(6)} %copy.35.length_ref, ...), custom_call_target="tpu_custom_call" | custom-call | flops 12884901888 | bytes 69206016 | tf_op jit(solution)/shard_map/cross_forward/pallas_call | solution.py:321
  173.7 13.5 %post_cross.1 = (f32[1024,1024]{1,0:T(8,128)}, bf16[1024,1024]{1,0:T(8,128)(2,1)}, bf16[1024,1024]{1,0:T(8,128)(2,1)}, bf16[1024,512]{1,0:T(8,128)(2,1)}, f32[10...) custom-call(f32[1]{0:T(128)S(6)} %div.3.ramp_ref, f32[1024,1024]{1,0:T(8,128)} %get-tuple-element.49.n1_ref.normal_ref, ...), custom_call_target="tpu_custom_call" | custom-call | flops 4294967296 | bytes 23068672 | tf_op jit(solution)/shard_map/post_cross/pallas_call | solution.py:396
  187.2 8.5 %all-gather.6.cloned.1.call-done.w1_ref.w2_ref = bf16[1024,8320]{1,0:T(8,128)(2,1)} async-done(((bf16[64,8320]{1,0:T(8,128)(2,1)}), bf16[1024,8320]{1,0:T(8,128)(2,1)}) %all-gather.6.cloned.1.call-update) | async-done | bytes 17039376 | tf_op jit(solution)/shard_map/all_gather | solution.py:953
  195.7 35.8 %middle.1 = (bf16[1024,4096]{1,0:T(8,128)(2,1)}, bf16[1024,1024]{1,0:T(8,128)(2,1)}, bf16[1024,1024]{1,0:T(8,128)(2,1)}, f32[1024,1024]{1,0:T(8,128)}, bf16[1024,1152]{1,0:T(8,128)(2,1)}) custom-call(f32[1]{0:T(128)S(6)} %div.3.ramp_ref, bf16[1024,1024]{1,0:T(8,128)(2,1)} %get-tuple-element.51.hidden_ref, ...), custom_call_target="tpu_custom_call" | custom-call | flops 21474836480 | bytes 54525952 | tf_op jit(solution)/shard_map/middle/pallas_call | solution.py:526
  231.5 0.0 reduce-scatter.2.cloned.1.call-update
  231.6 0.0 all-gather.8.cloned.1.call-start
  231.6 24.6 %ffn_backward.1 = (f32[1024,1024]{1,0:T(8,128)}, bf16[1024,1024]{1,0:T(8,128)(2,1)}) custom-call(bf16[1024,1024]{1,0:T(8,128)(2,1)} %get-tuple-element.59.g_ref, bf16[1024,8320]{1,0:T(8,128)(2,1)} %all-gather.6.cloned.1.call-done.w1_ref.w2_ref, bf16[1024,8320]{1,0:T(8,128)(2,1)} %all-gather.6.cloned.1.call-done.w1_ref.w2_ref, ...), custom_call_target="tpu_custom_call" | custom-call | flops 17179869184 | bytes 41943040 | tf_op jit(solution)/shard_map/ffn_backward/pallas_call | solution.py:657
  256.2 53.9 %cross_backward.1 = (f32[1024,1024]{1,0:T(8,128)}, f32[1024,1024]{1,0:T(8,128)}, bf16[1024,1024]{1,0:T(8,128)(2,1)}) custom-call(f32[1024,1024]{1,0:T(8,128)} %get-tuple-element.62.g_ref, bf16[1024,1024]{1,0:T(8,128)(2,1)} %get-tuple-element.63.low_ref, f32[1024,1024]{1,0:T(8,128)} %get-tuple-element.49.n1_ref.normal_ref, ...), custom_call_target="tpu_custom_call" | custom-call | flops 17179869184 | bytes 75497472 | tf_op jit(solution)/shard_map/cross_backward/pallas_call | solution.py:857
  310.1 0.0 reduce-scatter.2.cloned.1.call-done
  310.2 1.5 collective-permute-start
  311.7 4.7 %collective-permute-done = bf16[64,1152]{1,0:T(8,128)(2,1)S(1)} collective-permute-done((bf16[64,1152]{1,0:T(8,128)(2,1)}, bf16[64,1152]{1,0:T(8,128)(2,1)S(1)}, u32[]{:S(2)}, u32[]{:S(2)}) %collective-permute-start) | collective-permute-done | bytes 147488 | tf_op jit(solution)/shard_map/ppermute | solution.py:960
  316.4 1.6 add_convert_fusion
  318.0 0.0 all-gather.8.cloned.1.call-update
  318.0 38.4 %self_backward.1 = f32[1024,1024]{1,0:T(8,128)} custom-call(f32[1024,1024]{1,0:T(8,128)} %get-tuple-element.70.g_ref, bf16[1024,1024]{1,0:T(8,128)(2,1)} %get-tuple-element.73.low_ref, bf16[1024,8320]{1,0:T(8,128)(2,1)} %all-gather.4.cloned.1.call-done.wq_ref.wk_ref.wv_ref.wo_ref, ...), custom_call_target="tpu_custom_call" | custom-call | flops 12884901888 | bytes 62914560 | tf_op jit(solution)/shard_map/self_backward/pallas_call | solution.py:885
  356.4 4.1 %all-gather.8.cloned.1.call-done.up_in.down_in.small_in = bf16[1024,1152]{1,0:T(8,128)(2,1)} async-done(((bf16[64,1152]{1,0:T(8,128)(2,1)}), bf16[1024,1152]{1,0:T(8,128)(2,1)}) %all-gather.8.cloned.1.call-update) | async-done | bytes 2359312 | tf_op jit(solution)/shard_map/all_gather | solution.py:953
  360.6 4.2 %unpack.1 = (f32[2,512,512]{2,1,0:T(8,128)}, f32[512,1024]{1,0:T(8,128)}, f32[1,1024]{1,0:T(1,128)}, f32[1,1024]{1,0:T(1,128)}, f32[1,1024]{1,0:T(1,128)}, /*index=5*/f32[1,512]{1,0:T(1,128)}) custom-call(bf16[1024,1152]{1,0:T(8,128)(2,1)} %all-gather.8.cloned.1.call-done.up_in.down_in.small_in, ...), custom_call_target="tpu_custom_call" | custom-call | bytes 8388608 | tf_op jit(solution)/shard_map/unpack/pallas_call | solution.py:925
  (7 shorter events, 0.1 us)
Async XLA Ops:
  7.2 2.5 copy-start.1
  7.2 96.0 %all-gather.4.cloned.1.call-start = ((), (), s32[]{:S(2)}) async-start(), calls=%async_computation.1 | async-start | bytes 18104320 | tf_op jit(solution)/shard_map/all_gather | solution.py:953
  7.2 2.5 copy-start.2
  9.6 2.6 copy-start.6
  9.6 3.2 copy-start.3
  9.6 3.9 %copy-start.4 = (f32[3,1024]{1,0:T(4,128)S(1)}, f32[3,1024]{1,0:T(4,128)}, u32[]{:S(2)}) copy-start(f32[3,1024]{1,0:T(4,128)} %param.35) | copy-start | bytes 36868
  9.6 3.9 %copy-start.5 = (f32[3,1024]{1,0:T(4,128)S(1)}, f32[3,1024]{1,0:T(4,128)}, u32[]{:S(2)}) copy-start(f32[3,1024]{1,0:T(4,128)} %param.34) | copy-start | bytes 36868
  9.6 186.1 %all-gather.6.cloned.1.call-start = ((), (), s32[]{:S(2)}) async-start(), calls=%async_computation.2 | async-start | bytes 18104320 | tf_op jit(solution)/shard_map/all_gather | solution.py:953
  9.8 1.0 copy-start
  10.8 299.3 %reduce-scatter.2.cloned.1.call-start = ((), (), s32[]{:S(2)}) async-start(), calls=%async_computation.3 | async-start | bytes 2506752 | tf_op jit(solution)/shard_map/reduce_scatter | solution.py:1047
  231.6 129.0 %all-gather.8.cloned.1.call-start = ((), (), s32[]{:S(2)}) async-start(), calls=%async_computation.4 | async-start | bytes 2506752 | tf_op jit(solution)/shard_map/all_gather | solution.py:953
  310.2 6.3 %collective-permute-start = (bf16[64,1152]{1,0:T(8,128)(2,1)}, bf16[64,1152]{1,0:T(8,128)(2,1)S(1)}, u32[]{:S(2)}, u32[]{:S(2)}) collective-permute-start(bf16[64,1152]{1,0:T(8,128)(2,1)} %reduce-scatter.2.cloned.1.call-done), channel_id=1, source_target_pairs={{0,1},{1,0},{2,3},{3,2},{4,5},{5,4},{6,7},{7,6},{8,9},{9,8},{10,11... | collective-permute-start | bytes 442376 | tf_op jit(solution)/shard_map/ppermute | solution.py:960
Sparse Core Ops, SparseCore 0:
  10.2 93.0 all-gather.3
  105.4 90.2 all-gather.5
  231.7 62.9 reduce-scatter.1
  318.2 42.3 all-gather.7

commit v5 on v4

--- a/solution.py
+++ b/solution.py
@@ -143,33 +143,40 @@
     rows, keys = q_ref.shape[0], k_ref.shape[0]
     width = 2 * SIZE
     count = rows // CHUNK
+    pairs = q_ref.shape[1] // width
     lane = lax.broadcasted_iota(jnp.int32, (rows, width), 1)
     key_lane = lax.broadcasted_iota(jnp.int32, (keys, width), 1)
-    place = key_lane % SIZE
-    ones = jnp.where((place >= 1) & (place <= 3), 1.0, 0.0).astype(BF16)
-    for pair in range(q_ref.shape[1] // width):
+    place, key_place = lane % SIZE, key_lane % SIZE
+    ones = jnp.where((key_place >= 1) & (key_place <= 3), 1.0, 0.0).astype(BF16)
+    from_lane = lax.broadcasted_iota(jnp.int32, (2 * width, width), 0) % width
+    to_lane = lax.broadcasted_iota(jnp.int32, (2 * width, width), 1)
+    swap = jnp.where((from_lane < SIZE) != (to_lane < SIZE), 1.0, 0.0).astype(BF16)
+
+    def prepare(pair):
         span = slice(pair * width, (pair + 1) * width)
-        key_rows, value_rows = k_ref[:, span], v_ref[:, span]
+        value_rows = v_ref[:, span]
         grads = (grad_ref[:, span].astype(F32) * inverse_ref[:, span]).astype(BF16)
-        wide = grads.astype(F32)
-        products = wide * ctx_ref[:, span].astype(F32)
-        queries_t, grads_t = q_ref[:, span].T, grads.T
-        head_g, head_v = [], []
-        for head in range(2):
-            mine = (lane < SIZE) if head == 0 else (lane >= SIZE)
-            key_mine = (key_lane < SIZE) if head == 0 else (key_lane >= SIZE)
-            base = SIZE if head == 0 else 0
-            head_v.append(jnp.where(key_mine, value_rows, ones))
-            dots = split_three(-jnp.sum(jnp.where(mine, products, 0.0), 1, keepdims=True))
-            grad = jnp.where(mine, wide, 0.0)
-            for index, part in enumerate(dots):
-                grad = jnp.where(lane == base + index + 1, part, grad)
-            head_g.append(grad.astype(BF16))
-
+        products = grads.astype(F32) * ctx_ref[:, span].astype(F32)
+        high = products.astype(BF16)
+        low = (products - high.astype(F32)).astype(BF16)
+        parts = split_three(-dot(jnp.concatenate([high, low], 1), swap, 1, 0))
+        packed = jnp.zeros((rows, width), F32)
+        for index, part in enumerate(parts):
+            packed = jnp.where(place == index + 1, part, packed)
+        packed = packed.astype(BF16)
+        head_g = [jnp.where(lane < SIZE, grads, packed), jnp.where(lane < SIZE, packed, grads)]
+        head_v = [
+            jnp.where(key_lane < SIZE, value_rows, ones),
+            jnp.where(key_lane < SIZE, ones, value_rows),
+        ]
+        return head_g, head_v, q_ref[:, span].T, grads.T
+
+    def multiply(pair, head_g, head_v):
+        span = slice(pair * width, (pair + 1) * width)
+        key_rows = k_ref[:, span]
         grad_q, waiting = {}, []
-        before(pair)
-
-        def finish(at, head, grad_p, pair=pair, span=span, key_rows=key_rows, grad_q=grad_q):
+
+        def finish(at, head, grad_p):
             low, high = at * CHUNK, (at + 1) * CHUNK
             live = grad_p.shape[1]
             expo = expo_ref[2 * pair + head, low:high, :live]
@@ -189,6 +196,9 @@
                     finish(*waiting.pop(0))
         for unit in waiting:
             finish(*unit)
+
+    def collect(pair, queries_t, grads_t):
+        span = slice(pair * width, (pair + 1) * width)
         step = CHUNK if causal else keys
         for source, saved, first, to in (
             (grads_t, expo_ref, 2 * pair, dv_ref),
@@ -206,6 +216,14 @@
                     for head in range(2)
                 ]
                 to[low : low + step, span] = jnp.concatenate(parts, 0).T.astype(BF16)
+
+    ready = prepare(0)
+    for pair in range(pairs):
+        head_g, head_v, queries_t, grads_t = ready
+        before(pair)
+        multiply(pair, head_g, head_v)
+        ready = prepare(pair + 1) if pair + 1 < pairs else None
+        collect(pair, queries_t, grads_t)
         after(pair)
 
 
@@ -337,6 +355,7 @@
 
 
 FFN_STEP = 1024
+FFN_BACK_STEP = 512
 
 
 def second_block(w_ref, held, width):
@@ -361,7 +380,7 @@
     ramp_ref, n1_ref, ctx_ref, wo_ref, down_ref, up_ref,
     bo_ref, gain1_ref, shift1_ref, gain2_ref, shift2_ref, b2_ref, gain_a_ref, shift_a_ref, up_b_ref,
     down_b_ref,
-    normal_ref, hidden_ref, in_ref, act_ref, slope_ref, base_ref, stats_ref,
+    normal_ref, hidden_ref, in_ref, act_ref, slope_ref, base_ref, scale_ref, scale_a_ref,
 ):
     spans = parts_of(n1_ref.shape[0])
     sums = [dot(ctx_ref[span], wo_ref[...], 1, 0) + bo_ref[...] for span in spans]
@@ -371,16 +390,15 @@
         hidden = normal * gain2_ref[...] + shift2_ref[...]
         hidden_ref[span] = hidden.astype(BF16)
         base_ref[span] = hidden + b2_ref[...] + ramp_ref[0] * up_b_ref[...]
-        mean_a = jnp.mean(hidden, -1, keepdims=True)
         normal_a, scale_a = normalize(hidden)
         in_ref[span] = (normal_a * gain_a_ref[...] + shift_a_ref[...]).astype(BF16)
-        for at, value in enumerate((scale, mean_a, scale_a)):
-            stats_ref[span, at * 128 : (at + 1) * 128] = wide_scale(value)
+        scale_ref[span] = wide_scale(scale)
+        scale_a_ref[span] = wide_scale(scale_a)
     for span in spans:
         lower = dot(in_ref[span], down_ref[...], 1, 0) + down_b_ref[...]
         gate = 1.0 / (1.0 + jnp.exp(-lower))
         act_ref[span] = (lower * gate).astype(BF16)
-        slope_ref[span] = gate * (1.0 + lower * (1.0 - gate))
+        slope_ref[span] = (gate * (1.0 + lower * (1.0 - gate))).astype(BF16)
     for span in spans:
         base_ref[span] += ramp_ref[0] * dot(act_ref[span], up_ref[...], 1, 0)
 
@@ -400,15 +418,16 @@
         [scalar(), block(width), block(width), square(width, wo_at), whole(down.shape), whole(up.shape)]
         + [whole((1, width))] * 9
         + [whole((1, units))],
-        [block(width)] * 3 + [block(units)] * 2 + [block(width), block(384)],
+        [block(width)] * 3 + [block(units)] * 2 + [block(width)] + [block(128)] * 2,
         [
             jax.ShapeDtypeStruct((rows, width), F32),
             jax.ShapeDtypeStruct((rows, width), BF16),
             jax.ShapeDtypeStruct((rows, width), BF16),
             jax.ShapeDtypeStruct((rows, units), BF16),
-            jax.ShapeDtypeStruct((rows, units), F32),
+            jax.ShapeDtypeStruct((rows, units), BF16),
             jax.ShapeDtypeStruct((rows, width), F32),
-            jax.ShapeDtypeStruct((rows, 384), F32),
+            jax.ShapeDtypeStruct((rows, 128), F32),
+            jax.ShapeDtypeStruct((rows, 128), F32),
         ],
         2 * rows * width * width + 4 * rows * width * units,
         22 * rows * width,
@@ -417,11 +436,11 @@
 
 
 def middle_kernel(
-    held, factor, ramp_ref, hidden_ref, w1_ref, w2_ref, b1_ref, stats_ref,
-    gain2_ref, shift2_ref, gain3_ref, shift3_ref, gain_a_ref,
-    base_in, normal_in, in_in, act_in, slope_in, go_in, down_in, up_in,
+    held, factor, ramp_ref, hidden_ref, w1_ref, w2_ref, b1_ref, scale_a_ref,
+    gain3_ref, shift3_ref, gain_a_ref, shift_a_ref,
+    base_in, go_in, slope_in, up_in, act_in, down_in, in_in,
     slope_ref, out_out, gffn_out, rest_out, grads_out,
-    base_scr, normal_scr, in_scr, act_scr, slope_scr, go_scr, down_scr, up_scr,
+    base_scr, go_scr, slope_scr, up_scr, act_scr, down_scr, in_scr,
     total_scr, out_scr, gffn_scr, branch_scr, lower_scr, grads_scr, in_sems, out_sems,
 ):
     rows, width = hidden_ref.shape
@@ -430,8 +449,8 @@
     step = pl.program_id(0)
     loads = moved(
         [
-            (base_in, base_scr), (normal_in, normal_scr), (in_in, in_scr), (act_in, act_scr),
-            (slope_in, slope_scr), (go_in, go_scr), (down_in, down_scr), (up_in, up_scr),
+            (base_in, base_scr), (go_in, go_scr), (slope_in, slope_scr), (up_in, up_scr),
+            (act_in, act_scr), (down_in, down_scr), (in_in, in_scr),
         ],
         in_sems,
     )
@@ -440,9 +459,8 @@
     def _():
         total_scr[...] = jnp.zeros_like(total_scr)
 
-    @pl.when(step == 1)
-    def _():
-        start_all(loads)
+    for at, part in enumerate((loads[:1], loads[1:4], loads[4:])):
+        pl.when(step == at + 1)(functools.partial(start_all, part))
 
     def first(span):
         return dot(hidden_ref[span], w1_ref[...], 1, 0) + b1_ref[...]
@@ -459,7 +477,7 @@
     @pl.when(step == pl.num_programs(0) - 1)
     def _():
         ramp = ramp_ref[0]
-        wait_all(loads)
+        wait_all(loads[:4])
         outs = moved([(out_scr, out_out), (gffn_scr, gffn_out), (grads_scr, grads_out)], out_sems)
         kind = grads_scr.dtype
         sums = [jnp.zeros((1, width), F32)] * 3 + [jnp.zeros((1, units), F32)]
@@ -476,7 +494,7 @@
 
         def adapter_back(span):
             grad_act = dot(branch_scr[span], up_scr[...], 1, 1).astype(BF16).astype(F32)
-            grad_lower = (slope_scr[span] * grad_act).astype(BF16)
+            grad_lower = (slope_scr[span].astype(F32) * grad_act).astype(BF16)
             lower_scr[span] = grad_lower
             sums[3] = sums[3] + jnp.sum(grad_lower.astype(F32), 0, keepdims=True)
 
@@ -484,12 +502,12 @@
             norm_three(span)
             adapter_back(span)
         start_all(outs[:2])
+        wait_all(loads[4:])
         grads_scr[0:units, 0:width] = (dot(act_scr[...], branch_scr[...], 0, 0) * factor).astype(kind)
         for at, span in enumerate(spans):
             grad_adapt = dot(lower_scr[span], down_scr[...], 1, 1)
-            hidden = normal_scr[span] * gain2_ref[...] + shift2_ref[...]
-            scale_a = stats_ref[span, 256:257]
-            normal_a = (hidden - stats_ref[span, 128:129]) * scale_a
+            normal_a = (in_scr[span].astype(F32) - shift_a_ref[...]) * (1.0 / gain_a_ref[...])
+            scale_a = scale_a_ref[span, 0:1]
             total_scr[span] += normalize_back(normal_a, scale_a, gain_a_ref[...] * grad_adapt)
             outs.append(
                 pltpu.make_async_copy(total_scr.at[span], rest_out.at[span], out_sems.at[3 + at])
@@ -515,12 +533,11 @@
 
 
 def middle(
-    ramp, hidden, ffn_w, w2_at, w1_at, first_bias, stats, vectors, late, held, factor
+    ramp, hidden, ffn_w, w2_at, w1_at, first_bias, scale_a, vectors, late, held, factor
 ):
     rows, width = hidden.shape
     wide = first_bias.shape[1]
-    down, up = late[-2:]
-    units = down.shape[1]
+    units = late[2].shape[1]
     step = FFN_STEP
     groups = wide // width
     return call(
@@ -533,9 +550,9 @@
             columns(width, step, w1_at // step),
             pl.BlockSpec((step // groups, wide), lambda i: (i, w2_at // wide)),
             columns(1, step),
-            whole((rows, 384)),
+            whole((rows, 128)),
         ]
-        + [whole((1, width))] * 5
+        + [whole((1, width))] * 4
         + [anywhere()] * len(late),
         [columns(rows, step)] + [anywhere()] * 4,
         [
@@ -559,7 +576,7 @@
             pltpu.SemaphoreType.DMA((len(late),)),
             pltpu.SemaphoreType.DMA((3 + rows // CHUNK,)),
         ],
-    )(ramp, hidden, ffn_w, ffn_w, first_bias, stats, *vectors, *late)
+    )(ramp, hidden, ffn_w, ffn_w, first_bias, scale_a, *vectors, *late)
 
 
 def moved(pairs, sems):
@@ -579,63 +596,119 @@
         copy.wait()
 
 
-def norm_back_out(
-    grads, start_scr, normal_scr, scale_ref, gain_ref, low_scr, out_ref, low_ref, sems
-):
-    outs = []
-
-    def back(span):
-        grad = normalize_back(
-            normal_scr[span], scale_ref[span, 0:1], gain_ref[...] * (grads[span] + start_scr[span])
+def expo_loads(expo_ref, expo_scr, sems, group, count):
+    def load(which, pair):
+        heads = pl.ds(which * GROUP + 2 * pair, 2)
+        return pltpu.make_async_copy(
+            expo_ref.at[heads], expo_scr.at[pl.ds(2 * pair, 2)], sems.at[pair]
         )
-        start_scr[span] = grad
-        low_scr[span] = grad.astype(BF16)
-        copies = moved(
-            [(start_scr.at[span], out_ref.at[span]), (low_scr.at[span], low_ref.at[span])],
-            sems.at[pl.ds(len(outs), 2)],
-        )
-        start_all(copies)
-        outs.extend(copies)
-
-    return outs, back
-
-
-def ffn_backward_kernel(
-    held, g_ref, w1_ref, w2_ref, slope_ref, start_ref, normal_ref, scale_ref, gain_ref,
-    out_ref, low_ref, sum_scr, start_scr, normal_scr, low_scr, in_sems, out_sems,
+
+    def begin():
+        for pair in range(GROUP // 2):
+            load(0, pair).start()
+
+    def before(pair):
+        load(group, pair).wait()
+
+    def after(pair):
+        @pl.when(group < count - 1)
+        def _():
+            load(group + 1, pair).start()
+
+    return begin, before, after
+
+
+def group_loads(pairs, sems):
+    def copies(group, part):
+        slot = lax.rem(group, 2)
+        return [
+            pltpu.make_async_copy(source(group), target.at[slot], sems.at[at, slot])
+            for at, (source, target) in list(enumerate(pairs))[part]
+        ]
+
+    def start(group):
+        start_all(copies(group, slice(None)))
+
+    def wait(group, part):
+        wait_all(copies(group, part))
+
+    return start, wait
+
+
+def column_group(ref, first=0):
+    width = GROUP * SIZE
+    return lambda group: ref.at[:, pl.ds(pl.multiple_of(group * width, width) + first, width)]
+
+
+def row_group(ref, first, width):
+    depth = GROUP * SIZE
+    return lambda group: ref.at[
+        pl.ds(pl.multiple_of(group * depth, depth), depth), pl.ds(first, width)
+    ]
+
+
+def ffn_cross_backward_kernel(
+    held, ffn_steps, at,
+    g_ref, w1_ref, w2_ref, slope_ref, start_ref, normal2_ref, scale2_ref, gain2_ref,
+    normal1_ref, scale1_ref, gain1_ref, attn_ref, q_ref, k_ref, v_ref, ctx_ref, expo_ref, inverse_ref,
+    sum_ref, sum_low_ref, dk_ref, dv_ref,
+    total_scr, start_scr, normal_scr, low_scr, grad_scr, dq_scr, s_scr, expo_scr,
+    in_sems, out_sems, expo_sems,
+    wo_scr, wq_scr, q_scr, k_scr, v_scr, ctx_scr, inverse_scr, group_sems,
 ):
     rows, width = g_ref.shape
     spans = parts_of(rows)
-    step = pl.program_id(0)
-    loads = moved([(start_ref, start_scr), (normal_ref, normal_scr)], in_sems)
+    step, steps = pl.program_id(0), pl.num_programs(0)
+    loads = moved([(start_ref, start_scr), (normal2_ref, normal_scr)], in_sems)
+    late = pltpu.make_async_copy(normal1_ref, normal_scr, in_sems.at[2])
+    group, groups = step - ffn_steps, steps - ffn_steps
+    begin, before, after = expo_loads(expo_ref, expo_scr, expo_sems, group, groups)
+    start_group, wait_group = group_loads(
+        [
+            (row_group(attn_ref, at[0] * width, width), wo_scr),
+            (column_group(q_ref), q_scr),
+            (column_group(k_ref), k_scr),
+            (column_group(v_ref), v_scr),
+            (column_group(ctx_ref), ctx_scr),
+            (column_group(inverse_ref), inverse_scr),
+            (column_group(attn_ref, at[1] * width), wq_scr),
+        ],
+        group_sems,
+    )
 
     @pl.when(step == 0)
     def _():
-        sum_scr[...] = jnp.zeros_like(sum_scr)
-
-    @pl.when(step == 1)
-    def _():
-        start_all(loads)
+        total_scr[...] = jnp.zeros_like(total_scr)
+
+    pl.when(step == 1)(loads[0].start)
+    pl.when(step == ffn_steps // 2)(loads[1].start)
+    pl.when(step == ffn_steps - 2)(functools.partial(start_group, 0))
+
+    def first(span):
+        return dot(g_ref[span], second_block(w2_ref, held, width), 1, 1)
 
     def finish(span, grad_act):
         grad_pre = (slope_ref[span].astype(F32) * grad_act).astype(BF16)
-        sum_scr[span] += dot(grad_pre, w1_ref[...], 1, 1)
-
-    def first(span):
-        return dot(g_ref[span], second_block(w2_ref, held, width), 1, 1)
-
-    last = step == pl.num_programs(0) - 1
-
-    @pl.when(jnp.logical_not(last))
+        total_scr[span] += dot(grad_pre, w1_ref[...], 1, 1)
+
+    @pl.when(step < ffn_steps - 1)
     def _():
         in_turn([(first, span) for span in spans], finish)
 
-    @pl.when(last)
-    def _():
+    @pl.when(step == ffn_steps - 1)
+    def _():
+        begin()
         wait_all(loads)
-        outs, back = norm_back_out(
-            sum_scr, start_scr, normal_scr, scale_ref, gain_ref, low_scr, out_ref, low_ref, out_sems
-        )
+
+        def back(span):
+            grad = normalize_back(
+                normal_scr[span],
+                scale2_ref[span, 0:1],
+                gain2_ref[...] * (total_scr[span] + start_scr[span]),
+            )
+            total_scr[span] = grad
+            low_scr[span] = grad.astype(BF16)
+
         held_act, done = None, []
         for span in [*spans, None]:
             grad_act = first(span) if span is not None else None
@@ -646,161 +719,125 @@
             if len(done) > 1:
                 back(done.pop(0))
         back(done.pop(0))
-        wait_all(outs)
-
-
-def ffn_backward(grads, weights, w2_at, w1_at, slope, start, normal, scale, gain, held):
-    rows, width = grads.shape
-    wide = slope.shape[1]
-    step = FFN_STEP
-    groups = wide // width
-    return call(
-        functools.partial(ffn_backward_kernel, held),
-        "ffn_backward",
-        (wide // step,),
-        [
-            whole((rows, width)),
-            columns(width, step, w1_at // step),
-            pl.BlockSpec((step // groups, wide), lambda i: (i, w2_at // wide)),
-            columns(rows, step),
-            anywhere(),
-            anywhere(),
-            pl.BlockSpec((rows, 128), lambda i: (0, 0), pipeline_mode=pl.Buffered(1)),
-            whole((1, width)),
-        ],
-        [anywhere()] * 2,
-        [jax.ShapeDtypeStruct((rows, width), F32), jax.ShapeDtypeStruct((rows, width), BF16)],
-        4 * rows * width * wide,
-        16 * rows * width + 4 * width * wide + 2 * rows * wide,
-        0,
-        [pltpu.VMEM((rows, width), F32)] * 3
-        + [
-            pltpu.VMEM((rows, width), BF16),
-            pltpu.SemaphoreType.DMA((2,)),
-            pltpu.SemaphoreType.DMA((2 * rows // CHUNK,)),
-        ],
-    )(grads, weights, weights, slope, start, normal, scale, gain)
-
-
-def expo_loads(expo_ref, expo_scr, sems):
-    step, count = pl.program_id(0), pl.num_programs(0)
-
-    def load(group, pair):
-        heads = pl.ds(group * GROUP + 2 * pair, 2)
-        return pltpu.make_async_copy(
-            expo_ref.at[heads], expo_scr.at[pl.ds(2 * pair, 2)], sems.at[pair]
+        late.start()
+
+    slot = lax.rem(step, 2) if ffn_steps % 2 == 0 else lax.rem(step + 1, 2)
+
+    def add(span):
+        total_scr[span] += dot(dq_scr[span], wq_scr[slot], 1, 1)
+
+    @pl.when(step == ffn_steps)
+    def _():
+        dq_scr[...] = jnp.zeros_like(dq_scr)
+
+    @pl.when(step >= ffn_steps)
+    def _():
+        wait_group(group, slice(None))
+        for span in spans:
+            grad_scr[span] = dot(low_scr[span], wo_scr[slot], 1, 1).astype(BF16)
+        last_slot = jnp.where(group > 0, 1 - slot, slot)
+        for span in spans:
+            total_scr[span] += dot(dq_scr[span], wq_scr[last_slot], 1, 1)
+        pl.when(group < groups - 1)(functools.partial(start_group, group + 1))
+        attend_backward(
+            False, q_scr.at[slot], k_scr.at[slot], v_scr.at[slot], ctx_scr.at[slot], grad_scr, expo_scr,
+            inverse_scr.at[slot], dq_scr, dk_ref, dv_ref, s_scr, before, after,
         )
 
-    def begin():
-        load(0, 0).start()
-
-    def before(pair):
-        load(step, pair).wait()
-
-        @pl.when(step == 0)
-        def _():
-            for later in range(pair + 1, min(pair + 2, GROUP // 2)):
-                load(0, later).start()
-
-    def after(pair):
-        @pl.when(step < count - 1)
-        def _():
-            load(step + 1, pair).start()
-
-    return begin, before, after
-
-
-def cross_backward_kernel(
-    g_ref, low_ref, normal_ref, scale_ref, gain_ref, wo_ref, wq_ref, wk_ref, wv_ref,
-    q_ref, k_ref, v_ref, ctx_ref, expo_ref, inverse_ref,
-    states_ref, sum_ref, sum_low_ref,
-    total_scr, states_scr, start_scr, normal_scr, low_scr, grad_scr, dq_scr, dk_scr, dv_scr, s_scr, expo_scr,
-    in_sems, out_sems, expo_sems,
-):
-    spans = parts_of(low_ref.shape[0])
-    step = pl.program_id(0)
-    loads = moved([(g_ref, start_scr), (normal_ref, normal_scr)], in_sems)
-    begin, before, after = expo_loads(expo_ref, expo_scr, expo_sems)
-
-    @pl.when(step == 0)
-    def _():
-        begin()
-        total_scr[...] = jnp.zeros_like(total_scr)
-        states_scr[...] = jnp.zeros_like(states_scr)
-
-    @pl.when(step == 1)
-    def _():
-        start_all(loads)
-
-    for span in spans:
-        grad_scr[span] = dot(low_ref[span], wo_ref[...], 1, 1).astype(BF16)
-    attend_backward(
-        False, q_ref, k_ref, v_ref, ctx_ref, grad_scr, expo_scr, inverse_ref, dq_scr, dk_scr, dv_scr, s_scr,
-        before, after,
-    )
-    for span in parts_of(states_ref.shape[0]):
-        states_scr[span] += dot(dk_scr[span], wk_ref[...], 1, 1) + dot(dv_scr[span], wv_ref[...], 1, 1)
-
-    def add(span):
-        total_scr[span] += dot(dq_scr[span], wq_ref[...], 1, 1)
-
-    last = step == pl.num_programs(0) - 1
-
-    @pl.when(jnp.logical_not(last))
-    def _():
-        for span in spans:
-            add(span)
+    last = step == steps - 1
 
     @pl.when(last)
     def _():
-        states = pltpu.make_async_copy(states_scr, states_ref, out_sems.at[2 * len(spans)])
-        states.start()
-        wait_all(loads)
-        outs, back = norm_back_out(
-            total_scr, start_scr, normal_scr, scale_ref, gain_ref, low_scr, sum_ref, sum_low_ref, out_sems
-        )
+        late.wait()
+        outs = []
+
+        def back(span):
+            grad = normalize_back(
+                normal_scr[span], scale1_ref[span, 0:1], gain1_ref[...] * total_scr[span]
+            )
+            total_scr[span] = grad
+            low_scr[span] = grad.astype(BF16)
+            copies = moved(
+                [(total_scr.at[span], sum_ref.at[span]), (low_scr.at[span], sum_low_ref.at[span])],
+                out_sems.at[pl.ds(len(outs), 2)],
+            )
+            start_all(copies)
+            outs.extend(copies)
+
         add(spans[0])
         for before_span, span in zip(spans, spans[1:]):
             add(span)
             back(before_span)
         back(spans[-1])
-        wait_all([states, *outs])
+        wait_all(outs)
 
 
 def self_backward_kernel(
-    g_ref, low_ref, wo_ref, wq_ref, wk_ref, wv_ref, q_ref, k_ref, v_ref, ctx_ref, expo_ref, inverse_ref,
-    out_ref, total_scr, start_scr, grad_scr, dq_scr, dk_scr, dv_scr, s_scr, expo_scr,
+    at, cross_at,
+    g_ref, low_ref, cdk_ref, cdv_ref, attn_ref, q_ref, k_ref, v_ref, ctx_ref, expo_ref, inverse_ref,
+    out_ref, states_ref,
+    total_scr, states_scr, start_scr, low_scr, grad_scr, dq_scr, dk_scr, dv_scr, s_scr, expo_scr,
     in_sems, out_sems, expo_sems,
+    wo_scr, wq_scr, wk_scr, wv_scr, q_scr, k_scr, v_scr, ctx_scr, inverse_scr,
+    cdk_scr, cdv_scr, cwk_scr, cwv_scr, group_sems,
 ):
+    width = low_ref.shape[1]
     spans = parts_of(low_ref.shape[0])
-    step = pl.program_id(0)
-    load = pltpu.make_async_copy(g_ref, start_scr, in_sems.at[0])
-    begin, before, after = expo_loads(expo_ref, expo_scr, expo_sems)
+    step, steps = pl.program_id(0), pl.num_programs(0)
+    slot = lax.rem(step, 2)
+    load, low_load = moved([(g_ref, start_scr), (low_ref, low_scr)], in_sems)
+    begin, before, after = expo_loads(expo_ref, expo_scr, expo_sems, step, steps)
+    start_group, wait_group = group_loads(
+        [
+            (row_group(attn_ref, at[0] * width, width), wo_scr),
+            (column_group(cdk_ref), cdk_scr),
+            (column_group(attn_ref, cross_at[2] * width), cwk_scr),
+            (column_group(cdv_ref), cdv_scr),
+            (column_group(attn_ref, cross_at[3] * width), cwv_scr),
+            (column_group(q_ref), q_scr),
+            (column_group(k_ref), k_scr),
+            (column_group(v_ref), v_scr),
+            (column_group(ctx_ref), ctx_scr),
+            (column_group(inverse_ref), inverse_scr),
+            (column_group(attn_ref, at[1] * width), wq_scr),
+            (column_group(attn_ref, at[2] * width), wk_scr),
+            (column_group(attn_ref, at[3] * width), wv_scr),
+        ],
+        group_sems,
+    )
 
     @pl.when(step == 0)
     def _():
+        low_load.start()
+        start_group(0)
         begin()
         total_scr[...] = jnp.zeros_like(total_scr)
-
-    @pl.when(step == 1)
-    def _():
-        load.start()
-
+        states_scr[...] = jnp.zeros_like(states_scr)
+
+    pl.when(step == 1)(load.start)
+
+    pl.when(step == 0)(low_load.wait)
+    wait_group(step, slice(None))
+    pl.when(step < steps - 1)(functools.partial(start_group, step + 1))
     for span in spans:
-        grad_scr[span] = dot(low_ref[span], wo_ref[...], 1, 1).astype(BF16)
+        grad_scr[span] = dot(low_scr[span], wo_scr[slot], 1, 1).astype(BF16)
+    for span in parts_of(states_scr.shape[0]):
+        states_scr[span] += dot(cdk_scr[slot, span], cwk_scr[slot], 1, 1) + dot(
+            cdv_scr[slot, span], cwv_scr[slot], 1, 1
+        )
     attend_backward(
-        True, q_ref, k_ref, v_ref, ctx_ref, grad_scr, expo_scr, inverse_ref, dq_scr, dk_scr, dv_scr, s_scr,
-        before, after,
+        True, q_scr.at[slot], k_scr.at[slot], v_scr.at[slot], ctx_scr.at[slot], grad_scr, expo_scr,
+        inverse_scr.at[slot], dq_scr, dk_scr, dv_scr, s_scr, before, after,
     )
 
     def back(span):
         return (
-            dot(dq_scr[span], wq_ref[...], 1, 1)
-            + dot(dk_scr[span], wk_ref[...], 1, 1)
-            + dot(dv_scr[span], wv_ref[...], 1, 1)
+            dot(dq_scr[span], wq_scr[slot], 1, 1)
+            + dot(dk_scr[span], wk_scr[slot], 1, 1)
+            + dot(dv_scr[span], wv_scr[slot], 1, 1)
         )
 
-    last = step == pl.num_programs(0) - 1
+    last = step == steps - 1
 
     @pl.when(jnp.logical_not(last))
     def _():
@@ -810,90 +847,118 @@
     @pl.when(last)
     def _():
         load.wait()
-        outs = []
-        for at, span in enumerate(spans):
+        outs = [pltpu.make_async_copy(states_scr, states_ref, out_sems.at[len(spans)])]
+        outs[0].start()
+        for index, span in enumerate(spans):
             total_scr[span] += start_scr[span] + back(span)
             outs.append(
-                pltpu.make_async_copy(total_scr.at[span], out_ref.at[span], out_sems.at[at])
+                pltpu.make_async_copy(total_scr.at[span], out_ref.at[span], out_sems.at[index])
             )
             outs[-1].start()
         wait_all(outs)
 
 
-def attend_in(rows, keys, width, at):
-    group = GROUP * SIZE
-    per = width // group
-    weights = [pl.BlockSpec((group, width), lambda i: (i, at[0]))] + [
-        columns(width, group, first * per) for first in at[1:]
-    ]
-    return weights + [
-        columns(rows, group),
-        columns(keys, group),
-        columns(keys, group),
-        columns(rows, group),
-        anywhere(),
-        columns(rows, group),
-    ]
-
-
 def attend_scratch(rows, keys):
-    group = GROUP * SIZE
     return [
-        pltpu.VMEM((rows, group), BF16),
-        pltpu.VMEM((rows, group), BF16),
-        pltpu.VMEM((keys, group), BF16),
-        pltpu.VMEM((keys, group), BF16),
         pltpu.VMEM((2, rows, keys), BF16),
         pltpu.VMEM((GROUP, rows, keys), BF16),
-        pltpu.SemaphoreType.DMA((2,)),
-        pltpu.SemaphoreType.DMA((2 * rows // CHUNK + 1,)),
+        pltpu.SemaphoreType.DMA((3,)),
+        pltpu.SemaphoreType.DMA((2 * rows // CHUNK,)),
         pltpu.SemaphoreType.DMA((GROUP // 2,)),
     ]
 
 
-def cross_backward(grads, low, normal, scale, gain, weights, at, saved):
+def group_scratch(rows, keys, width, weights):
+    group = GROUP * SIZE
+    return (
+        [pltpu.VMEM((2, group, width), BF16)]
+        + [pltpu.VMEM((2, width, group), BF16)] * weights
+        + [pltpu.VMEM((2, rows, group), BF16)]
+        + [pltpu.VMEM((2, keys, group), BF16)] * 2
+        + [pltpu.VMEM((2, rows, group), BF16), pltpu.VMEM((2, rows, group), F32)]
+    )
+
+
+def ffn_cross_backward(
+    grads, ffn_w, w2_at, w1_at, slope, start, normal2, scale2, gain2, normal1, scale1, gain1, attn_w, at, saved,
+    held,
+):
     rows, width = grads.shape
     keys = saved[1].shape[0]
+    wide = slope.shape[1]
+    groups = wide // width
+    block = FFN_BACK_STEP
+    steps = wide // block
+    group = GROUP * SIZE
+
+    def unit(i):
+        return jnp.minimum(i, steps - 1)
+
+    def out(i):
+        return (0, jnp.maximum(i - steps, 0))
+
     return call(
-        cross_backward_kernel,
-        "cross_backward",
-        (width // (GROUP * SIZE),),
-        [anywhere(), whole((rows, width)), anywhere(), whole((rows, 128)), whole((1, width))]
-        + attend_in(rows, keys, width, at),
-        [anywhere()] * 3,
+        functools.partial(ffn_cross_backward_kernel, held, steps, at),
+        "ffn_cross_backward",
+        (steps + width // group,),
         [
-            jax.ShapeDtypeStruct((keys, width), F32),
+            whole((rows, width)),
+            pl.BlockSpec((width, block), lambda i: (0, unit(i) + w1_at // block)),
+            pl.BlockSpec((block // groups, wide), lambda i: (unit(i), w2_at // wide)),
+            pl.BlockSpec((rows, block), lambda i: (0, unit(i))),
+            anywhere(),
+            anywhere(),
+            whole((rows, 128)),
+            whole((1, width)),
+            anywhere(),
+            whole((rows, 128)),
+            whole((1, width)),
+        ]
+        + [anywhere()] * 7,
+        [anywhere()] * 2 + [pl.BlockSpec((keys, group), out)] * 2,
+        [
             jax.ShapeDtypeStruct((rows, width), F32),
             jax.ShapeDtypeStruct((rows, width), BF16),
+            jax.ShapeDtypeStruct((keys, width), BF16),
+            jax.ShapeDtypeStruct((keys, width), BF16),
         ],
-        8 * rows * width * width + 8 * rows * keys * width,
-        32 * rows * width + 8 * width * width + 32 * rows * keys,
+        4 * rows * width * (width + wide) + 8 * rows * keys * width,
+        48 * rows * width + 4 * width * (width + wide) + 2 * rows * wide + 32 * rows * keys,
         0,
-        [
-            pltpu.VMEM((rows, width), F32),
-            pltpu.VMEM((keys, width), F32),
-            pltpu.VMEM((rows, width), F32),
-            pltpu.VMEM((rows, width), F32),
-            pltpu.VMEM((rows, width), BF16),
-        ]
-        + attend_scratch(rows, keys),
-    )(grads, low, normal, scale, gain, weights, weights, weights, weights, *saved)
-
-
-def self_backward(grads, low, weights, at, saved):
+        [pltpu.VMEM((rows, width), F32)] * 3
+        + [pltpu.VMEM((rows, width), BF16)]
+        + [pltpu.VMEM((rows, group), BF16)] * 2
+        + attend_scratch(rows, keys)
+        + group_scratch(rows, keys, width, 1)
+        + [pltpu.SemaphoreType.DMA((7, 2))],
+    )(
+        grads, ffn_w, ffn_w, slope, start, normal2, scale2, gain2, normal1, scale1, gain1, attn_w, *saved
+    )
+
+
+def self_backward(grads, low, cross_grads, weights, at, cross_at, saved):
     rows, width = grads.shape
+    keys = cross_grads[0].shape[0]
+    group = GROUP * SIZE
     return call(
-        self_backward_kernel,
+        functools.partial(self_backward_kernel, at, cross_at),
         "self_backward",
-        (width // (GROUP * SIZE),),
-        [anywhere(), whole((rows, width))] + attend_in(rows, rows, width, at),
-        anywhere(),
-        jax.ShapeDtypeStruct((rows, width), F32),
-        8 * rows * width * width + 4 * rows * rows * width,
-        20 * rows * width + 8 * width * width + 32 * rows * rows,
+        (width // group,),
+        [anywhere()] * 11,
+        [anywhere()] * 2,
+        [jax.ShapeDtypeStruct((rows, width), F32), jax.ShapeDtypeStruct((keys, width), F32)],
+        8 * rows * width * width + 4 * keys * width * width + 4 * rows * rows * width,
+        28 * rows * width + 12 * width * width + 32 * rows * rows,
         0,
-        [pltpu.VMEM((rows, width), F32)] * 2 + attend_scratch(rows, rows),
-    )(grads, low, weights, weights, weights, weights, *saved)
+        [pltpu.VMEM((rows, width), F32), pltpu.VMEM((keys, width), F32), pltpu.VMEM((rows, width), F32)]
+        + [pltpu.VMEM((rows, width), BF16)]
+        + [pltpu.VMEM((rows, group), BF16)] * 4
+        + attend_scratch(rows, rows)
+        + group_scratch(rows, rows, width, 3)
+        + [pltpu.VMEM((2, keys, group), BF16)] * 2
+        + [pltpu.VMEM((2, width, group), BF16)] * 2
+        + [pltpu.SemaphoreType.DMA((13, 2))],
+    )(grads, low, *cross_grads, weights, *saved)
 
 
 def unpack_kernel(up_in, down_in, small_in, down_ref, up_ref, up_b_ref, gain_ref, shift_ref, down_b_ref):
@@ -1018,7 +1083,7 @@
         (bias[2], gain[0], shift[0], bias[3], bias[4]),
     )
     token_total = sequences * row_count * lax.axis_size("fsdp") * lax.axis_size("dp")
-    normal2, hidden2, adapt_in, adapt_act, adapt_slope, base, stats = post_cross(
+    normal2, hidden2, adapt_in, adapt_act, adapt_slope, base, scale2, scale_a = post_cross(
         ramp,
         normal1,
         cross_ctx,
@@ -1037,31 +1102,41 @@
         w2_at,
         w1_at,
         ffn_in_bias[None],
-        stats,
-        (gain[1], shift[1], gain[2], shift[2], adapter_gain[None]),
-        (base, normal2, adapt_in, adapt_act, adapt_slope)
-        + (grad_out.reshape(-1, width), adapter_down, adapter_up),
+        scale_a,
+        (gain[2], shift[2], adapter_gain[None], adapter_shift[None]),
+        (base, grad_out.reshape(-1, width), adapt_slope, adapter_up, adapt_act, adapter_down, adapt_in),
         held,
         1.0 / math.sqrt(token_total),
     )
     scattered = lax.psum_scatter(adapter_grads, "fsdp", scatter_dimension=0, tiled=True)
-    grad_sum2, low_sum2 = ffn_backward(
-        grad_ffn, ffn_w, w2_at, w1_at, slope, grad_rest, normal2, stats, gain[1], held
-    )
-    grad_encoder, grad_sum1, low_sum1 = cross_backward(
-        grad_sum2,
-        low_sum2,
+    grad_sum1, low_sum1, *cross_grads = ffn_cross_backward(
+        grad_ffn,
+        ffn_w,
+        w2_at,
+        w1_at,
+        slope,
+        grad_rest,
+        normal2,
+        scale2,
+        gain[1],
         normal1,
         scale1,
         gain[0],
         attn_w,
         cross_at,
         (*cross_saved, cross_ctx, cross_expo, cross_inverse),
+        held,
     )
     scattered, low_sum1 = lax.optimization_barrier((scattered, low_sum1))
     adapter_grads = gather(sum_over(scattered, "dp"))
-    grad_input = self_backward(
-        grad_sum1, low_sum1, attn_w, self_at, (*self_saved, self_ctx, self_expo, self_inverse)
+    grad_input, grad_encoder = self_backward(
+        grad_sum1,
+        low_sum1,
+        cross_grads,
+        attn_w,
+        self_at,
+        cross_at,
+        (*self_saved, self_ctx, self_expo, self_inverse),
     )
     grad_down, grad_up, up_bias, grad_gain, grad_shift, down_bias = unpack(
         adapter_grads, adapter_down.shape

time: 377 us -> 366 us (0.971)
  Pallas kernels: 241 us -> 234 us
  waiting for transfers between devices: 107 us -> 103 us
    pallas_call x3 -> x2, Pallas kernels: 117 us -> 111 us  [the longest x1 67.5 us: ffn_cross_backward(): call(functools.partial(ffn_cross_backward_kernel, held, steps, at), 'ffn_...]
    all_gather x3, waiting for transfers between devices: 102 us -> 97.9 us  [gather(): return lax.all_gather(shard, 'fsdp', axis=0, tiled=True)]
  transfers between devices with their start and end apart: 5 -> 5, of which waited for: 4 -> 3; matrix products, arithmetic and copies ran while one was open for 1% -> 1% of each run, Pallas kernels for 54% -> 54%
where the time goes in v5:
time: 366 us; the launch traced here: 361 us
  Pallas kernels  234 us (64%)
  waiting for transfers between devices  103 us (28%)
  between operations  15.5 us (4%)
  other arithmetic  4.59 us (1%)
    all_gather x3, waiting for transfers between devices, gather(): return lax.all_gather(shard, 'fsdp', axis=0, tiled=True)  97.9 us
    pallas_call x1, Pallas kernels, ffn_cross_backward(): call(functools.partial(ffn_cross_backward_kernel, held, steps, at), 'ffn_...  67.5 us
    pallas_call x1, Pallas kernels, self_backward(): call(functools.partial(self_backward_kernel, at, cross_at), 'self_backwar...  43.1 us
    pallas_call x1, Pallas kernels, cross_forward(): call(cross_forward_kernel, 'cross_forward', (per,), [scalar(), whole((row...  40.9 us
    pallas_call x1, Pallas kernels, middle(): call(functools.partial(middle_kernel, held, factor), 'middle', (wide // s...  35.3 us
    pallas_call x1, Pallas kernels, self_forward(): call(self_forward_kernel, 'self_forward', (per,), [scalar(), whole((rows,...  29.5 us
    pallas_call x1, Pallas kernels, post_cross(): call(post_cross_kernel, 'post_cross', (rows // step,), [scalar(), block(w...  13.3 us
  transfers between devices with their start and end apart: 5, of which 3 were waited for; matrix products, arithmetic and copies ran while one was open for 1% of the time, Pallas kernels for 54%

profile of v5, /device:TPU:0, one launch (start us, length us, event | category | flops | bytes accessed | tf_op | source)
XLA Modules:
  0.0 360.7 jit_solution(18165343450709561395)
XLA Ops:
  7.2 0.0 copy-start.1
  7.2 0.0 all-gather.4.cloned.1.call-start
  7.2 0.0 copy-start.2
  7.3 2.3 pad_maximum_fusion
  9.6 0.0 copy-start.6
  9.6 0.0 copy-start.3
  9.6 0.0 copy-start.4
  9.6 0.0 copy-start.5
  9.6 0.0 all-gather.4.cloned.1.call-update
  9.6 0.0 all-gather.6.cloned.1.call-start
  9.7 0.0 copy-done.1
  9.8 0.0 copy-done.2
  9.8 0.0 copy-start
  9.8 1.0 copy-done
  10.8 0.0 all-gather.6.cloned.1.call-update
  10.8 0.0 reduce-scatter.2.cloned.1.call-start
  12.2 0.0 copy-done.6
  12.2 0.6 fusion
  12.8 0.0 copy-done.3
  12.8 0.6 fusion.1
  13.5 0.0 copy-done.4
  13.5 0.0 copy-done.5
  13.5 0.6 fusion.2
  14.1 89.2 %all-gather.4.cloned.1.call-done.wq_ref.wk_ref.wv_ref.wo_ref.attn_ref = bf16[1024,8320]{1,0:T(8,128)(2,1)} async-done(((bf16[64,8320]{1,0:T(8,128)(2,1)}), bf16[1024,8320]{1,0:T(8,128)(2,1)}) %all-gather.4.cloned.1.call-update) | async-done | bytes 17039376 | tf_op jit(solution)/shard_map/all_gather | solution.py:1018
  103.2 29.5 %self_forward.1 = (bf16[1024,1024]{1,0:T(8,128)(2,1)}, bf16[1024,1024]{1,0:T(8,128)(2,1)}, bf16[1024,1024]{1,0:T(8,128)(2,1)}, bf16[1024,1024]{1,0:T(8,128)(2,1)...) custom-call(s32[1]{0:T(128)} %bitcast.1.length_ref, bf16[1024,1024]{1,0:T(8,128)(2,1)} %bitcast.18, ...), custom_call_target="tpu_custom_call" | custom-call | flops 10737418240 | bytes 58720256 | tf_op jit(solution)/shard_map/self_forward/pallas_call | solution.py:287
  132.7 40.9 %cross_forward.1 = (f32[1024,1024]{1,0:T(8,128)}, f32[1024,128]{1,0:T(8,128)}, bf16[1024,1024]{1,0:T(8,128)(2,1)}, bf16[1024,1024]{1,0:T(8,128)(2,1)}, bf16[1024...) custom-call(s32[1]{0:T(128)S(6)} %copy.35.length_ref, ...), custom_call_target="tpu_custom_call" | custom-call | flops 12884901888 | bytes 69206016 | tf_op jit(solution)/shard_map/cross_forward/pallas_call | solution.py:339
  173.7 13.3 %post_cross.1 = (f32[1024,1024]{1,0:T(8,128)}, bf16[1024,1024]{1,0:T(8,128)(2,1)}, bf16[1024,1024]{1,0:T(8,128)(2,1)}, bf16[1024,512]{1,0:T(8,128)(2,1)}, bf16[1...) custom-call(f32[1]{0:T(128)S(6)} %div.3.ramp_ref, ...), custom_call_target="tpu_custom_call" | custom-call | flops 4294967296 | bytes 23068672 | tf_op jit(solution)/shard_map/post_cross/pallas_call | solution.py:414
  187.0 8.8 %all-gather.6.cloned.1.call-done.w1_ref.w2_ref = bf16[1024,8320]{1,0:T(8,128)(2,1)} async-done(((bf16[64,8320]{1,0:T(8,128)(2,1)}), bf16[1024,8320]{1,0:T(8,128)(2,1)}) %all-gather.6.cloned.1.call-update) | async-done | bytes 17039376 | tf_op jit(solution)/shard_map/all_gather | solution.py:1018
  195.7 35.3 %middle.1 = (bf16[1024,4096]{1,0:T(8,128)(2,1)}, bf16[1024,1024]{1,0:T(8,128)(2,1)}, bf16[1024,1024]{1,0:T(8,128)(2,1)}, f32[1024,1024]{1,0:T(8,128)}, bf16[1024,1152]{1,0:T(8,128)(2,1)}) custom-call(f32[1]{0:T(128)S(6)} %div.3.ramp_ref, bf16[1024,1024]{1,0:T(8,128)(2,1)} %get-tuple-element.53.hidden_ref, ...), custom_call_target="tpu_custom_call" | custom-call | flops 21474836480 | bytes 54525952 | tf_op jit(solution)/shard_map/middle/pallas_call | solution.py:543
  231.0 0.0 reduce-scatter.2.cloned.1.call-update
  231.1 0.0 all-gather.8.cloned.1.call-start
  231.1 67.5 %ffn_cross_backward.1 = (f32[1024,1024]{1,0:T(8,128)}, bf16[1024,1024]{1,0:T(8,128)(2,1)}, bf16[1024,1024]{1,0:T(8,128)(2,1)}, bf16[1024,1024]{1,0:T(8,128)(2,1)}) custom-call(bf16[1024,1024]{1,0:T(8,128)(2,1)} %get-tuple-element.60.g_ref, bf16[1024,8320]{1,0:T(8,128)(2,1)} %all-gather.6.cloned.1.call-done.w1_ref.w2_ref, ...), custom_call_target="tpu_custom_call" | custom-call | flops 30064771072 | bytes 113246208 | tf_op jit(solution)/shard_map/ffn_cross_backward/pallas_call | solution.py:900
  298.6 0.0 reduce-scatter.2.cloned.1.call-done
  298.6 1.5 collective-permute-start
  300.2 4.8 %collective-permute-done = bf16[64,1152]{1,0:T(8,128)(2,1)S(1)} collective-permute-done((bf16[64,1152]{1,0:T(8,128)(2,1)}, bf16[64,1152]{1,0:T(8,128)(2,1)S(1)}, u32[]{:S(2)}, u32[]{:S(2)}) %collective-permute-start) | collective-permute-done | bytes 147488 | tf_op jit(solution)/shard_map/ppermute | solution.py:1025
  304.9 1.6 add_convert_fusion
  306.5 0.0 all-gather.8.cloned.1.call-update
  306.6 43.1 %self_backward.1 = (f32[1024,1024]{1,0:T(8,128)}, f32[1024,1024]{1,0:T(8,128)}) custom-call(f32[1024,1024]{1,0:T(8,128)} %get-tuple-element.71.g_ref, bf16[1024,1024]{1,0:T(8,128)(2,1)} %get-tuple-element.74.low_ref, bf16[1024,1024]{1,0:T(8,128)(2,1)} %get-tuple-element.75.cdk_ref, bf16[1024,1024]{1,0:T(8,128)(2,1)} %get-tuple-element.76.cdv_ref, ...), custom_call_target="tpu_custom_call" | custom-call | flops 17179869184 | bytes 75497472 | tf_op jit(solution)/shard_map/self_backward/pallas_call | solution.py:943
  349.7 0.0 all-gather.8.cloned.1.call-done.up_in.down_in.small_in
  349.7 4.2 %unpack.1 = (f32[2,512,512]{2,1,0:T(8,128)}, f32[512,1024]{1,0:T(8,128)}, f32[1,1024]{1,0:T(1,128)}, f32[1,1024]{1,0:T(1,128)}, f32[1,1024]{1,0:T(1,128)}, /*index=5*/f32[1,512]{1,0:T(1,128)}) custom-call(bf16[1024,1152]{1,0:T(8,128)(2,1)} %all-gather.8.cloned.1.call-done.up_in.down_in.small_in, ...), custom_call_target="tpu_custom_call" | custom-call | bytes 8388608 | tf_op jit(solution)/shard_map/unpack/pallas_call | solution.py:990
  (7 shorter events, 0.1 us)
Async XLA Ops:
  7.2 2.5 copy-start.1
  7.2 96.0 %all-gather.4.cloned.1.call-start = ((), (), s32[]{:S(2)}) async-start(), calls=%async_computation.1 | async-start | bytes 18104320 | tf_op jit(solution)/shard_map/all_gather | solution.py:1018
  7.2 2.5 copy-start.2
  9.6 2.6 copy-start.6
  9.6 3.2 copy-start.3
  9.6 3.9 %copy-start.4 = (f32[3,1024]{1,0:T(4,128)S(1)}, f32[3,1024]{1,0:T(4,128)}, u32[]{:S(2)}) copy-start(f32[3,1024]{1,0:T(4,128)} %param.35) | copy-start | bytes 36868
  9.6 3.9 %copy-start.5 = (f32[3,1024]{1,0:T(4,128)S(1)}, f32[3,1024]{1,0:T(4,128)}, u32[]{:S(2)}) copy-start(f32[3,1024]{1,0:T(4,128)} %param.34) | copy-start | bytes 36868
  9.6 186.1 %all-gather.6.cloned.1.call-start = ((), (), s32[]{:S(2)}) async-start(), calls=%async_computation.2 | async-start | bytes 18104320 | tf_op jit(solution)/shard_map/all_gather | solution.py:1018
  9.8 1.0 copy-start
  10.8 287.8 %reduce-scatter.2.cloned.1.call-start = ((), (), s32[]{:S(2)}) async-start(), calls=%async_computation.3 | async-start | bytes 2506752 | tf_op jit(solution)/shard_map/reduce_scatter | solution.py:1111
  231.1 118.7 %all-gather.8.cloned.1.call-start = ((), (), s32[]{:S(2)}) async-start(), calls=%async_computation.4 | async-start | bytes 2506752 | tf_op jit(solution)/shard_map/all_gather | solution.py:1018
  298.6 6.3 %collective-permute-start = (bf16[64,1152]{1,0:T(8,128)(2,1)}, bf16[64,1152]{1,0:T(8,128)(2,1)S(1)}, u32[]{:S(2)}, u32[]{:S(2)}) collective-permute-start(bf16[64,1152]{1,0:T(8,128)(2,1)} %reduce-scatter.2.cloned.1.call-done), channel_id=1, source_target_pairs={{0,1},{1,0},{2,3},{3,2},{4,5},{5,4},{6,7},{7,6},{8,9},{9,8},{10,11... | collective-permute-start | bytes 442376 | tf_op jit(solution)/shard_map/ppermute | solution.py:1025
Sparse Core Ops, SparseCore 0:
  10.2 93.0 all-gather.3
  105.4 90.2 all-gather.5
  231.2 62.9 reduce-scatter.1
  306.7 42.3 all-gather.7

commit v6 on v5

--- a/solution.py
+++ b/solution.py
@@ -222,8 +222,12 @@
         head_g, head_v, queries_t, grads_t = ready
         before(pair)
         multiply(pair, head_g, head_v)
-        ready = prepare(pair + 1) if pair + 1 < pairs else None
+        more = pair + 1 < pairs
+        if causal and more:
+            ready = prepare(pair + 1)
         collect(pair, queries_t, grads_t)
+        if more and not causal:
+            ready = prepare(pair + 1)
         after(pair)
 
 
@@ -478,7 +482,15 @@
     def _():
         ramp = ramp_ref[0]
         wait_all(loads[:4])
-        outs = moved([(out_scr, out_out), (gffn_scr, gffn_out), (grads_scr, grads_out)], out_sems)
+        main, beside = pl.ds(0, width), pl.ds(width, 128)
+        outs = moved(
+            [
+                (out_scr, out_out),
+                (gffn_scr, gffn_out),
+                (grads_scr.at[:, main], grads_out.at[:, main]),
+            ],
+            out_sems,
+        )
         kind = grads_scr.dtype
         sums = [jnp.zeros((1, width), F32)] * 3 + [jnp.zeros((1, units), F32)]
 
@@ -519,6 +531,7 @@
             grads_scr[units : 2 * units, at : at + units] = (
                 dot(in_scr[:, at : at + units], lower_scr[...], 0, 0) * factor
             ).astype(kind)
+        outs[2].start()
         vectors = []
         for row in sums:
             row = row * factor
@@ -528,7 +541,12 @@
         lines = small.shape[0]
         grads_scr[0:lines, width:] = small
         grads_scr[lines:, width:] = jnp.zeros((2 * units - lines, 128), kind)
-        outs[2].start()
+        outs.append(
+            pltpu.make_async_copy(
+                grads_scr.at[:, beside], grads_out.at[:, beside], out_sems.at[3 + len(spans)]
+            )
+        )
+        outs[-1].start()
         wait_all(outs)
 
 
@@ -574,7 +592,7 @@
             pltpu.VMEM((rows, units), BF16),
             pltpu.VMEM((2 * units, width + 128), BF16),
             pltpu.SemaphoreType.DMA((len(late),)),
-            pltpu.SemaphoreType.DMA((3 + rows // CHUNK,)),
+            pltpu.SemaphoreType.DMA((4 + rows // CHUNK,)),
         ],
     )(ramp, hidden, ffn_w, ffn_w, first_bias, scale_a, *vectors, *late)
 
@@ -980,7 +998,7 @@
 def unpack(grads, down_shape):
     width, units = down_shape
     halves = width // units
-    steps = 4
+    steps = 2
     step = units // steps
     small = 4 * width // 128
 
@@ -1012,6 +1030,51 @@
         16 * width * units,
     )(grads, grads, grads)
     return down.reshape(down_shape), *rest
+
+
+def join_kernel(first_ref, second_ref, out_ref, held_scr, in_sems, out_sems):
+    rows = first_ref.shape[0]
+    wide, more = first_ref.shape[1], second_ref.shape[1]
+    parts = [pl.ds(at, rows // 2) for at in range(0, rows, rows // 2)]
+    loads = []
+    for at, part in enumerate(parts):
+        loads.append(
+            moved(
+                [
+                    (first_ref.at[part], held_scr.at[part, pl.ds(0, wide)]),
+                    (second_ref.at[part], held_scr.at[part, pl.ds(wide, more)]),
+                ],
+                in_sems.at[at],
+            )
+        )
+        start_all(loads[-1])
+    held_scr[:, wide + more :] = jnp.zeros((rows, held_scr.shape[1] - wide - more), BF16)
+    outs = moved([(held_scr.at[part], out_ref.at[part]) for part in parts], out_sems)
+    for load, out in zip(loads, outs):
+        wait_all(load)
+        out.start()
+    wait_all(outs)
+
+
+def join(first, second, spare):
+    rows = first.shape[0]
+    shape = (rows, first.shape[1] + second.shape[1] + spare)
+    return call(
+        join_kernel,
+        "join",
+        (),
+        [anywhere()] * 2,
+        anywhere(),
+        jax.ShapeDtypeStruct(shape, BF16),
+        0,
+        4 * rows * shape[1],
+        0,
+        [
+            pltpu.VMEM(shape, BF16),
+            pltpu.SemaphoreType.DMA((2, 2)),
+            pltpu.SemaphoreType.DMA((2,)),
+        ],
+    )(first, second)
 
 
 def gather(shard):
@@ -1055,7 +1118,7 @@
     groups = ffn_out.shape[0] // held
     wide = ffn_in.shape[1]
     pad = jnp.zeros((held, 128), BF16)
-    attn_w = gather(jnp.concatenate([attn_in, attn_out, pad], 1))
+    attn_w = gather(join(attn_in, attn_out, 128))
     ffn_w = jnp.concatenate(
         [ffn_out[at * held : (at + 1) * held] for at in range(groups)] + [ffn_in, pad], 1
     )

time: 366 us -> 364 us (level)
  no operation moved by 1% of the time
where the time goes in v6:
time: 364 us; the launch traced here: 359 us
  Pallas kernels  234 us (64%)
  waiting for transfers between devices  103 us (28%)
  between operations  15.5 us (4%)
    all_gather x3, waiting for transfers between devices, gather(): return lax.all_gather(shard, 'fsdp', axis=0, tiled=True)  98.1 us
    pallas_call x1, Pallas kernels, ffn_cross_backward(): call(functools.partial(ffn_cross_backward_kernel, held, steps, at), 'ffn_...  66.5 us
    pallas_call x1, Pallas kernels, self_backward(): call(functools.partial(self_backward_kernel, at, cross_at), 'self_backwar...  43.1 us
    pallas_call x1, Pallas kernels, cross_forward(): call(cross_forward_kernel, 'cross_forward', (per,), [scalar(), whole((row...  40.9 us
    pallas_call x1, Pallas kernels, middle(): call(functools.partial(middle_kernel, held, factor), 'middle', (wide // s...  35.3 us
    pallas_call x1, Pallas kernels, self_forward(): call(self_forward_kernel, 'self_forward', (per,), [scalar(), whole((rows,...  29.5 us
    pallas_call x1, Pallas kernels, post_cross(): call(post_cross_kernel, 'post_cross', (rows // step,), [scalar(), block(w...  13.3 us
  transfers between devices with their start and end apart: 5, of which 3 were waited for; matrix products, arithmetic and copies ran while one was open for 1% of the time, Pallas kernels for 54%

profile of v6, /device:TPU:0, one launch (start us, length us, event | category | flops | bytes accessed | tf_op | source)
XLA Modules:
  0.0 358.9 jit_solution(9146607238918943791)
XLA Ops:
  7.2 0.0 copy-start.1
  7.2 0.0 copy-start.2
  7.2 0.0 all-gather.4.cloned.1.call-start
  7.2 2.1 join.1
  9.4 0.0 copy-start.6
  9.4 0.0 copy-start.3
  9.4 0.0 copy-start.4
  9.4 0.0 copy-start.5
  9.4 0.0 all-gather.4.cloned.1.call-update
  9.5 0.0 all-gather.6.cloned.1.call-start
  9.5 0.0 copy-done.1
  9.6 0.0 copy-done.2
  9.7 0.0 copy-start
  9.7 1.0 copy-done
  10.6 0.0 all-gather.6.cloned.1.call-update
  10.7 0.0 reduce-scatter.2.cloned.1.call-start
  12.0 0.0 copy-done.6
  12.0 0.6 fusion
  12.7 0.0 copy-done.3
  12.7 0.6 fusion.1
  13.3 0.0 copy-done.4
  13.3 0.0 copy-done.5
  13.3 0.6 fusion.2
  13.9 89.3 %all-gather.4.cloned.1.call-done.wq_ref.wk_ref.wv_ref.wo_ref.attn_ref = bf16[1024,8320]{1,0:T(8,128)(2,1)} async-done(((bf16[64,8320]{1,0:T(8,128)(2,1)}), bf16[1024,8320]{1,0:T(8,128)(2,1)}) %all-gather.4.cloned.1.call-update) | async-done | bytes 17039376 | tf_op jit(solution)/shard_map/all_gather | solution.py:1081
  103.2 29.5 %self_forward.1 = (bf16[1024,1024]{1,0:T(8,128)(2,1)}, bf16[1024,1024]{1,0:T(8,128)(2,1)}, bf16[1024,1024]{1,0:T(8,128)(2,1)}, bf16[1024,1024]{1,0:T(8,128)(2,1)...) custom-call(s32[1]{0:T(128)} %bitcast.1.length_ref, bf16[1024,1024]{1,0:T(8,128)(2,1)} %bitcast.18, ...), custom_call_target="tpu_custom_call" | custom-call | flops 10737418240 | bytes 58720256 | tf_op jit(solution)/shard_map/self_forward/pallas_call | solution.py:291
  132.8 40.9 %cross_forward.1 = (f32[1024,1024]{1,0:T(8,128)}, f32[1024,128]{1,0:T(8,128)}, bf16[1024,1024]{1,0:T(8,128)(2,1)}, bf16[1024,1024]{1,0:T(8,128)(2,1)}, bf16[1024...) custom-call(s32[1]{0:T(128)S(6)} %copy.35.length_ref, ...), custom_call_target="tpu_custom_call" | custom-call | flops 12884901888 | bytes 69206016 | tf_op jit(solution)/shard_map/cross_forward/pallas_call | solution.py:343
  173.7 13.3 %post_cross.1 = (f32[1024,1024]{1,0:T(8,128)}, bf16[1024,1024]{1,0:T(8,128)(2,1)}, bf16[1024,1024]{1,0:T(8,128)(2,1)}, bf16[1024,512]{1,0:T(8,128)(2,1)}, bf16[1...) custom-call(f32[1]{0:T(128)S(6)} %div.3.ramp_ref, ...), custom_call_target="tpu_custom_call" | custom-call | flops 4294967296 | bytes 23068672 | tf_op jit(solution)/shard_map/post_cross/pallas_call | solution.py:418
  187.0 8.8 %all-gather.6.cloned.1.call-done.w1_ref.w2_ref = bf16[1024,8320]{1,0:T(8,128)(2,1)} async-done(((bf16[64,8320]{1,0:T(8,128)(2,1)}), bf16[1024,8320]{1,0:T(8,128)(2,1)}) %all-gather.6.cloned.1.call-update) | async-done | bytes 17039376 | tf_op jit(solution)/shard_map/all_gather | solution.py:1081
  195.7 35.3 %middle.1 = (bf16[1024,4096]{1,0:T(8,128)(2,1)}, bf16[1024,1024]{1,0:T(8,128)(2,1)}, bf16[1024,1024]{1,0:T(8,128)(2,1)}, f32[1024,1024]{1,0:T(8,128)}, bf16[1024,1152]{1,0:T(8,128)(2,1)}) custom-call(f32[1]{0:T(128)S(6)} %div.3.ramp_ref, bf16[1024,1024]{1,0:T(8,128)(2,1)} %get-tuple-element.53.hidden_ref, ...), custom_call_target="tpu_custom_call" | custom-call | flops 21474836480 | bytes 54525952 | tf_op jit(solution)/shard_map/middle/pallas_call | solution.py:561
  231.0 0.0 reduce-scatter.2.cloned.1.call-update
  231.1 0.0 all-gather.8.cloned.1.call-start
  231.1 66.5 %ffn_cross_backward.1 = (f32[1024,1024]{1,0:T(8,128)}, bf16[1024,1024]{1,0:T(8,128)(2,1)}, bf16[1024,1024]{1,0:T(8,128)(2,1)}, bf16[1024,1024]{1,0:T(8,128)(2,1)}) custom-call(bf16[1024,1024]{1,0:T(8,128)(2,1)} %get-tuple-element.60.g_ref, bf16[1024,8320]{1,0:T(8,128)(2,1)} %all-gather.6.cloned.1.call-done.w1_ref.w2_ref, ...), custom_call_target="tpu_custom_call" | custom-call | flops 30064771072 | bytes 113246208 | tf_op jit(solution)/shard_map/ffn_cross_backward/pallas_call | solution.py:918
  297.6 0.0 reduce-scatter.2.cloned.1.call-done
  297.7 1.5 collective-permute-start
  299.2 4.7 %collective-permute-done = bf16[64,1152]{1,0:T(8,128)(2,1)S(1)} collective-permute-done((bf16[64,1152]{1,0:T(8,128)(2,1)}, bf16[64,1152]{1,0:T(8,128)(2,1)S(1)}, u32[]{:S(2)}, u32[]{:S(2)}) %collective-permute-start) | collective-permute-done | bytes 147488 | tf_op jit(solution)/shard_map/ppermute | solution.py:1088
  304.0 1.6 add_convert_fusion
  305.6 0.0 all-gather.8.cloned.1.call-update
  305.6 43.1 %self_backward.1 = (f32[1024,1024]{1,0:T(8,128)}, f32[1024,1024]{1,0:T(8,128)}) custom-call(f32[1024,1024]{1,0:T(8,128)} %get-tuple-element.71.g_ref, bf16[1024,1024]{1,0:T(8,128)(2,1)} %get-tuple-element.74.low_ref, bf16[1024,1024]{1,0:T(8,128)(2,1)} %get-tuple-element.75.cdk_ref, bf16[1024,1024]{1,0:T(8,128)(2,1)} %get-tuple-element.76.cdv_ref, ...), custom_call_target="tpu_custom_call" | custom-call | flops 17179869184 | bytes 75497472 | tf_op jit(solution)/shard_map/self_backward/pallas_call | solution.py:961
  348.7 0.0 all-gather.8.cloned.1.call-done.up_in.down_in.small_in
  348.8 3.4 unpack.1
  (6 shorter events, 0.1 us)
Async XLA Ops:
  7.2 2.3 copy-start.1
  7.2 2.4 copy-start.2
  7.2 96.0 %all-gather.4.cloned.1.call-start = ((), (), s32[]{:S(2)}) async-start(), calls=%async_computation.1 | async-start | bytes 18104320 | tf_op jit(solution)/shard_map/all_gather | solution.py:1081
  9.4 2.6 copy-start.6
  9.4 3.3 copy-start.3
  9.4 3.9 %copy-start.4 = (f32[3,1024]{1,0:T(4,128)S(1)}, f32[3,1024]{1,0:T(4,128)}, u32[]{:S(2)}) copy-start(f32[3,1024]{1,0:T(4,128)} %param.35) | copy-start | bytes 36868
  9.4 3.9 %copy-start.5 = (f32[3,1024]{1,0:T(4,128)S(1)}, f32[3,1024]{1,0:T(4,128)}, u32[]{:S(2)}) copy-start(f32[3,1024]{1,0:T(4,128)} %param.34) | copy-start | bytes 36868
  9.5 186.3 %all-gather.6.cloned.1.call-start = ((), (), s32[]{:S(2)}) async-start(), calls=%async_computation.2 | async-start | bytes 18104320 | tf_op jit(solution)/shard_map/all_gather | solution.py:1081
  9.7 1.0 copy-start
  10.7 287.0 %reduce-scatter.2.cloned.1.call-start = ((), (), s32[]{:S(2)}) async-start(), calls=%async_computation.3 | async-start | bytes 2506752 | tf_op jit(solution)/shard_map/reduce_scatter | solution.py:1174
  231.1 117.7 %all-gather.8.cloned.1.call-start = ((), (), s32[]{:S(2)}) async-start(), calls=%async_computation.4 | async-start | bytes 2506752 | tf_op jit(solution)/shard_map/all_gather | solution.py:1081
  297.7 6.3 %collective-permute-start = (bf16[64,1152]{1,0:T(8,128)(2,1)}, bf16[64,1152]{1,0:T(8,128)(2,1)S(1)}, u32[]{:S(2)}, u32[]{:S(2)}) collective-permute-start(bf16[64,1152]{1,0:T(8,128)(2,1)} %reduce-scatter.2.cloned.1.call-done), channel_id=1, source_target_pairs={{0,1},{1,0},{2,3},{3,2},{4,5},{5,4},{6,7},{7,6},{8,9},{9,8},{10,11... | collective-permute-start | bytes 442376 | tf_op jit(solution)/shard_map/ppermute | solution.py:1088
Sparse Core Ops, SparseCore 0:
  10.2 93.0 all-gather.3
  105.4 90.2 all-gather.5
  231.2 62.9 reduce-scatter.1
  305.7 42.3 all-gather.7

commit v7 on v6

--- a/solution.py
+++ b/solution.py
@@ -123,7 +123,7 @@
             first, second = done[head - 1], done[head]
             inverse = 1.0 / jnp.where(left, pltpu.roll(first, SIZE, 1), pltpu.roll(second, SIZE, 1))
             span = slice(head // 2 * width, (head // 2 + 1) * width)
-            inverse_ref[low:high, span] = inverse
+            inverse_ref[low:high, span] = inverse.astype(BF16)
             ctx_ref[low:high, span] = (jnp.where(left, first, second) * inverse).astype(BF16)
 
     for pair in range(len(head_q) // 2):
@@ -155,7 +155,7 @@
     def prepare(pair):
         span = slice(pair * width, (pair + 1) * width)
         value_rows = v_ref[:, span]
-        grads = (grad_ref[:, span].astype(F32) * inverse_ref[:, span]).astype(BF16)
+        grads = (grad_ref[:, span].astype(F32) * inverse_ref[:, span].astype(F32)).astype(BF16)
         products = grads.astype(F32) * ctx_ref[:, span].astype(F32)
         high = products.astype(BF16)
         low = (products - high.astype(F32)).astype(BF16)
@@ -277,7 +277,7 @@
         + [jax.ShapeDtypeStruct((rows, width), BF16)]
         + [
             jax.ShapeDtypeStruct((heads, rows, keys), BF16),
-            jax.ShapeDtypeStruct((rows, width), F32),
+            jax.ShapeDtypeStruct((rows, width), BF16),
         ]
     )
     return specs, shapes
@@ -672,13 +672,14 @@
     sum_ref, sum_low_ref, dk_ref, dv_ref,
     total_scr, start_scr, normal_scr, low_scr, grad_scr, dq_scr, s_scr, expo_scr,
     in_sems, out_sems, expo_sems,
-    wo_scr, wq_scr, q_scr, k_scr, v_scr, ctx_scr, inverse_scr, group_sems,
+    wo_scr, wq_scr, q_scr, k_scr, v_scr, ctx_scr, inverse_scr, group_sems, scale2_scr, scale1_scr, scale_sems,
 ):
     rows, width = g_ref.shape
     spans = parts_of(rows)
     step, steps = pl.program_id(0), pl.num_programs(0)
     loads = moved([(start_ref, start_scr), (normal2_ref, normal_scr)], in_sems)
     late = pltpu.make_async_copy(normal1_ref, normal_scr, in_sems.at[2])
+    scales = moved([(scale2_ref, scale2_scr), (scale1_ref, scale1_scr)], scale_sems)
     group, groups = step - ffn_steps, steps - ffn_steps
     begin, before, after = expo_loads(expo_ref, expo_scr, expo_sems, group, groups)
     start_group, wait_group = group_loads(
@@ -700,6 +701,7 @@
 
     pl.when(step == 1)(loads[0].start)
     pl.when(step == ffn_steps // 2)(loads[1].start)
+    pl.when(step == ffn_steps // 2 + 1)(functools.partial(start_all, scales))
     pl.when(step == ffn_steps - 2)(functools.partial(start_group, 0))
 
     def first(span):
@@ -717,11 +719,12 @@
     def _():
         begin()
         wait_all(loads)
+        wait_all(scales)
 
         def back(span):
             grad = normalize_back(
                 normal_scr[span],
-                scale2_ref[span, 0:1],
+                scale2_scr[span, 0:1],
                 gain2_ref[...] * (total_scr[span] + start_scr[span]),
             )
             total_scr[span] = grad
@@ -771,7 +774,7 @@
 
         def back(span):
             grad = normalize_back(
-                normal_scr[span], scale1_ref[span, 0:1], gain1_ref[...] * total_scr[span]
+                normal_scr[span], scale1_scr[span, 0:1], gain1_ref[...] * total_scr[span]
             )
             total_scr[span] = grad
             low_scr[span] = grad.astype(BF16)
@@ -893,7 +896,7 @@
         + [pltpu.VMEM((2, width, group), BF16)] * weights
         + [pltpu.VMEM((2, rows, group), BF16)]
         + [pltpu.VMEM((2, keys, group), BF16)] * 2
-        + [pltpu.VMEM((2, rows, group), BF16), pltpu.VMEM((2, rows, group), F32)]
+        + [pltpu.VMEM((2, rows, group), BF16)] * 2
     )
 
 
@@ -926,10 +929,10 @@
             pl.BlockSpec((rows, block), lambda i: (0, unit(i))),
             anywhere(),
             anywhere(),
-            whole((rows, 128)),
+            anywhere(),
             whole((1, width)),
             anywhere(),
-            whole((rows, 128)),
+            anywhere(),
             whole((1, width)),
         ]
         + [anywhere()] * 7,
@@ -948,7 +951,9 @@
         + [pltpu.VMEM((rows, group), BF16)] * 2
         + attend_scratch(rows, keys)
         + group_scratch(rows, keys, width, 1)
-        + [pltpu.SemaphoreType.DMA((7, 2))],
+        + [pltpu.SemaphoreType.DMA((7, 2))]
+        + [pltpu.VMEM((rows, 128), F32)] * 2
+        + [pltpu.SemaphoreType.DMA((2,))],
     )(
         grads, ffn_w, ffn_w, slope, start, normal2, scale2, gain2, normal1, scale1, gain1, attn_w, *saved
     )

time: 364 us -> 363 us (level)
  no operation moved by 1% of the time
where the time goes in v7:
time: 363 us; the launch traced here: 358 us
  Pallas kernels  235 us (65%)
  waiting for transfers between devices  101 us (28%)
  between operations  15.5 us (4%)
    all_gather x3, waiting for transfers between devices, gather(): return lax.all_gather(shard, 'fsdp', axis=0, tiled=True)  96.6 us
    pallas_call x1, Pallas kernels, ffn_cross_backward(): call(functools.partial(ffn_cross_backward_kernel, held, steps, at), 'ffn_...  66.2 us
    pallas_call x1, Pallas kernels, self_backward(): call(functools.partial(self_backward_kernel, at, cross_at), 'self_backwar...  42.8 us
    pallas_call x1, Pallas kernels, cross_forward(): call(cross_forward_kernel, 'cross_forward', (per,), [scalar(), whole((row...  42.4 us
    pallas_call x1, Pallas kernels, middle(): call(functools.partial(middle_kernel, held, factor), 'middle', (wide // s...  35.3 us
    pallas_call x1, Pallas kernels, self_forward(): call(self_forward_kernel, 'self_forward', (per,), [scalar(), whole((rows,...  29.6 us
    pallas_call x1, Pallas kernels, post_cross(): call(post_cross_kernel, 'post_cross', (rows // step,), [scalar(), block(w...  13.2 us
  transfers between devices with their start and end apart: 5, of which 3 were waited for; matrix products, arithmetic and copies ran while one was open for 1% of the time, Pallas kernels for 54%

profile of v7, /device:TPU:0, one launch (start us, length us, event | category | flops | bytes accessed | tf_op | source)
XLA Modules:
  0.0 358.3 jit_solution(5755921195122415941)
XLA Ops:
  7.2 0.0 copy-start.1
  7.2 0.0 copy-start.2
  7.2 0.0 all-gather.4.cloned.1.call-start
  7.2 2.1 join.1
  9.4 0.0 copy-start.6
  9.4 0.0 copy-start.3
  9.4 0.0 copy-start.4
  9.4 0.0 copy-start.5
  9.4 0.0 all-gather.4.cloned.1.call-update
  9.5 0.0 all-gather.6.cloned.1.call-start
  9.5 0.0 copy-done.1
  9.6 0.0 copy-done.2
  9.7 0.0 copy-start
  9.7 1.0 copy-done
  10.6 0.0 all-gather.6.cloned.1.call-update
  10.7 0.0 reduce-scatter.2.cloned.1.call-start
  12.0 0.0 copy-done.6
  12.0 0.6 fusion
  12.7 0.0 copy-done.3
  12.7 0.6 fusion.1
  13.3 0.0 copy-done.4
  13.3 0.0 copy-done.5
  13.3 0.6 fusion.2
  13.9 89.3 %all-gather.4.cloned.1.call-done.wq_ref.wk_ref.wv_ref.wo_ref.attn_ref = bf16[1024,8320]{1,0:T(8,128)(2,1)} async-done(((bf16[64,8320]{1,0:T(8,128)(2,1)}), bf16[1024,8320]{1,0:T(8,128)(2,1)}) %all-gather.4.cloned.1.call-update) | async-done | bytes 17039376 | tf_op jit(solution)/shard_map/all_gather | solution.py:1086
  103.2 29.6 %self_forward.1 = (bf16[1024,1024]{1,0:T(8,128)(2,1)}, bf16[1024,1024]{1,0:T(8,128)(2,1)}, bf16[1024,1024]{1,0:T(8,128)(2,1)}, bf16[1024,1024]{1,0:T(8,128)(2,1)...) custom-call(s32[1]{0:T(128)} %bitcast.1.length_ref, bf16[1024,1024]{1,0:T(8,128)(2,1)} %bitcast.18, ...), custom_call_target="tpu_custom_call" | custom-call | flops 10737418240 | bytes 58720256 | tf_op jit(solution)/shard_map/self_forward/pallas_call | solution.py:291
  132.8 42.4 %cross_forward.1 = (f32[1024,1024]{1,0:T(8,128)}, f32[1024,128]{1,0:T(8,128)}, bf16[1024,1024]{1,0:T(8,128)(2,1)}, bf16[1024,1024]{1,0:T(8,128)(2,1)}, bf16[1024...) custom-call(s32[1]{0:T(128)S(6)} %copy.35.length_ref, ...), custom_call_target="tpu_custom_call" | custom-call | flops 12884901888 | bytes 69206016 | tf_op jit(solution)/shard_map/cross_forward/pallas_call | solution.py:343
  175.3 13.2 %post_cross.1 = (f32[1024,1024]{1,0:T(8,128)}, bf16[1024,1024]{1,0:T(8,128)(2,1)}, bf16[1024,1024]{1,0:T(8,128)(2,1)}, bf16[1024,512]{1,0:T(8,128)(2,1)}, bf16[1...) custom-call(f32[1]{0:T(128)S(6)} %div.3.ramp_ref, ...), custom_call_target="tpu_custom_call" | custom-call | flops 4294967296 | bytes 23068672 | tf_op jit(solution)/shard_map/post_cross/pallas_call | solution.py:418
  188.5 7.2 %all-gather.6.cloned.1.call-done.w1_ref.w2_ref = bf16[1024,8320]{1,0:T(8,128)(2,1)} async-done(((bf16[64,8320]{1,0:T(8,128)(2,1)}), bf16[1024,8320]{1,0:T(8,128)(2,1)}) %all-gather.6.cloned.1.call-update) | async-done | bytes 17039376 | tf_op jit(solution)/shard_map/all_gather | solution.py:1086
  195.8 35.3 %middle.1 = (bf16[1024,4096]{1,0:T(8,128)(2,1)}, bf16[1024,1024]{1,0:T(8,128)(2,1)}, bf16[1024,1024]{1,0:T(8,128)(2,1)}, f32[1024,1024]{1,0:T(8,128)}, bf16[1024,1152]{1,0:T(8,128)(2,1)}) custom-call(f32[1]{0:T(128)S(6)} %div.3.ramp_ref, bf16[1024,1024]{1,0:T(8,128)(2,1)} %get-tuple-element.53.hidden_ref, ...), custom_call_target="tpu_custom_call" | custom-call | flops 21474836480 | bytes 54525952 | tf_op jit(solution)/shard_map/middle/pallas_call | solution.py:561
  231.0 0.0 reduce-scatter.2.cloned.1.call-update
  231.0 0.0 all-gather.8.cloned.1.call-start
  231.1 66.2 %ffn_cross_backward.1 = (f32[1024,1024]{1,0:T(8,128)}, bf16[1024,1024]{1,0:T(8,128)(2,1)}, bf16[1024,1024]{1,0:T(8,128)(2,1)}, bf16[1024,1024]{1,0:T(8,128)(2,1)}) custom-call(bf16[1024,1024]{1,0:T(8,128)(2,1)} %get-tuple-element.60.g_ref, bf16[1024,8320]{1,0:T(8,128)(2,1)} %all-gather.6.cloned.1.call-done.w1_ref.w2_ref, ...), custom_call_target="tpu_custom_call" | custom-call | flops 30064771072 | bytes 113246208 | tf_op jit(solution)/shard_map/ffn_cross_backward/pallas_call | solution.py:921
  297.3 0.0 reduce-scatter.2.cloned.1.call-done
  297.3 1.5 collective-permute-start
  298.9 4.7 %collective-permute-done = bf16[64,1152]{1,0:T(8,128)(2,1)S(1)} collective-permute-done((bf16[64,1152]{1,0:T(8,128)(2,1)}, bf16[64,1152]{1,0:T(8,128)(2,1)S(1)}, u32[]{:S(2)}, u32[]{:S(2)}) %collective-permute-start) | collective-permute-done | bytes 147488 | tf_op jit(solution)/shard_map/ppermute | solution.py:1093
  303.6 1.6 add_convert_fusion
  305.2 0.0 all-gather.8.cloned.1.call-update
  305.2 42.8 %self_backward.1 = (f32[1024,1024]{1,0:T(8,128)}, f32[1024,1024]{1,0:T(8,128)}) custom-call(f32[1024,1024]{1,0:T(8,128)} %get-tuple-element.71.g_ref, bf16[1024,1024]{1,0:T(8,128)(2,1)} %get-tuple-element.74.low_ref, bf16[1024,1024]{1,0:T(8,128)(2,1)} %get-tuple-element.75.cdk_ref, bf16[1024,1024]{1,0:T(8,128)(2,1)} %get-tuple-element.76.cdv_ref, ...), custom_call_target="tpu_custom_call" | custom-call | flops 17179869184 | bytes 75497472 | tf_op jit(solution)/shard_map/self_backward/pallas_call | solution.py:966
  348.1 0.0 all-gather.8.cloned.1.call-done.up_in.down_in.small_in
  348.1 3.4 unpack.1
  (6 shorter events, 0.1 us)
Async XLA Ops:
  7.2 2.3 copy-start.1
  7.2 2.4 copy-start.2
  7.2 96.0 %all-gather.4.cloned.1.call-start = ((), (), s32[]{:S(2)}) async-start(), calls=%async_computation.1 | async-start | bytes 18104320 | tf_op jit(solution)/shard_map/all_gather | solution.py:1086
  9.4 2.6 copy-start.6
  9.4 3.3 copy-start.3
  9.4 3.9 %copy-start.4 = (f32[3,1024]{1,0:T(4,128)S(1)}, f32[3,1024]{1,0:T(4,128)}, u32[]{:S(2)}) copy-start(f32[3,1024]{1,0:T(4,128)} %param.35) | copy-start | bytes 36868
  9.4 3.9 %copy-start.5 = (f32[3,1024]{1,0:T(4,128)S(1)}, f32[3,1024]{1,0:T(4,128)}, u32[]{:S(2)}) copy-start(f32[3,1024]{1,0:T(4,128)} %param.34) | copy-start | bytes 36868
  9.5 186.3 %all-gather.6.cloned.1.call-start = ((), (), s32[]{:S(2)}) async-start(), calls=%async_computation.2 | async-start | bytes 18104320 | tf_op jit(solution)/shard_map/all_gather | solution.py:1086
  9.7 1.0 copy-start
  10.7 286.7 %reduce-scatter.2.cloned.1.call-start = ((), (), s32[]{:S(2)}) async-start(), calls=%async_computation.3 | async-start | bytes 2506752 | tf_op jit(solution)/shard_map/reduce_scatter | solution.py:1179
  231.0 117.1 %all-gather.8.cloned.1.call-start = ((), (), s32[]{:S(2)}) async-start(), calls=%async_computation.4 | async-start | bytes 2506752 | tf_op jit(solution)/shard_map/all_gather | solution.py:1086
  297.3 6.3 %collective-permute-start = (bf16[64,1152]{1,0:T(8,128)(2,1)}, bf16[64,1152]{1,0:T(8,128)(2,1)S(1)}, u32[]{:S(2)}, u32[]{:S(2)}) collective-permute-start(bf16[64,1152]{1,0:T(8,128)(2,1)} %reduce-scatter.2.cloned.1.call-done), channel_id=1, source_target_pairs={{0,1},{1,0},{2,3},{3,2},{4,5},{5,4},{6,7},{7,6},{8,9},{9,8},{10,11... | collective-permute-start | bytes 442376 | tf_op jit(solution)/shard_map/ppermute | solution.py:1093
Sparse Core Ops, SparseCore 0:
  10.2 93.0 all-gather.3
  105.4 90.2 all-gather.5
  231.2 62.9 reduce-scatter.1
  305.4 42.2 all-gather.7
